TPU v7x, 256 devices: a whole 4x4x8 slice. The times are simulated.
256 devices in a mesh: gz: 32 (over y_lo, z, core), ta: 8 (over y_hi, x).
Axes of the slice: x: 4, y: 4 (y_hi: 2, y_lo: 2; y = y_hi * 2 + y_lo), z: 8, core: 2. Of those that a mesh axis runs over, the one named last changes fastest.
Arguments:
- outputs_fwd: bfloat16 [16, 64, 64, 1280], P('ta', 'gz'), may hold values from -6 to 6
- cotangent: bfloat16 [16, 64, 64, 1280], P('ta', 'gz'), may hold values from -6 to 6
- spatial_weight: bfloat16 [3, 64, 288], replicated, may hold values from -0.21875 to 0.21875
- hidden_bias: float32 [64], replicated, may hold values from -1 to 1
- temporal_weight: bfloat16 [3, 32, 64], replicated, may hold values from -0.4375 to 0.4375
Outputs:
- rebuilt: bfloat16 [16, 64, 32, 1280], P('ta', 'gz')
- grad_in: bfloat16 [16, 64, 32, 1280], P('ta', 'gz')
- grad_spatial: float32 [3, 64, 288], replicated
- grad_bias: float32 [64], replicated
- grad_temporal: float32 [3, 32, 64], replicated
All inputs are finite; a program needn't handle non-finite values.
Results may differ from a plain program's by a relative error of at most 0.0075.
Values may be sent and summed in bfloat16 or wider, within the bound.
No kernel may reach another device: no remote copies, remote signals or barrier semaphores. Data moves between devices by JAX's collectives and lax.ppermute only.
A program may use at most 64 MiB of HBM per device.

v0:
```python
import math

import jax
import jax.numpy as jnp
from jax import lax
from jax.sharding import PartitionSpec as P

ROWS = 8
COLS = 160


def with_halo(cells, sides, width, closed):
    for axis, dim in sides:
        count = lax.axis_size(axis)
        ends = count if closed else count - 1
        head = lax.slice_in_dim(cells, 0, width, axis=dim)
        tail = lax.slice_in_dim(cells, cells.shape[dim] - width, cells.shape[dim], axis=dim)
        cells = jnp.concatenate(
            [
                lax.ppermute(tail, axis, [(i, (i + 1) % count) for i in range(ends)]),
                cells,
                lax.ppermute(head, axis, [((i + 1) % count, i) for i in range(ends)]),
            ],
            axis=dim,
        )
    return cells


def unfold(field):
    leading = field.shape[:-1]
    planar = field.reshape(leading + (ROWS, COLS))
    padded = jnp.pad(planar, [(0, 0)] * len(leading) + [(1, 1), (1, 1)])
    windows = [
        padded[..., row_off : row_off + ROWS, col_off : col_off + COLS]
        for row_off in range(3)
        for col_off in range(3)
    ]
    stacked = jnp.stack(windows, axis=-4)
    return stacked.reshape(leading[:-1] + (9 * leading[-1], ROWS * COLS))


def spatial(columns, spatial_weight, plane_count):
    total = jnp.einsum(
        "oi,fzir->fzor",
        spatial_weight[0],
        columns[:, 0:plane_count],
        preferred_element_type=jnp.float32,
    )
    total = total + jnp.einsum(
        "oi,fzir->fzor",
        spatial_weight[1],
        columns[:, 1 : plane_count + 1],
        preferred_element_type=jnp.float32,
    )
    total = total + jnp.einsum(
        "oi,fzir->fzor",
        spatial_weight[2],
        columns[:, 2 : plane_count + 2],
        preferred_element_type=jnp.float32,
    )
    return total


def temporal_back(temporal_weight, grad_around, frame_count):
    through = jnp.einsum(
        "oi,fzor->fzir",
        temporal_weight[0],
        grad_around[2 : frame_count + 2],
        preferred_element_type=jnp.float32,
    )
    through = through + jnp.einsum(
        "oi,fzor->fzir",
        temporal_weight[1],
        grad_around[1 : frame_count + 1],
        preferred_element_type=jnp.float32,
    )
    through = through + jnp.einsum(
        "oi,fzor->fzir",
        temporal_weight[2],
        grad_around[0:frame_count],
        preferred_element_type=jnp.float32,
    )
    return through


def hidden_gradient(through, hidden_in):
    sigmoid_val = jax.nn.sigmoid(hidden_in)
    return (through * sigmoid_val * (1.0 + hidden_in * (1.0 - sigmoid_val))).astype(jnp.bfloat16)


def shards(outputs_fwd, cotangent, spatial_weight, hidden_bias, temporal_weight):
    half = spatial_weight.shape[2] // 9
    hidden_count = spatial_weight.shape[1]
    front_half = outputs_fwd[:, :, :half]
    back_half = outputs_fwd[:, :, half:]
    grad_front = cotangent[:, :, :half]
    grad_back = cotangent[:, :, half:]
    frame_count = front_half.shape[0]
    plane_count = front_half.shape[1]
    bias_row = hidden_bias[None, None, :, None]
    depth_rim = 1
    padded_wide = with_halo(front_half, (("gz", 1),), depth_rim, False)
    columns = unfold(padded_wide)
    hidden_in = spatial(columns, spatial_weight, plane_count) + bias_row
    active = jax.nn.silu(hidden_in).astype(jnp.bfloat16)
    beside_all = with_halo(active, (("ta", 0),), 1, True)
    mapped = jnp.einsum(
        "oi,fzir->fzor",
        temporal_weight[0],
        beside_all[0:frame_count],
        preferred_element_type=jnp.float32,
    )
    mapped = mapped + jnp.einsum(
        "oi,fzir->fzor",
        temporal_weight[1],
        beside_all[1 : frame_count + 1],
        preferred_element_type=jnp.float32,
    )
    mapped = mapped + jnp.einsum(
        "oi,fzir->fzor",
        temporal_weight[2],
        beside_all[2 : frame_count + 2],
        preferred_element_type=jnp.float32,
    )
    rebuilt = (back_half.astype(jnp.float32) - mapped).astype(jnp.bfloat16)
    grad_around = with_halo(grad_back, (("ta", 0),), 1, True)
    through = temporal_back(temporal_weight, grad_around, frame_count)
    temporal_grad = jnp.stack(
        [
            jnp.einsum(
                "fzor,fzir->oi",
                grad_back,
                beside_all[offset : offset + frame_count],
                preferred_element_type=jnp.float32,
            )
            for offset in range(3)
        ]
    )
    hidden_grad = hidden_gradient(through, hidden_in)
    spatial_grad = jnp.stack(
        [
            jnp.einsum(
                "fzor,fzir->oi",
                hidden_grad,
                columns[:, depth : depth + plane_count],
                preferred_element_type=jnp.float32,
            )
            for depth in range(3)
        ]
    )
    bias_grad = jnp.einsum("fzor->o", hidden_grad.astype(jnp.float32))
    grad_planes = with_halo(hidden_grad, (("gz", 1),), 1, False)
    flipped = (
        spatial_weight.reshape((3, hidden_count, 9, half))[:, :, ::-1]
        .transpose((0, 3, 2, 1))
        .reshape((3, half, 9 * hidden_count))
    )

    def adjoint_frame(frame_planes):
        grad_columns = unfold(frame_planes)
        total = jnp.einsum(
            "ci,zir->zcr",
            flipped[0],
            grad_columns[2 : plane_count + 2],
            preferred_element_type=jnp.float32,
        )
        total = total + jnp.einsum(
            "ci,zir->zcr",
            flipped[1],
            grad_columns[1 : plane_count + 1],
            preferred_element_type=jnp.float32,
        )
        total = total + jnp.einsum(
            "ci,zir->zcr",
            flipped[2],
            grad_columns[0:plane_count],
            preferred_element_type=jnp.float32,
        )
        return total

    input_grad = lax.map(adjoint_frame, grad_planes)
    grad_in = (grad_front.astype(jnp.float32) + input_grad).astype(jnp.bfloat16)
    totals = lax.psum((spatial_grad, bias_grad, temporal_grad), ("gz", "ta"))
    factor = 1.0 / math.sqrt(
        frame_count * lax.axis_size("ta") * plane_count * lax.axis_size("gz") * ROWS * COLS
    )
    return (rebuilt, grad_in, totals[0] * factor, totals[1] * factor, totals[2] * factor)


def solution(mesh):
    placed = (P("ta", "gz", None, None), P("ta", "gz", None, None), P(), P(), P())
    return jax.shard_map(
        shards,
        mesh=mesh,
        in_specs=placed,
        out_specs=(P("ta", "gz", None, None), P("ta", "gz", None, None), P(), P(), P()),
        check_vma=False,
    )
```

profile of v0, /device:TPU:1, one launch (start us, length us, event | category | flops | bytes accessed | tf_op | source)
XLA Modules:
  0.0 494.4 jit_solution(1915802341013810308)
XLA Ops:
  7.2 1.1 fusion.125
  8.3 4.9 collective-permute-start
  13.3 1.9 collective-permute-start.1
  15.2 1.7 fusion.123
  16.9 5.1 %collective-permute-start.4 = (bf16[1,2,32,1280]{3,2,1,0:T(8,128)(2,1)}, bf16[1,2,32,1280]{3,2,1,0:T(8,128)(2,1)}, u32[]{:S(2)}, u32[]{:S(2)}) collective-permute-start(bf16[1,2,32,1280]{3,2,1,0:T(8,128)(2,1)} %get-tuple-element.74), channel_id=1, source_target_pairs={{1,0},{2,1},{3,2},{4,3},{5,4},{6,5},{7,6},{0,7},{9,8},{10,9},{11,1... | collective-permute-start | bytes 491528 | tf_op jit(solution)/shard_map/ppermute | solution.py:22
  22.0 1.7 slice.236
  23.7 1.1 copy.41
  25.2 1.4 fusion.99
  26.8 1.3 reshape.45
  28.1 1.3 stack.118
  29.4 1.5 fusion.56
  30.9 1.2 fusion.58
  32.2 1.6 fusion.60
  33.7 1.4 fusion.62
  35.2 1.0 bitcast_dynamic-update-slice_fusion
  36.2 1.4 fusion.64
  37.6 1.7 fusion.66
  39.3 1.2 fusion.68
  40.6 1.6 fusion.70
  42.1 15.8 %reshape.46 = bf16[2,4,288,1280]{3,2,1,0:T(8,128)(2,1)} reshape(bf16[2,4,9,32,8,160]{5,4,3,2,1,0:T(8,128)(2,1)} %fusion.70) | data formatting | bytes 11796480 | tf_op jit(solution)/shard_map/reshape | solution.py:39
  57.9 2.7 fusion.40
  60.7 2.6 convolution_add_fusion.4
  63.4 0.9 multiply_convert_fusion
  64.3 1.5 fusion.87
  65.8 1.8 convert_reduce_fusion
  67.6 1.1 fusion.49
  68.7 1.1 fusion.46
  69.8 1.1 fusion.52
  71.0 1.1 fusion.101
  72.1 0.9 fusion.124
  73.0 0.7 pad_maximum_fusion.2
  73.7 3.9 collective-permute-start.6
  77.7 1.9 collective-permute-start.7
  79.7 5.4 %collective-permute-start.3 = (bf16[1,2,64,1280]{3,2,1,0:T(8,128)(2,1)}, bf16[1,2,64,1280]{3,2,1,0:T(8,128)(2,1)}, u32[]{:S(2)}, u32[]{:S(2)}) collective-permute-start(bf16[1,2,64,1280]{3,2,1,0:T(8,128)(2,1)} %get-tuple-element.77), channel_id=1, source_target_pairs={{1,0},{2,1},{3,2},{4,3},{5,4},{6,5},{7,6},{0,7},{9,8},{10,9},{11,1... | collective-permute-start | bytes 983048 | tf_op jit(solution)/shard_map/ppermute | solution.py:22
  85.4 236.6 %all-reduce.5.cloned.1.call-done = f32[3,64,288]{2,1,0:T(8,128)} async-done(((f32[3,64,288]{2,1,0:T(8,128)}), f32[3,64,288]{2,1,0:T(8,128)}) %all-reduce.5.cloned.1.call-update) | async-done | bytes 221200 | tf_op jit(solution)/shard_map/psum | solution.py:183
  322.0 1.7 broadcast_multiply_fusion
  323.8 1.2 pad_maximum_fusion
  325.0 77.5 %while.12 = (s32[]{:T(128)}, f32[2,2,32,1280]{3,2,1,0:T(8,128)}, bf16[2,4,64,1280]{3,2,1,0:T(8,128)(2,1)}, bf16[3,32,576]{2,1,0:T(8,128)(2,1)S(1)}, s32[]{:T(128)}) while((s32[]{:T(128)}, f32[2,2,32,1280]{3,2,1,0:T(8,128)}, bf16[2,4,64,1280]{3,2,1,0:T(8,128)(2,1)}, bf16[3,32,576]{2,1,0:T(8,128)(2,1)S(1)}, s32[]{:T(128)}) %tuple.40), condition=%wide.region_1.2_spmd, body=%wide.region_0.1_spmd.sunk | while | flops 283279360 | bytes 69722216 | solution.py:181
  325.0 1.1 constant_dynamic-slice_fusion.2
  326.1 1.3 reshape.65
  327.4 1.3 stack.133
  331.1 0.8 fusion.162
  332.7 5.4 %fusion.165 = (bf16[2,9,64,8,160]{4,3,2,1,0:T(8,128)(2,1)}, bf16[2,9,64,8,160]{4,3,2,1,0:T(8,128)(2,1)}, bf16[2,9,64,8,160]{4,3,2,1,0:T(8,128)(2,1)}) fusion(bf16[4,9,64,8,160]{4,3,2,1,0:T(8,128)(2,1)S(1)} %fusion.164), kind=kLoop, calls=%fused_computation.155.clone.1 | loop fusion | bytes 17694720 | tf_op jit(solution)/shard_map/while/body/eval_jaxpr/slice | solution.py:176
  338.1 7.4 %slice.457 = bf16[2,576,1280]{2,1,0:T(8,128)(2,1)S(1)} reshape(bf16[2,9,64,8,160]{4,3,2,1,0:T(8,128)(2,1)} %get-tuple-element.112) | data formatting | bytes 5898240 | tf_op jit(solution)/shard_map/while/body/eval_jaxpr/slice | solution.py:164
  346.1 7.4 %slice.458 = bf16[2,576,1280]{2,1,0:T(8,128)(2,1)S(1)} reshape(bf16[2,9,64,8,160]{4,3,2,1,0:T(8,128)(2,1)} %get-tuple-element.113) | data formatting | bytes 5898240 | tf_op jit(solution)/shard_map/while/body/eval_jaxpr/slice | solution.py:170
  353.6 1.3 convolution_add_fusion.7
  354.9 7.4 %slice.459 = bf16[2,576,1280]{2,1,0:T(8,128)(2,1)S(1)} reshape(bf16[2,9,64,8,160]{4,3,2,1,0:T(8,128)(2,1)} %get-tuple-element.114) | data formatting | bytes 5898240 | tf_op jit(solution)/shard_map/while/body/eval_jaxpr/slice | solution.py:176
  362.4 1.4 fusion.167
  363.7 1.1 constant_dynamic-slice_fusion.2
  364.9 1.3 reshape.65
  366.2 1.3 stack.133
  369.8 0.8 fusion.162
  371.5 5.4 %fusion.165 = (bf16[2,9,64,8,160]{4,3,2,1,0:T(8,128)(2,1)}, bf16[2,9,64,8,160]{4,3,2,1,0:T(8,128)(2,1)}, bf16[2,9,64,8,160]{4,3,2,1,0:T(8,128)(2,1)}) fusion(bf16[4,9,64,8,160]{4,3,2,1,0:T(8,128)(2,1)S(1)} %fusion.164), kind=kLoop, calls=%fused_computation.155.clone.1 | loop fusion | bytes 17694720 | tf_op jit(solution)/shard_map/while/body/eval_jaxpr/slice | solution.py:176
  376.9 7.4 %slice.457 = bf16[2,576,1280]{2,1,0:T(8,128)(2,1)S(1)} reshape(bf16[2,9,64,8,160]{4,3,2,1,0:T(8,128)(2,1)} %get-tuple-element.112) | data formatting | bytes 5898240 | tf_op jit(solution)/shard_map/while/body/eval_jaxpr/slice | solution.py:164
  384.9 7.4 %slice.458 = bf16[2,576,1280]{2,1,0:T(8,128)(2,1)S(1)} reshape(bf16[2,9,64,8,160]{4,3,2,1,0:T(8,128)(2,1)} %get-tuple-element.113) | data formatting | bytes 5898240 | tf_op jit(solution)/shard_map/while/body/eval_jaxpr/slice | solution.py:170
  392.3 1.3 convolution_add_fusion.7
  393.7 7.4 %slice.459 = bf16[2,576,1280]{2,1,0:T(8,128)(2,1)S(1)} reshape(bf16[2,9,64,8,160]{4,3,2,1,0:T(8,128)(2,1)} %get-tuple-element.114) | data formatting | bytes 5898240 | tf_op jit(solution)/shard_map/while/body/eval_jaxpr/slice | solution.py:176
  401.1 1.3 fusion.167
  402.5 2.1 add_convert_fusion
  404.6 1.5 convolution_bitcast_fusion.1
  406.1 1.5 convolution_bitcast_fusion
  407.5 75.7 %all-reduce.2 = (f32[64]{0:T(128)S(1)}, f32[3,32,64]{2,1,0:T(8,128)S(1)}) all-reduce(f32[64]{0:T(128)S(1)} %get-tuple-element.82, f32[3,32,64]{2,1,0:T(8,128)S(1)} %pad_maximum_fusion.3), channel_id=1, replica_groups=mesh['gz'=32,'ta'=8] {'gz','ta'}, use_global_device_ids=true, to_apply=%region_4.5 | all-reduce | flops 6208 | bytes 49664 | tf_op jit(solution)/shard_map/psum | solution.py:183
  484.4 1.2 fusion.77
  485.6 1.9 fusion.45
  (70 shorter events, 9.7 us)
Async XLA Ops:
  7.2 19.5 %slice-start = ((bf16[2,2,64,1280]{3,2,1,0:T(8,128)(2,1)}), bf16[2,2,32,1280]{3,2,1,0:T(8,128)(2,1)S(1)}, s32[]{:S(2)}) async-start(bf16[2,2,64,1280]{3,2,1,0:T(8,128)(2,1)} %param.7), calls=%async_computation.1 | async-start | bytes 655360 | tf_op jit(solution)/shard_map/slice | solution.py:94
  7.2 18.0 %copy-start.4 = (bf16[2,2,64,1280]{3,2,1,0:T(8,128)(2,1)S(1)}, bf16[2,2,64,1280]{3,2,1,0:T(8,128)(2,1)}, u32[]{:S(2)}) copy-start(bf16[2,2,64,1280]{3,2,1,0:T(8,128)(2,1)} %param.8) | copy-start | bytes 1966084
  7.2 18.0 %copy-start.11 = (bf16[3,32,64]{2,1,0:T(8,128)(2,1)S(1)}, bf16[3,32,64]{2,1,0:T(8,128)(2,1)}, u32[]{:S(2)}) copy-start(bf16[3,32,64]{2,1,0:T(8,128)(2,1)} %param.11) | copy-start | bytes 36868
  7.2 314.8 %all-reduce.5.cloned.1.call-start = ((), (), s32[]{:S(2)}) async-start(), calls=%async_computation | async-start | bytes 589824 | tf_op jit(solution)/shard_map/psum | solution.py:183
  8.3 18.3 %collective-permute-start = (bf16[2,1,32,1280]{3,2,1,0:T(8,128)(2,1)S(1)}, bf16[2,1,32,1280]{3,2,1,0:T(8,128)(2,1)S(1)}, u32[]{:S(2)}, u32[]{:S(2)}) collective-permute-start(bf16[2,1,32,1280]{3,2,1,0:T(8,128)(2,1)S(1)} %get-tuple-element.78), channel_id=1, source_target_pairs={{0,8},{8,16},{16,24},{24,32},{32,40},{40,48},{48,56},{56,64},{64,7... | collective-permute-start | bytes 491528 | tf_op jit(solution)/shard_map/ppermute | solution.py:20
  13.3 13.4 %collective-permute-start.1 = (bf16[2,1,32,1280]{3,2,1,0:T(8,128)(2,1)S(1)}, bf16[2,1,32,1280]{3,2,1,0:T(8,128)(2,1)S(1)}, u32[]{:S(2)}, u32[]{:S(2)}) collective-permute-start(bf16[2,1,32,1280]{3,2,1,0:T(8,128)(2,1)S(1)} %get-tuple-element.79), channel_id=1, source_target_pairs={{8,0},{16,8},{24,16},{32,24},{40,32},{48,40},{56,48},{64,56},{72,6... | collective-permute-start | bytes 491528 | tf_op jit(solution)/shard_map/ppermute | solution.py:22
  16.9 48.9 %collective-permute-start.4 = (bf16[1,2,32,1280]{3,2,1,0:T(8,128)(2,1)}, bf16[1,2,32,1280]{3,2,1,0:T(8,128)(2,1)}, u32[]{:S(2)}, u32[]{:S(2)}) collective-permute-start(bf16[1,2,32,1280]{3,2,1,0:T(8,128)(2,1)} %get-tuple-element.74), channel_id=1, source_target_pairs={{1,0},{2,1},{3,2},{4,3},{5,4},{6,5},{7,6},{0,7},{9,8},{10,9},{11,1... | collective-permute-start | bytes 491528 | tf_op jit(solution)/shard_map/ppermute | solution.py:22
  22.0 42.3 %collective-permute-start.5 = (bf16[1,2,32,1280]{3,2,1,0:T(8,128)(2,1)S(1)}, bf16[1,2,32,1280]{3,2,1,0:T(8,128)(2,1)}, u32[]{:S(2)}, u32[]{:S(2)}) collective-permute-start(bf16[1,2,32,1280]{3,2,1,0:T(8,128)(2,1)S(1)} %get-tuple-element.75), channel_id=1, source_target_pairs={{0,1},{1,2},{2,3},{3,4},{4,5},{5,6},{6,7},{7,0},{8,9},{9,10},{10,1... | collective-permute-start | bytes 491528 | tf_op jit(solution)/shard_map/ppermute | solution.py:20
  42.1 15.8 %copy-start.10 = (bf16[3,64,288]{2,1,0:T(8,128)(2,1)S(1)}, bf16[3,64,288]{2,1,0:T(8,128)(2,1)}, u32[]{:S(2)}) copy-start(bf16[3,64,288]{2,1,0:T(8,128)(2,1)} %param.9) | copy-start | bytes 331780
  57.9 5.4 %copy-start.1 = (bf16[2,4,288,1280]{3,2,1,0:T(8,128)(2,1)S(1)}, bf16[2,4,288,1280]{3,2,1,0:T(8,128)(2,1)}, u32[]{:S(2)}) copy-start(bf16[2,4,288,1280]{3,2,1,0:T(8,128)(2,1)} %reshape.46) | copy-start | bytes 17694724
  60.7 2.7 copy-start.12
  63.3 1.0 copy-start.8
  63.4 2.5 copy-start.9
  64.3 20.9 %copy-start.2 = (bf16[2,2,64,1280]{3,2,1,0:T(8,128)(2,1)}, bf16[2,2,64,1280]{3,2,1,0:T(8,128)(2,1)S(1)}, u32[]{:S(2)}) copy-start(bf16[2,2,64,1280]{3,2,1,0:T(8,128)(2,1)S(1)} %get-tuple-element.80) | copy-start | bytes 1966084
  70.9 14.2 %copy-start.5 = (bf16[2,2,64,1280]{3,2,1,0:T(8,128)(2,1)S(1)}, bf16[2,2,64,1280]{3,2,1,0:T(8,128)(2,1)}, u32[]{:S(2)}) copy-start(bf16[2,2,64,1280]{3,2,1,0:T(8,128)(2,1)} %param.8) | copy-start | bytes 1966084
  73.7 250.0 %collective-permute-start.6 = (bf16[2,1,64,1280]{3,2,1,0:T(8,128)(2,1)S(1)}, bf16[2,1,64,1280]{3,2,1,0:T(8,128)(2,1)S(1)}, u32[]{:S(2)}, u32[]{:S(2)}) collective-permute-start(bf16[2,1,64,1280]{3,2,1,0:T(8,128)(2,1)S(1)} %get-tuple-element.72), channel_id=1, source_target_pairs={{0,8},{8,16},{16,24},{24,32},{32,40},{40,48},{48,56},{56,64},{64,7... | collective-permute-start | bytes 983048 | tf_op jit(solution)/shard_map/ppermute | solution.py:20
  77.7 246.1 %collective-permute-start.7 = (bf16[2,1,64,1280]{3,2,1,0:T(8,128)(2,1)S(1)}, bf16[2,1,64,1280]{3,2,1,0:T(8,128)(2,1)S(1)}, u32[]{:S(2)}, u32[]{:S(2)}) collective-permute-start(bf16[2,1,64,1280]{3,2,1,0:T(8,128)(2,1)S(1)} %get-tuple-element.73), channel_id=1, source_target_pairs={{8,0},{16,8},{24,16},{32,24},{40,32},{48,40},{56,48},{64,56},{72,6... | collective-permute-start | bytes 983048 | tf_op jit(solution)/shard_map/ppermute | solution.py:22
  79.6 325.0 %collective-permute-start.2 = (bf16[1,2,64,1280]{3,2,1,0:T(8,128)(2,1)}, bf16[1,2,64,1280]{3,2,1,0:T(8,128)(2,1)}, u32[]{:S(2)}, u32[]{:S(2)}) collective-permute-start(bf16[1,2,64,1280]{3,2,1,0:T(8,128)(2,1)} %get-tuple-element.76), channel_id=1, source_target_pairs={{0,1},{1,2},{2,3},{3,4},{4,5},{5,6},{6,7},{7,0},{8,9},{9,10},{10,1... | collective-permute-start | bytes 983048 | tf_op jit(solution)/shard_map/ppermute | solution.py:20
  79.7 326.4 %collective-permute-start.3 = (bf16[1,2,64,1280]{3,2,1,0:T(8,128)(2,1)}, bf16[1,2,64,1280]{3,2,1,0:T(8,128)(2,1)}, u32[]{:S(2)}, u32[]{:S(2)}) collective-permute-start(bf16[1,2,64,1280]{3,2,1,0:T(8,128)(2,1)} %get-tuple-element.77), channel_id=1, source_target_pairs={{1,0},{2,1},{3,2},{4,3},{5,4},{6,5},{7,6},{0,7},{9,8},{10,9},{11,1... | collective-permute-start | bytes 983048 | tf_op jit(solution)/shard_map/ppermute | solution.py:22
  354.9 7.5 %copy-start = (f32[2,1280,32]{1,2,0:T(8,128)S(1)}, f32[2,1280,32]{1,2,0:T(8,128)}, u32[]{:S(2)}) copy-start(f32[2,1280,32]{1,2,0:T(8,128)} %convolution_add_fusion.7) | copy-start | bytes 983044 | tf_op jit(solution)/shard_map/while
  393.7 7.5 %copy-start = (f32[2,1280,32]{1,2,0:T(8,128)S(1)}, f32[2,1280,32]{1,2,0:T(8,128)}, u32[]{:S(2)}) copy-start(f32[2,1280,32]{1,2,0:T(8,128)} %convolution_add_fusion.7) | copy-start | bytes 983044 | tf_op jit(solution)/shard_map/while
  402.5 81.9 %copy-start.3 = (bf16[2,2,64,1280]{3,2,1,0:T(8,128)(2,1)S(1)}, bf16[2,2,64,1280]{3,2,1,0:T(8,128)(2,1)}, u32[]{:S(2)}) copy-start(bf16[2,2,64,1280]{3,2,1,0:T(8,128)(2,1)} %copy-done.2) | copy-start | bytes 1966084
  402.5 83.1 %copy-start.6 = (f32[2,2,1280,32]{2,3,1,0:T(8,128)S(1)}, f32[2,2,1280,32]{2,3,1,0:T(8,128)}, u32[]{:S(2)}) copy-start(f32[2,2,1280,32]{2,3,1,0:T(8,128)} %fusion.101) | copy-start | bytes 1966084
  402.5 83.1 %copy-start.7 = (bf16[2,2,64,1280]{3,2,1,0:T(8,128)(2,1)S(1)}, bf16[2,2,64,1280]{3,2,1,0:T(8,128)(2,1)}, u32[]{:S(2)}) copy-start(bf16[2,2,64,1280]{3,2,1,0:T(8,128)(2,1)} %param.7) | copy-start | bytes 1966084
Sparse Core Ops, SparseCore 0:
  73.8 248.1 all-reduce.4
where the time goes:
time: 496 us; the launch traced here: 494 us
  waiting for transfers between devices  237 us (48%)
  local copies, waits for them, and re-layouts  109 us (22%)
  blocking collectives  75.7 us (15%)
  matrix products  28.3 us (6%)
  starting transfers between devices  23.4 us (5%)
  between operations  14.4 us (3%)
  other arithmetic  6.97 us (1%)
    psum x1, waiting for transfers between devices, shards(): totals = lax.psum((spatial_grad, bias_grad, temporal_grad), ('gz', 'ta'))  237 us
    psum x1, blocking collectives, shards(): totals = lax.psum((spatial_grad, bias_grad, temporal_grad), ('gz', 'ta'))  75.7 us
    slice x4, local copies, waits for them, and re-layouts, adjoint_frame(): grad_columns[0:plane_count]  25.7 us
    reshape x1, local copies, waits for them, and re-layouts, unfold(): return stacked.reshape(leading[:-1] + (9 * leading[-1], ROWS * COLS))  15.8 us
    slice x2, local copies, waits for them, and re-layouts, adjoint_frame(): grad_columns[1:plane_count + 1]  14.8 us
    slice x2, local copies, waits for them, and re-layouts, adjoint_frame(): grad_columns[2:plane_count + 2]  14.8 us
    ppermute x4, starting transfers between devices, with_halo(): lax.ppermute(head, axis, [((i + 1) % count, i) for i in range(ends)])  14.4 us
    unnamed x33, local copies, waits for them, and re-layouts  12.3 us
  transfers between devices with their start and end apart: 9, of which 1 were waited for; matrix products, arithmetic and copies ran while one was open for 26% of the time, Pallas kernels for 0%

commit v1 on v0

v1 whole, which is shorter than its diff:
```python
import math

import jax
import jax.numpy as jnp
from jax import lax
from jax.experimental import pallas as pl
from jax.experimental.pallas import tpu as pltpu
from jax.sharding import PartitionSpec as P

ROWS = 8
COLS = 160
PIX = ROWS * COLS
CH = 32
HID = 64
WIN = 9 * CH
F32 = jnp.float32
BF16 = jnp.bfloat16
VMEM_LIMIT = 48 * 1024 * 1024


def nn(a, b):
    return lax.dot_general(a, b, (((1,), (0,)), ((), ())), preferred_element_type=F32)


def nt(a, b):
    return lax.dot_general(a, b, (((1,), (1,)), ((), ())), preferred_element_type=F32)


def moved_rows(field, rows):
    if rows == 0:
        return field
    edge = jnp.zeros((field.shape[0], COLS), field.dtype)
    if rows > 0:
        return jnp.concatenate([field[:, COLS:], edge], axis=1)
    return jnp.concatenate([edge, field[:, : PIX - COLS]], axis=1)


def moved_cols(field, cols, col_of):
    if cols == 0:
        return field
    rolled = pltpu.roll(field, (-cols) % PIX, 1)
    return jnp.where(col_of == (COLS - 1 if cols > 0 else 0), jnp.zeros_like(rolled), rolled)


def hidden_kernel(
    y1_ref, low_ref, high_ref, g2_ref, before_ref, after_ref, sw_ref, bias_ref, tw_ref,
    active_ref, hgrad_ref, pay_ref,
    columns, cots,
):
    col_of = lax.rem(lax.broadcasted_iota(jnp.int32, (CH, PIX), 1), COLS)
    weight = jnp.concatenate([sw_ref[0], sw_ref[1], sw_ref[2]], axis=1)
    bias = bias_ref[...]
    tback = jnp.concatenate([tw_ref[2], tw_ref[1], tw_ref[0]], axis=0)
    for z in range(2):
        cots[z, 0:32] = before_ref[0, z]
        cots[z, 32:64] = g2_ref[0, z]
        cots[z, 64:96] = g2_ref[1, z]
        cots[z, 96:128] = after_ref[0, z]
    sgrad = [None, None, None]
    tgrad = None
    bgrad = None
    for f in range(2):
        for p in range(4):
            plane = low_ref[f, 0] if p == 0 else high_ref[f, 0] if p == 3 else y1_ref[f, p - 1]
            for c in (-1, 0, 1):
                across = moved_cols(plane, c, col_of)
                for r in (-1, 0, 1):
                    at = p * WIN + (3 * (r + 1) + c + 1) * CH
                    columns[f, at : at + CH, :] = moved_rows(across, r)
        for z in range(2):
            pre = nn(weight, columns[f, z * WIN : (z + 3) * WIN, :]) + bias
            sigma = 1.0 / (1.0 + jnp.exp(-pre))
            active = (pre * sigma).astype(BF16)
            around = cots[z, f * CH : (f + 3) * CH, :]
            through = lax.dot_general(tback, around, (((0,), (0,)), ((), ())), preferred_element_type=F32)
            hgrad = (through * sigma * (1.0 + pre * (1.0 - sigma))).astype(BF16)
            active_ref[f, z] = active
            hgrad_ref[f, z] = hgrad
            tpart = nt(around, active)
            tgrad = tpart if tgrad is None else tgrad + tpart
            bpart = jnp.sum(hgrad.astype(F32), axis=1, keepdims=True)
            bgrad = bpart if bgrad is None else bgrad + bpart
            for dz in range(3):
                part = nt(hgrad, columns[f, (z + dz) * WIN : (z + dz + 1) * WIN, :])
                sgrad[dz] = part if sgrad[dz] is None else sgrad[dz] + part
    for dz in range(3):
        for half in range(2):
            at = (2 * dz + half) * HID
            pay_ref[at : at + HID, :] = sgrad[dz][:, half * 128 : (half + 1) * 128].astype(BF16)
    tail = jnp.concatenate(
        [sgrad[dz][:, 256:288] for dz in range(3)] + [jnp.broadcast_to(bgrad, (HID, CH))], axis=1
    )
    pay_ref[384:448, :] = tail.astype(BF16)
    pay_ref[448:480, :] = jnp.concatenate([tgrad[64:96], tgrad[32:64]], axis=1).astype(BF16)
    pay_ref[480:512, :] = jnp.concatenate([tgrad[0:32], jnp.zeros((32, 64), F32)], axis=1).astype(BF16)


def outputs_kernel(
    y2_ref, g1_ref, act_ref, before_ref, after_ref, hg_ref, low_ref, high_ref, sw_ref, tw_ref,
    rebuilt_ref, gin_ref,
    acts, hgs,
):
    col_of = lax.rem(lax.broadcasted_iota(jnp.int32, (CH, PIX), 1), COLS)
    tahead = jnp.concatenate([tw_ref[0], tw_ref[1], tw_ref[2]], axis=1)
    wback = jnp.concatenate([sw_ref[2], sw_ref[1], sw_ref[0]], axis=0)
    for z in range(2):
        acts[z, 0:64] = before_ref[0, z]
        acts[z, 64:128] = act_ref[0, z]
        acts[z, 128:192] = act_ref[1, z]
        acts[z, 192:256] = after_ref[0, z]
        for f in range(2):
            mapped = nn(tahead, acts[z, f * HID : (f + 3) * HID, :])
            rebuilt_ref[f, z] = (y2_ref[f, z].astype(F32) - mapped).astype(BF16)
    for f in range(2):
        hgs[f, 0:64] = low_ref[f, 0]
        hgs[f, 64:128] = hg_ref[f, 0]
        hgs[f, 128:192] = hg_ref[f, 1]
        hgs[f, 192:256] = high_ref[f, 0]
        for z in range(2):
            spread = lax.dot_general(
                wback, hgs[f, z * HID : (z + 3) * HID, :], (((0,), (0,)), ((), ())), preferred_element_type=F32
            )
            total = g1_ref[f, z].astype(F32)
            for c in (-1, 0, 1):
                lines = None
                for r in (-1, 0, 1):
                    at = (3 * (r + 1) + c + 1) * CH
                    part = moved_rows(spread[at : at + CH], -r)
                    lines = part if lines is None else lines + part
                total = total + moved_cols(lines, -c, col_of)
            gin_ref[f, z] = total.astype(BF16)


def grads_kernel(factor, got_ref, gs_ref, gb_ref, gt_ref):
    tail = got_ref[384:448, :].astype(F32) * factor
    for dz in range(3):
        at = 2 * dz * HID
        gs_ref[dz, :, 0:128] = got_ref[at : at + HID, :].astype(F32) * factor
        gs_ref[dz, :, 128:256] = got_ref[at + HID : at + 2 * HID, :].astype(F32) * factor
        gs_ref[dz, :, 256:288] = tail[:, dz * CH : (dz + 1) * CH]
    gb_ref[...] = tail[:, 96:128].T[0:1]
    taps = got_ref[448:512, :].astype(F32) * factor
    gt_ref[0] = taps[0:32, 0:64]
    gt_ref[1] = taps[0:32, 64:128]
    gt_ref[2] = taps[32:64, 0:64]


def whole(shape):
    return pl.BlockSpec(shape, lambda i: (0,) * len(shape))


def half(which):
    return pl.BlockSpec((2, 2, CH, PIX), lambda i: (0, 0, which, 0))


def shards(outputs_fwd, cotangent, spatial_weight, hidden_bias, temporal_weight):
    axes = ("gz", "ta")
    gz, ta = lax.axis_size("gz"), lax.axis_size("ta")
    up = [(i, i + 1) for i in range(gz - 1)]
    down = [(i + 1, i) for i in range(gz - 1)]
    later = [(i, (i + 1) % ta) for i in range(ta)]
    sooner = [((i + 1) % ta, i) for i in range(ta)]
    params = pltpu.CompilerParams(vmem_limit_bytes=VMEM_LIMIT)

    low = lax.ppermute(outputs_fwd[:, 1:2, :CH], "gz", up)
    high = lax.ppermute(outputs_fwd[:, 0:1, :CH], "gz", down)
    before = lax.ppermute(cotangent[1:2, :, CH:], "ta", later)
    after = lax.ppermute(cotangent[0:1, :, CH:], "ta", sooner)

    active, hgrad, pay = pl.pallas_call(
        hidden_kernel,
        grid=(1,),
        in_specs=[
            half(0), whole((2, 1, CH, PIX)), whole((2, 1, CH, PIX)),
            half(1), whole((1, 2, CH, PIX)), whole((1, 2, CH, PIX)),
            whole((3, HID, WIN)), whole((HID, 1)), whole((3, CH, HID)),
        ],
        out_specs=[whole((2, 2, HID, PIX)), whole((2, 2, HID, PIX)), whole((512, 128))],
        out_shape=[
            jax.ShapeDtypeStruct((2, 2, HID, PIX), BF16),
            jax.ShapeDtypeStruct((2, 2, HID, PIX), BF16),
            jax.ShapeDtypeStruct((512, 128), BF16),
        ],
        scratch_shapes=[pltpu.VMEM((2, 4 * WIN, PIX), BF16), pltpu.VMEM((2, 4 * CH, PIX), BF16)],
        compiler_params=params,
        cost_estimate=pl.CostEstimate(flops=10**9, bytes_accessed=4 * 10**6, transcendentals=0),
        name="hidden",
    )(outputs_fwd, low, high, cotangent, before, after, spatial_weight, hidden_bias.reshape(HID, 1), temporal_weight)

    parts = lax.all_to_all(pay.reshape(256, 2, 128), axes, 0, 0)
    summed = jnp.sum(parts.astype(F32), axis=0).astype(BF16)
    got = lax.all_to_all(jnp.broadcast_to(summed[None], (256, 2, 128)), axes, 0, 0)

    act_before = lax.ppermute(active[1:2], "ta", later)
    act_after = lax.ppermute(active[0:1], "ta", sooner)
    hg_low = lax.ppermute(hgrad[:, 1:2], "gz", up)
    hg_high = lax.ppermute(hgrad[:, 0:1], "gz", down)

    rebuilt, grad_in = pl.pallas_call(
        outputs_kernel,
        grid=(1,),
        in_specs=[
            half(1), half(0),
            whole((2, 2, HID, PIX)), whole((1, 2, HID, PIX)), whole((1, 2, HID, PIX)),
            whole((2, 2, HID, PIX)), whole((2, 1, HID, PIX)), whole((2, 1, HID, PIX)),
            whole((3, HID, WIN)), whole((3, CH, HID)),
        ],
        out_specs=[whole((2, 2, CH, PIX)), whole((2, 2, CH, PIX))],
        out_shape=[jax.ShapeDtypeStruct((2, 2, CH, PIX), BF16)] * 2,
        scratch_shapes=[pltpu.VMEM((2, 4 * HID, PIX), BF16), pltpu.VMEM((2, 4 * HID, PIX), BF16)],
        compiler_params=params,
        cost_estimate=pl.CostEstimate(flops=10**9, bytes_accessed=4 * 10**6, transcendentals=0),
        name="outputs",
    )(outputs_fwd, cotangent, active, act_before, act_after, hgrad, hg_low, hg_high, spatial_weight, temporal_weight)

    factor = 1.0 / math.sqrt(2 * ta * 2 * gz * PIX)
    grad_spatial, grad_bias, grad_temporal = pl.pallas_call(
        lambda *refs: grads_kernel(factor, *refs),
        out_shape=[
            jax.ShapeDtypeStruct((3, HID, WIN), F32),
            jax.ShapeDtypeStruct((1, HID), F32),
            jax.ShapeDtypeStruct((3, CH, HID), F32),
        ],
        name="grads",
    )(got.reshape(512, 128))
    return rebuilt, grad_in, grad_spatial, grad_bias.reshape(HID), grad_temporal


def solution(mesh):
    placed = P("ta", "gz", None, None)
    return jax.shard_map(
        shards,
        mesh=mesh,
        in_specs=(placed, placed, P(), P(), P()),
        out_specs=(placed, placed, P(), P(), P()),
        check_vma=False,
    )
```

time: 496 us -> 82.6 us (0.17)
  waiting for transfers between devices: 237 us -> 17.4 us
  local copies, waits for them, and re-layouts: 109 us -> 5.69 us
  blocking collectives: 75.7 us -> 0 us
  matrix products: 28.3 us -> 0 us
  starting transfers between devices: 23.4 us -> 46.4 us
  between operations: 14.4 us -> 0.79 us
  Pallas kernels: 0 us -> 11.7 us
  other arithmetic: 6.97 us -> 0.28 us
    psum x1 -> x0, waiting for transfers between devices: 237 us -> none  [shards(): totals = lax.psum((spatial_grad, bias_grad, temporal_grad), ('gz', 'ta'))]
    psum x1 -> x0, blocking collectives: 75.7 us -> none  [shards(): totals = lax.psum((spatial_grad, bias_grad, temporal_grad), ('gz', 'ta'))]
    slice x15 -> x4, local copies, waits for them, and re-layouts: 60.8 us -> 3.94 us  [the longest x1 1.12 us: shards(): high = lax.ppermute(outputs_fwd[:, 0:1, :CH], 'gz', down)]
    dot_general x21 -> x0, matrix products: 28.3 us -> none  [the longest x3 3.28 us: shards(): jnp.einsum('fzor,fzir->oi', hidden_grad, columns[:, depth:depth + plane_c...]
    all_to_all x0 -> x2, starting transfers between devices: none -> 23.1 us  [the longest x1 13.4 us: shards(): parts = lax.all_to_all(pay.reshape(256, 2, 128), axes, 0, 0)]
    reshape x5 -> x1, local copies, waits for them, and re-layouts: 20 us -> 0.1 us  [shards(): hidden_bias.reshape(HID, 1)]
    all_to_all x0 -> x2, waiting for transfers between devices: none -> 13.5 us  [the longest x1 7.8 us: shards(): lax.all_to_all(jnp.broadcast_to(summed[None], (256, 2, 128)), axes, 0, 0)]
    pallas_call x0 -> x3, Pallas kernels: none -> 11.7 us  [the longest x1 6 us: shards(): pl.pallas_call(hidden_kernel, grid=(1,), in_specs=[half(0), whole((2, 1,...]
  transfers between devices with their start and end apart: 9 -> 10, of which waited for: 1 -> 3; matrix products, arithmetic and copies ran while one was open for 26% -> 4% of each run, Pallas kernels for 0% -> 5%
where the time goes in v1:
time: 82.6 us; the launch traced here: 82.2 us
  starting transfers between devices  46.4 us (56%)
  waiting for transfers between devices  17.4 us (21%)
  Pallas kernels  11.7 us (14%)
  local copies, waits for them, and re-layouts  5.69 us (7%)
    all_to_all x1, starting transfers between devices, shards(): parts = lax.all_to_all(pay.reshape(256, 2, 128), axes, 0, 0)  13.4 us
    all_to_all x1, starting transfers between devices, shards(): lax.all_to_all(jnp.broadcast_to(summed[None], (256, 2, 128)), axes, 0, 0)  9.7 us
    all_to_all x1, waiting for transfers between devices, shards(): lax.all_to_all(jnp.broadcast_to(summed[None], (256, 2, 128)), axes, 0, 0)  7.8 us
    pallas_call x1, Pallas kernels, shards(): pl.pallas_call(hidden_kernel, grid=(1,), in_specs=[half(0), whole((2, 1,...  6 us
    all_to_all x1, waiting for transfers between devices, shards(): parts = lax.all_to_all(pay.reshape(256, 2, 128), axes, 0, 0)  5.72 us
    ppermute x1, starting transfers between devices, shards(): act_after = lax.ppermute(active[0:1], 'ta', sooner)  5.17 us
    ppermute x1, starting transfers between devices, shards(): low = lax.ppermute(outputs_fwd[:, 1:2, :CH], 'gz', up)  4.94 us
    ppermute x1, starting transfers between devices, shards(): after = lax.ppermute(cotangent[0:1, :, CH:], 'ta', sooner)  3.99 us
  transfers between devices with their start and end apart: 10, of which 3 were waited for; matrix products, arithmetic and copies ran while one was open for 4% of the time, Pallas kernels for 5%

profile of v1, /device:TPU:1, one launch (start us, length us, event | category | flops | bytes accessed | tf_op | source)
XLA Modules:
  0.0 82.2 jit_solution(18370567219878630059)
XLA Ops:
  0.6 0.0 copy-start
  0.6 0.0 copy-start.1
  0.7 1.1 %fusion.3 = (bf16[2,1,32,1280]{3,2,1,0:T(8,128)(2,1)S(1)}, bf16[2,1,32,1280]{3,2,1,0:T(8,128)(2,1)S(1)}) fusion(bf16[2,2,64,1280]{3,2,1,0:T(8,128)(2,1)} %y2_ref.1), kind=kLoop, calls=%fused_computation.3 | loop fusion | bytes 655360 | tf_op jit(solution)/shard_map/slice | solution.py:166
  1.8 4.9 %collective-permute-start = (bf16[2,1,32,1280]{3,2,1,0:T(8,128)(2,1)S(1)}, bf16[2,1,32,1280]{3,2,1,0:T(8,128)(2,1)S(1)}, u32[]{:S(2)}, u32[]{:S(2)}) collective-permute-start(bf16[2,1,32,1280]{3,2,1,0:T(8,128)(2,1)S(1)} %get-tuple-element.28), channel_id=1, source_target_pairs={{0,8},{8,16},{16,24},{24,32},{32,40},{40,48},{48,56},{56,64},{64,7... | collective-permute-start | bytes 491528 | tf_op jit(solution)/shard_map/ppermute | solution.py:165
  6.7 1.9 %collective-permute-start.1 = (bf16[2,1,32,1280]{3,2,1,0:T(8,128)(2,1)S(1)}, bf16[2,1,32,1280]{3,2,1,0:T(8,128)(2,1)S(1)}, u32[]{:S(2)}, u32[]{:S(2)}) collective-permute-start(bf16[2,1,32,1280]{3,2,1,0:T(8,128)(2,1)S(1)} %get-tuple-element.27), channel_id=1, source_target_pairs={{8,0},{16,8},{24,16},{32,24},{40,32},{48,40},{56,48},{64,56},{72,6... | collective-permute-start | bytes 491528 | tf_op jit(solution)/shard_map/ppermute | solution.py:166
  8.6 0.0 copy-start.5
  8.7 1.0 %fusion.2 = (bf16[1,2,32,1280]{3,2,1,0:T(8,128)(2,1)S(1)}, bf16[1,2,32,1280]{3,2,1,0:T(8,128)(2,1)S(1)}) fusion(bf16[2,2,64,1280]{3,2,1,0:T(8,128)(2,1)} %g1_ref.1), kind=kLoop, calls=%fused_computation.2 | loop fusion | bytes 655360 | tf_op jit(solution)/shard_map/slice | solution.py:168
  9.7 0.0 copy-start.4
  9.7 1.3 %collective-permute-start.2 = (bf16[1,2,32,1280]{3,2,1,0:T(8,128)(2,1)S(1)}, bf16[1,2,32,1280]{3,2,1,0:T(8,128)(2,1)S(1)}, u32[]{:S(2)}, u32[]{:S(2)}) collective-permute-start(bf16[1,2,32,1280]{3,2,1,0:T(8,128)(2,1)S(1)} %get-tuple-element.26), channel_id=1, source_target_pairs={{0,1},{1,2},{2,3},{3,4},{4,5},{5,6},{6,7},{7,0},{8,9},{9,10},{10,1... | collective-permute-start | bytes 491528 | tf_op jit(solution)/shard_map/ppermute | solution.py:167
  11.0 4.0 %collective-permute-start.3 = (bf16[1,2,32,1280]{3,2,1,0:T(8,128)(2,1)S(1)}, bf16[1,2,32,1280]{3,2,1,0:T(8,128)(2,1)S(1)}, u32[]{:S(2)}, u32[]{:S(2)}) collective-permute-start(bf16[1,2,32,1280]{3,2,1,0:T(8,128)(2,1)S(1)} %get-tuple-element.25), channel_id=1, source_target_pairs={{1,0},{2,1},{3,2},{4,3},{5,4},{6,5},{7,6},{0,7},{9,8},{10,9},{11,1... | collective-permute-start | bytes 491528 | tf_op jit(solution)/shard_map/ppermute | solution.py:168
  15.0 0.0 copy-done.5
  15.0 0.1 copy.10.bias_ref
  15.1 0.0 collective-permute-done.low_ref
  15.1 0.0 collective-permute-done.1.high_ref
  15.1 3.8 %collective-permute-done.2.before_ref = bf16[1,2,32,1280]{3,2,1,0:T(8,128)(2,1)S(1)} collective-permute-done((bf16[1,2,32,1280]{3,2,1,0:T(8,128)(2,1)S(1)}, bf16[1,2,32,1280]{3,2,1,0:T(8,128)(2,1)S(1)}, u32[]{:S(2)}, u32[]{:S(2)}) %collective-permute-start.2) | collective-permute-done | bytes 163872 | tf_op jit(solution)/shard_map/ppermute | solution.py:167
  18.9 0.0 collective-permute-done.3.after_ref
  18.9 0.0 copy-done
  18.9 0.0 copy-done.1
  18.9 0.0 copy-done.4
  19.0 0.0 copy-start.2
  19.0 0.9 %copy-done.2 = bf16[3,64,288]{2,1,0:T(8,128)(2,1)S(1)} copy-done((bf16[3,64,288]{2,1,0:T(8,128)(2,1)S(1)}, bf16[3,64,288]{2,1,0:T(8,128)(2,1)}, u32[]{:S(2)}) %copy-start.2) | copy-done | bytes 110616
  19.9 6.0 %hidden.1 = (bf16[2,2,64,1280]{3,2,1,0:T(8,128)(2,1)S(1)}, bf16[2,2,64,1280]{3,2,1,0:T(8,128)(2,1)S(1)}, bf16[512,128]{1,0:T(8,128)(2,1)}) custom-call(bf16[2,2,64,1280]{3,2,1,0:T(8,128)(2,1)S(1)} %copy-done, bf16[2,1,32,1280]{3,2,1,0:T(8,128)(2,1)S(1)} %collective-permute-done.low_ref, bf16[2,1,32,1280]{3,2,1,0:T(8,128)(2,1)S(1)} %collective-permute-done.1.high_ref, ...), custom_call_target="tpu_custom_call" | custom-call | flops 1000000000 | bytes 4000000 | tf_op jit(solution)/shard_map/hidden/pallas_call | solution.py:170
  25.9 0.9 %fusion.1 = (bf16[1,2,64,1280]{3,2,1,0:T(8,128)(2,1)}, bf16[1,2,64,1280]{3,2,1,0:T(8,128)(2,1)}) fusion(bf16[2,2,64,1280]{3,2,1,0:T(8,128)(2,1)S(1)} %get-tuple-element.13.act_ref), kind=kLoop, calls=%fused_computation.1 | loop fusion | bytes 1310720 | tf_op jit(solution)/shard_map/slice | solution.py:195
  26.7 0.0 collective-permute-start.4
  26.8 5.2 %collective-permute-start.5 = (bf16[1,2,64,1280]{3,2,1,0:T(8,128)(2,1)}, bf16[1,2,64,1280]{3,2,1,0:T(8,128)(2,1)S(1)}, u32[]{:S(2)}, u32[]{:S(2)}) collective-permute-start(bf16[1,2,64,1280]{3,2,1,0:T(8,128)(2,1)} %get-tuple-element.23), channel_id=1, source_target_pairs={{1,0},{2,1},{3,2},{4,3},{5,4},{6,5},{7,6},{0,7},{9,8},{10,9},{11,1... | collective-permute-start | bytes 983048 | tf_op jit(solution)/shard_map/ppermute | solution.py:195
  31.9 13.4 %all-to-all-start = ((bf16[256,2,128]{2,1,0:T(2,128)(2,1)}), bf16[256,2,128]{2,1,0:T(2,128)(2,1)S(1)}, u32[]{:S(2)}, u32[]{:S(2)}) async-start(bf16[256,2,128]{2,1,0:T(2,128)(2,1)} %bitcast.1), calls=%async_computation | async-start | bytes 262144 | tf_op jit(solution)/shard_map/all_to_all | solution.py:190
  45.3 0.9 %fusion = (bf16[2,1,64,1280]{3,2,1,0:T(8,128)(2,1)}, bf16[2,1,64,1280]{3,2,1,0:T(8,128)(2,1)}) fusion(bf16[2,2,64,1280]{3,2,1,0:T(8,128)(2,1)S(1)} %get-tuple-element.14.hg_ref), kind=kLoop, calls=%fused_computation | loop fusion | bytes 1310720 | tf_op jit(solution)/shard_map/slice | solution.py:197
  46.2 3.7 %collective-permute-start.6 = (bf16[2,1,64,1280]{3,2,1,0:T(8,128)(2,1)}, bf16[2,1,64,1280]{3,2,1,0:T(8,128)(2,1)}, u32[]{:S(2)}, u32[]{:S(2)}) collective-permute-start(bf16[2,1,64,1280]{3,2,1,0:T(8,128)(2,1)} %get-tuple-element.22), channel_id=1, source_target_pairs={{0,8},{8,16},{16,24},{24,32},{32,40},{40,48},{48,56},{56,64},{64,7... | collective-permute-start | bytes 983048 | tf_op jit(solution)/shard_map/ppermute | solution.py:196
  49.9 2.4 %collective-permute-start.7 = (bf16[2,1,64,1280]{3,2,1,0:T(8,128)(2,1)}, bf16[2,1,64,1280]{3,2,1,0:T(8,128)(2,1)}, u32[]{:S(2)}, u32[]{:S(2)}) collective-permute-start(bf16[2,1,64,1280]{3,2,1,0:T(8,128)(2,1)} %get-tuple-element.21), channel_id=1, source_target_pairs={{8,0},{16,8},{24,16},{32,24},{40,32},{48,40},{56,48},{64,56},{72,6... | collective-permute-start | bytes 983048 | tf_op jit(solution)/shard_map/ppermute | solution.py:197
  52.3 5.7 %all-to-all-done = bf16[256,2,128]{2,1,0:T(2,128)(2,1)S(1)} async-done(((bf16[256,2,128]{2,1,0:T(2,128)(2,1)}), bf16[256,2,128]{2,1,0:T(2,128)(2,1)S(1)}, u32[]{:S(2)}, u32[]{:S(2)}) %all-to-all-start) | async-done | bytes 131104 | tf_op jit(solution)/shard_map/all_to_all | solution.py:190
  58.0 0.3 reduce_sum.12
  58.3 0.7 broadcast_in_dim.2
  59.0 0.0 copy-start.3
  59.0 9.7 %all-to-all-start.1 = ((bf16[256,2,128]{2,1,0:T(2,128)(2,1)}), bf16[256,2,128]{2,1,0:T(2,128)(2,1)}, u32[]{:S(2)}, u32[]{:S(2)}) async-start(bf16[256,2,128]{2,1,0:T(2,128)(2,1)} %broadcast_in_dim.2), calls=%async_computation.1 | async-start | bytes 262144 | tf_op jit(solution)/shard_map/all_to_all | solution.py:192
  68.7 0.0 collective-permute-done.4.before_ref
  68.7 0.0 collective-permute-done.5.after_ref
  68.8 0.0 collective-permute-done.6.low_ref
  68.8 0.0 collective-permute-done.7.high_ref
  68.8 0.0 copy-done.3
  68.8 3.9 %outputs.1 = (bf16[2,2,32,1280]{3,2,1,0:T(8,128)(2,1)}, bf16[2,2,32,1280]{3,2,1,0:T(8,128)(2,1)}) custom-call(bf16[2,2,64,1280]{3,2,1,0:T(8,128)(2,1)S(1)} %copy-done, bf16[2,2,64,1280]{3,2,1,0:T(8,128)(2,1)S(1)} %copy-done.1, bf16[2,2,64,1280]{3,2,1,0:T(8,128)(2,1)S(1)} %get-tuple-element.13.act_ref, ...), custom_call_target="tpu_custom_call" | custom-call | flops 1000000000 | bytes 4000000 | tf_op jit(solution)/shard_map/outputs/pallas_call | solution.py:199
  72.7 7.8 %all-to-all-done.1 = bf16[256,2,128]{2,1,0:T(2,128)(2,1)} async-done(((bf16[256,2,128]{2,1,0:T(2,128)(2,1)}), bf16[256,2,128]{2,1,0:T(2,128)(2,1)}, u32[]{:S(2)}, u32[]{:S(2)}) %all-to-all-start.1) | async-done | bytes 131104 | tf_op jit(solution)/shard_map/all_to_all | solution.py:192
  80.5 1.7 %grads.1 = (f32[3,64,288]{2,1,0:T(8,128)}, f32[1,64]{1,0:T(1,128)}, f32[3,32,64]{2,1,0:T(8,128)}) custom-call(bf16[512,128]{1,0:T(8,128)(2,1)} %bitcast.2.refs_0_), custom_call_target="tpu_custom_call" | custom-call | tf_op jit(solution)/shard_map/grads/pallas_call | solution.py:217
Async XLA Ops:
  0.6 18.3 %copy-start = (bf16[2,2,64,1280]{3,2,1,0:T(8,128)(2,1)S(1)}, bf16[2,2,64,1280]{3,2,1,0:T(8,128)(2,1)}, u32[]{:S(2)}) copy-start(bf16[2,2,64,1280]{3,2,1,0:T(8,128)(2,1)} %y2_ref.1) | copy-start | bytes 1966084
  0.6 18.3 %copy-start.1 = (bf16[2,2,64,1280]{3,2,1,0:T(8,128)(2,1)S(1)}, bf16[2,2,64,1280]{3,2,1,0:T(8,128)(2,1)}, u32[]{:S(2)}) copy-start(bf16[2,2,64,1280]{3,2,1,0:T(8,128)(2,1)} %g1_ref.1) | copy-start | bytes 1966084
  1.8 13.3 %collective-permute-start = (bf16[2,1,32,1280]{3,2,1,0:T(8,128)(2,1)S(1)}, bf16[2,1,32,1280]{3,2,1,0:T(8,128)(2,1)S(1)}, u32[]{:S(2)}, u32[]{:S(2)}) collective-permute-start(bf16[2,1,32,1280]{3,2,1,0:T(8,128)(2,1)S(1)} %get-tuple-element.28), channel_id=1, source_target_pairs={{0,8},{8,16},{16,24},{24,32},{32,40},{40,48},{48,56},{56,64},{64,7... | collective-permute-start | bytes 491528 | tf_op jit(solution)/shard_map/ppermute | solution.py:165
  6.7 8.4 %collective-permute-start.1 = (bf16[2,1,32,1280]{3,2,1,0:T(8,128)(2,1)S(1)}, bf16[2,1,32,1280]{3,2,1,0:T(8,128)(2,1)S(1)}, u32[]{:S(2)}, u32[]{:S(2)}) collective-permute-start(bf16[2,1,32,1280]{3,2,1,0:T(8,128)(2,1)S(1)} %get-tuple-element.27), channel_id=1, source_target_pairs={{8,0},{16,8},{24,16},{32,24},{40,32},{48,40},{56,48},{64,56},{72,6... | collective-permute-start | bytes 491528 | tf_op jit(solution)/shard_map/ppermute | solution.py:166
  8.6 6.3 %copy-start.5 = (f32[64]{0:T(128)S(1)}, f32[64]{0:T(128)}, u32[]{:S(2)}) copy-start(f32[64]{0:T(128)} %param.8) | copy-start | bytes 772
  9.7 9.3 %copy-start.4 = (bf16[3,32,64]{2,1,0:T(8,128)(2,1)S(1)}, bf16[3,32,64]{2,1,0:T(8,128)(2,1)}, u32[]{:S(2)}) copy-start(bf16[3,32,64]{2,1,0:T(8,128)(2,1)} %tw_ref.3) | copy-start | bytes 36868
  9.7 9.2 %collective-permute-start.2 = (bf16[1,2,32,1280]{3,2,1,0:T(8,128)(2,1)S(1)}, bf16[1,2,32,1280]{3,2,1,0:T(8,128)(2,1)S(1)}, u32[]{:S(2)}, u32[]{:S(2)}) collective-permute-start(bf16[1,2,32,1280]{3,2,1,0:T(8,128)(2,1)S(1)} %get-tuple-element.26), channel_id=1, source_target_pairs={{0,1},{1,2},{2,3},{3,4},{4,5},{5,6},{6,7},{7,0},{8,9},{9,10},{10,1... | collective-permute-start | bytes 491528 | tf_op jit(solution)/shard_map/ppermute | solution.py:167
  11.0 7.9 %collective-permute-start.3 = (bf16[1,2,32,1280]{3,2,1,0:T(8,128)(2,1)S(1)}, bf16[1,2,32,1280]{3,2,1,0:T(8,128)(2,1)S(1)}, u32[]{:S(2)}, u32[]{:S(2)}) collective-permute-start(bf16[1,2,32,1280]{3,2,1,0:T(8,128)(2,1)S(1)} %get-tuple-element.25), channel_id=1, source_target_pairs={{1,0},{2,1},{3,2},{4,3},{5,4},{6,5},{7,6},{0,7},{9,8},{10,9},{11,1... | collective-permute-start | bytes 491528 | tf_op jit(solution)/shard_map/ppermute | solution.py:168
  19.0 0.9 %copy-start.2 = (bf16[3,64,288]{2,1,0:T(8,128)(2,1)S(1)}, bf16[3,64,288]{2,1,0:T(8,128)(2,1)}, u32[]{:S(2)}) copy-start(bf16[3,64,288]{2,1,0:T(8,128)(2,1)} %sw_ref.3) | copy-start | bytes 331780
  26.7 42.0 %collective-permute-start.4 = (bf16[1,2,64,1280]{3,2,1,0:T(8,128)(2,1)}, bf16[1,2,64,1280]{3,2,1,0:T(8,128)(2,1)S(1)}, u32[]{:S(2)}, u32[]{:S(2)}) collective-permute-start(bf16[1,2,64,1280]{3,2,1,0:T(8,128)(2,1)} %get-tuple-element.24), channel_id=1, source_target_pairs={{0,1},{1,2},{2,3},{3,4},{4,5},{5,6},{6,7},{7,0},{8,9},{9,10},{10,1... | collective-permute-start | bytes 983048 | tf_op jit(solution)/shard_map/ppermute | solution.py:194
  26.8 42.0 %collective-permute-start.5 = (bf16[1,2,64,1280]{3,2,1,0:T(8,128)(2,1)}, bf16[1,2,64,1280]{3,2,1,0:T(8,128)(2,1)S(1)}, u32[]{:S(2)}, u32[]{:S(2)}) collective-permute-start(bf16[1,2,64,1280]{3,2,1,0:T(8,128)(2,1)} %get-tuple-element.23), channel_id=1, source_target_pairs={{1,0},{2,1},{3,2},{4,3},{5,4},{6,5},{7,6},{0,7},{9,8},{10,9},{11,1... | collective-permute-start | bytes 983048 | tf_op jit(solution)/shard_map/ppermute | solution.py:195
  31.9 26.1 %all-to-all-start = ((bf16[256,2,128]{2,1,0:T(2,128)(2,1)}), bf16[256,2,128]{2,1,0:T(2,128)(2,1)S(1)}, u32[]{:S(2)}, u32[]{:S(2)}) async-start(bf16[256,2,128]{2,1,0:T(2,128)(2,1)} %bitcast.1), calls=%async_computation | async-start | bytes 262144 | tf_op jit(solution)/shard_map/all_to_all | solution.py:190
  46.2 22.5 %collective-permute-start.6 = (bf16[2,1,64,1280]{3,2,1,0:T(8,128)(2,1)}, bf16[2,1,64,1280]{3,2,1,0:T(8,128)(2,1)}, u32[]{:S(2)}, u32[]{:S(2)}) collective-permute-start(bf16[2,1,64,1280]{3,2,1,0:T(8,128)(2,1)} %get-tuple-element.22), channel_id=1, source_target_pairs={{0,8},{8,16},{16,24},{24,32},{32,40},{40,48},{48,56},{56,64},{64,7... | collective-permute-start | bytes 983048 | tf_op jit(solution)/shard_map/ppermute | solution.py:196
  49.9 18.9 %collective-permute-start.7 = (bf16[2,1,64,1280]{3,2,1,0:T(8,128)(2,1)}, bf16[2,1,64,1280]{3,2,1,0:T(8,128)(2,1)}, u32[]{:S(2)}, u32[]{:S(2)}) collective-permute-start(bf16[2,1,64,1280]{3,2,1,0:T(8,128)(2,1)} %get-tuple-element.21), channel_id=1, source_target_pairs={{8,0},{16,8},{24,16},{32,24},{40,32},{48,40},{56,48},{64,56},{72,6... | collective-permute-start | bytes 983048 | tf_op jit(solution)/shard_map/ppermute | solution.py:197
  59.0 9.8 %copy-start.3 = (bf16[3,64,288]{2,1,0:T(8,128)(2,1)S(1)}, bf16[3,64,288]{2,1,0:T(8,128)(2,1)}, u32[]{:S(2)}) copy-start(bf16[3,64,288]{2,1,0:T(8,128)(2,1)} %sw_ref.3) | copy-start | bytes 331780
  59.0 21.5 %all-to-all-start.1 = ((bf16[256,2,128]{2,1,0:T(2,128)(2,1)}), bf16[256,2,128]{2,1,0:T(2,128)(2,1)}, u32[]{:S(2)}, u32[]{:S(2)}) async-start(bf16[256,2,128]{2,1,0:T(2,128)(2,1)} %broadcast_in_dim.2), calls=%async_computation.1 | async-start | bytes 262144 | tf_op jit(solution)/shard_map/all_to_all | solution.py:192

commit v2 on v1

v2 whole, which is shorter than its diff:
```python
import math

import jax
import jax.numpy as jnp
from jax import lax
from jax.experimental import pallas as pl
from jax.experimental.pallas import tpu as pltpu
from jax.sharding import PartitionSpec as P

ROWS = 8
COLS = 160
PIX = ROWS * COLS
CH = 32
HID = 64
WIN = 9 * CH
F32 = jnp.float32
BF16 = jnp.bfloat16
VMEM_LIMIT = 24 * 1024 * 1024
GZ = ("yl", "z", "c")
TA = ("yh", "x")
FLAT = ("yl", "yh", "x", "c")
LONG = pl.CostEstimate(flops=2 * 10**9, bytes_accessed=4 * 10**6, transcendentals=0)
PARAMS = pltpu.CompilerParams(vmem_limit_bytes=VMEM_LIMIT)
IN_VMEM = pl.BlockSpec(memory_space=pltpu.VMEM)
ANYWHERE = pl.BlockSpec(memory_space=pl.ANY)
IN_HBM = pl.BlockSpec(memory_space=pltpu.HBM)


def nn(a, b):
    return lax.dot_general(a, b, (((1,), (0,)), ((), ())), preferred_element_type=F32)


def nt(a, b):
    return lax.dot_general(a, b, (((1,), (1,)), ((), ())), preferred_element_type=F32)


def tn(a, b):
    return lax.dot_general(a, b, (((0,), (0,)), ((), ())), preferred_element_type=F32)


def moved_rows(field, rows):
    if rows == 0:
        return field
    edge = jnp.zeros((field.shape[0], COLS), field.dtype)
    if rows > 0:
        return jnp.concatenate([field[:, COLS:], edge], axis=1)
    return jnp.concatenate([edge, field[:, : PIX - COLS]], axis=1)


def moved_cols(field, cols, col_of):
    if cols == 0:
        return field
    rolled = pltpu.roll(field, (-cols) % PIX, 1)
    return jnp.where(col_of == (COLS - 1 if cols > 0 else 0), jnp.zeros_like(rolled), rolled)


def parities():
    return lax.axis_index("c"), lax.rem(lax.axis_index("x"), 2)


def edges_kernel(fwd_ref, cot_ref, odd_ref, even_ref, far_ref, near_ref, sems):
    core, odd = parities()
    copies = [
        pltpu.make_async_copy(cot_ref.at[pl.ds(odd, 1), :, CH : 2 * CH], odd_ref, sems.at[0]),
        pltpu.make_async_copy(cot_ref.at[pl.ds(1 - odd, 1), :, CH : 2 * CH], even_ref, sems.at[1]),
        pltpu.make_async_copy(fwd_ref.at[:, pl.ds(core, 1), 0:CH], far_ref, sems.at[2]),
        pltpu.make_async_copy(fwd_ref.at[:, pl.ds(1 - core, 1), 0:CH], near_ref, sems.at[3]),
    ]
    for copy in copies:
        copy.start()
    for copy in copies:
        copy.wait()


def hidden_kernel(
    odd_ref, even_ref, far_ref, near_ref, fwd_ref, cot_ref, weight_ref, bias_ref, tw_ref,
    active_ref, hgrad_ref, pay_ref,
    columns, cots,
):
    core, odd = parities()
    col_of = lax.rem(lax.broadcasted_iota(jnp.int32, (CH, PIX), 1), COLS)
    weight = weight_ref[...]
    bias = bias_ref[...]
    tback = jnp.concatenate([tw_ref[2], tw_ref[1], tw_ref[0]], axis=0)
    for z in range(2):
        cots[z, 0:32] = jnp.where(odd == 0, odd_ref[0, z], even_ref[0, z])
        cots[z, 32:64] = cot_ref[0, z, CH : 2 * CH]
        cots[z, 64:96] = cot_ref[1, z, CH : 2 * CH]
        cots[z, 96:128] = jnp.where(odd == 0, even_ref[0, z], odd_ref[0, z])
    sgrad = [None, None, None]
    tgrad = None
    bgrad = None
    for f in range(2):
        low = jnp.where(core == 0, far_ref[f, 0], near_ref[f, 0])
        high = jnp.where(core == 0, near_ref[f, 0], far_ref[f, 0])
        for p in range(4):
            plane = low if p == 0 else high if p == 3 else fwd_ref[f, p - 1, 0:CH]
            for c in (-1, 0, 1):
                across = moved_cols(plane, c, col_of)
                for r in (-1, 0, 1):
                    at = p * WIN + (3 * (r + 1) + c + 1) * CH
                    columns[f, at : at + CH, :] = moved_rows(across, r)
        for z in range(2):
            pre = nn(weight, columns[f, z * WIN : (z + 3) * WIN, :]) + bias
            sigma = 1.0 / (1.0 + jnp.exp(-pre))
            active = (pre * sigma).astype(BF16)
            around = cots[z, f * CH : (f + 3) * CH, :]
            through = tn(tback, around)
            hgrad = (through * sigma * (1.0 + pre * (1.0 - sigma))).astype(BF16)
            active_ref[f, z] = active
            hgrad_ref[f, z] = hgrad
            tpart = nt(around, active)
            tgrad = tpart if tgrad is None else tgrad + tpart
            bpart = jnp.sum(hgrad.astype(F32), axis=1, keepdims=True)
            bgrad = bpart if bgrad is None else bgrad + bpart
            for dz in range(3):
                part = nt(hgrad, columns[f, (z + dz) * WIN : (z + dz + 1) * WIN, :])
                sgrad[dz] = part if sgrad[dz] is None else sgrad[dz] + part
    for dz in range(3):
        for side in range(2):
            at = (2 * dz + side) * HID
            pay_ref[at : at + HID, :] = sgrad[dz][:, side * 128 : (side + 1) * 128].astype(BF16)
    bhigh, blow = two_parts(bgrad)
    pay_ref[384:448, :] = jnp.concatenate(
        [sgrad[dz][:, 256:288].astype(BF16) for dz in range(3)]
        + [jnp.broadcast_to(bhigh, (HID, 16)), jnp.broadcast_to(blow, (HID, 16))],
        axis=1,
    )
    pay_ref[448:480, :] = jnp.concatenate([tgrad[64:96], tgrad[32:64]], axis=1).astype(BF16)
    pay_ref[480:512, :] = jnp.concatenate([tgrad[0:32], jnp.zeros((32, 64), F32)], axis=1).astype(BF16)


def two_parts(value):
    high = value.astype(BF16)
    return high, (value - high.astype(F32)).astype(BF16)


def sum_kernel(count, got_ref, out_ref):
    rank = ((lax.axis_index("yl") * 2 + lax.axis_index("yh")) * 4 + lax.axis_index("x")) * 2 + lax.axis_index("c")
    total = got_ref[0].astype(F32)
    for i in range(1, got_ref.shape[0]):
        total = total + got_ref[i].astype(F32)
    both = total[:, 96:112] + total[:, 112:128]
    high, low = two_parts(both)
    split = jnp.concatenate([total[:, 0:96].astype(BF16), high, low], axis=1)
    has_bias = jnp.logical_and(rank >= 24, rank < 28)
    out = jnp.where(has_bias, split, total.astype(BF16))
    for i in range(count):
        out_ref[i] = out


def own_kernel(
    act_ref, hg_ref, sw_ref, tw_ref,
    mapped_ref, gin_ref, odd_ref, even_ref, far_ref, near_ref,
):
    core, odd = parities()
    col_of = lax.rem(lax.broadcasted_iota(jnp.int32, (CH, PIX), 1), COLS)
    none = jnp.zeros((CH, HID), BF16)
    ahead = jnp.concatenate(
        [
            jnp.concatenate([tw_ref[2], none], axis=1),
            jnp.concatenate([tw_ref[1], tw_ref[2]], axis=1),
            jnp.concatenate([tw_ref[0], tw_ref[1]], axis=1),
            jnp.concatenate([none, tw_ref[0]], axis=1),
        ],
        axis=0,
    )
    for z in range(2):
        mapped = nn(ahead, jnp.concatenate([act_ref[0, z], act_ref[1, z]], axis=0))
        for f in range(2):
            mapped_ref[f, z] = mapped[(f + 1) * CH : (f + 2) * CH]
        sooner, later = mapped[0:CH], mapped[3 * CH : 4 * CH]
        odd_ref[0, z] = jnp.where(odd == 0, sooner, later).astype(BF16)
        even_ref[0, z] = jnp.where(odd == 0, later, sooner).astype(BF16)

    def gathered(spread):
        total = None
        for c in (-1, 0, 1):
            lines = None
            for r in (-1, 0, 1):
                at = (3 * (r + 1) + c + 1) * CH
                part = moved_rows(spread[at : at + CH], -r)
                lines = part if lines is None else lines + part
            lines = moved_cols(lines, -c, col_of)
            total = lines if total is None else total + lines
        return total

    upper = jnp.concatenate([sw_ref[1], sw_ref[0]], axis=0)
    lower = jnp.concatenate([sw_ref[2], sw_ref[1]], axis=0)
    for f in range(2):
        both = jnp.concatenate([hg_ref[f, 0], hg_ref[f, 1]], axis=0)
        below = gathered(tn(sw_ref[0], hg_ref[f, 0]))
        above = gathered(tn(sw_ref[2], hg_ref[f, 1]))
        far_ref[f, 0] = jnp.where(core == 0, below, above).astype(BF16)
        near_ref[f, 0] = jnp.where(core == 0, above, below).astype(BF16)
        gin_ref[f, 0] = gathered(tn(upper, both))
        gin_ref[f, 1] = gathered(tn(lower, both))


def outputs_kernel(
    odd_ref, even_ref, far_ref, near_ref, mapped_ref, gpart_ref, fwd_ref, cot_ref, rebuilt_ref, gin_ref
):
    core, odd = parities()
    for f in range(2):
        for z in range(2):
            beside = jnp.where(odd == f, odd_ref[0, z], even_ref[0, z])
            mapped = mapped_ref[f, z] + beside.astype(F32)
            rebuilt_ref[f, z] = (fwd_ref[f, z, CH : 2 * CH].astype(F32) - mapped).astype(BF16)
            beside = jnp.where(core == z, far_ref[f, 0], near_ref[f, 0])
            back = gpart_ref[f, z] + beside.astype(F32)
            gin_ref[f, z] = (cot_ref[f, z, 0:CH].astype(F32) + back).astype(BF16)


def grads_kernel(factor, got_ref, gs_ref, gb_ref, gt_ref):
    tail = got_ref[384:448, :].astype(F32) * factor
    for dz in range(3):
        at = 2 * dz * HID
        gs_ref[dz, :, 0:128] = got_ref[at : at + HID, :].astype(F32) * factor
        gs_ref[dz, :, 128:256] = got_ref[at + HID : at + 2 * HID, :].astype(F32) * factor
        gs_ref[dz, :, 256:288] = tail[:, dz * CH : (dz + 1) * CH]
    gb_ref[...] = (tail[:, 96:112] + tail[:, 112:128]).T[0:1]
    taps = got_ref[448:512, :].astype(F32) * factor
    gt_ref[0] = taps[0:32, 0:64]
    gt_ref[1] = taps[0:32, 64:128]
    gt_ref[2] = taps[32:64, 0:64]


def shaped(*dims, dtype=BF16):
    return jax.ShapeDtypeStruct(dims, dtype)


def swaps(pairs):
    return [(a, b) for a, b in pairs] + [(b, a) for a, b in pairs]


def total_of(parts, count, name):
    return pl.pallas_call(
        lambda *refs: sum_kernel(count, *refs),
        in_specs=[IN_VMEM],
        out_specs=IN_VMEM,
        out_shape=shaped(count, 16, 128),
        compiler_params=PARAMS,
        cost_estimate=LONG,
        name=name,
    )(parts)


def shards(outputs_fwd, cotangent, spatial_weight, hidden_bias, temporal_weight):
    gz, ta = lax.axis_size(GZ), lax.axis_size(TA)
    to_far = swaps([(i, i + 1) for i in range(1, gz - 1, 2)])
    to_near = swaps([(i, i + 1) for i in range(0, gz, 2)])
    to_even = swaps([(i, i + 1) for i in range(0, ta, 2)])
    to_odd = swaps([(i, (i + 1) % ta) for i in range(1, ta, 2)])

    g2_odd, g2_even, y1_far, y1_near = pl.pallas_call(
        edges_kernel,
        in_specs=[IN_HBM] * 2,
        out_specs=[ANYWHERE] * 4,
        out_shape=[shaped(1, 2, CH, PIX)] * 2 + [shaped(2, 1, CH, PIX)] * 2,
        scratch_shapes=[pltpu.SemaphoreType.DMA((4,))],
        compiler_params=pltpu.CompilerParams(vmem_limit_bytes=54200 * 1024),
        name="edges",
    )(outputs_fwd, cotangent)
    g2_odd = lax.ppermute(g2_odd, TA, to_odd)
    g2_even = lax.ppermute(g2_even, TA, to_even)
    y1_far = lax.ppermute(y1_far, GZ, to_far)
    y1_near = lax.ppermute(y1_near, GZ, to_near)

    weight = jnp.concatenate([spatial_weight[0], spatial_weight[1], spatial_weight[2]], axis=1)
    active, hgrad, pay = pl.pallas_call(
        hidden_kernel,
        in_specs=[IN_VMEM] * 9,
        out_specs=[IN_VMEM] * 3,
        out_shape=[shaped(2, 2, HID, PIX)] * 2 + [shaped(512, 128)],
        scratch_shapes=[pltpu.VMEM((2, 4 * WIN, PIX), BF16), pltpu.VMEM((2, 4 * CH, PIX), BF16)],
        compiler_params=PARAMS,
        cost_estimate=pl.CostEstimate(flops=10**9, bytes_accessed=4 * 10**6, transcendentals=0),
        name="hidden",
    )(g2_odd, g2_even, y1_far, y1_near, outputs_fwd, cotangent, weight, hidden_bias.reshape(HID, 1), temporal_weight)

    parts = lax.all_to_all(pay.reshape(32, 16, 128), FLAT, 0, 0)
    mapped_own, gin_own, map_odd, map_even, gin_far, gin_near = pl.pallas_call(
        own_kernel,
        in_specs=[IN_VMEM] * 4,
        out_specs=[IN_VMEM] * 6,
        out_shape=[shaped(2, 2, CH, PIX, dtype=F32)] * 2
        + [shaped(1, 2, CH, PIX)] * 2
        + [shaped(2, 1, CH, PIX)] * 2,
        compiler_params=PARAMS,
        cost_estimate=LONG,
        name="own",
    )(active, hgrad, spatial_weight, temporal_weight)
    parts, map_odd, map_even, gin_far, gin_near = lax.optimization_barrier(
        (parts, map_odd, map_even, gin_far, gin_near)
    )
    parts = lax.all_to_all(total_of(parts, 8, "plane_sums"), "z", 0, 0)
    got = lax.all_to_all(total_of(parts, 32, "all_sums"), FLAT, 0, 0)

    map_odd = lax.ppermute(map_odd, TA, to_odd)
    map_even = lax.ppermute(map_even, TA, to_even)
    gin_far = lax.ppermute(gin_far, GZ, to_far)
    gin_near = lax.ppermute(gin_near, GZ, to_near)

    rebuilt, grad_in = pl.pallas_call(
        outputs_kernel,
        in_specs=[IN_VMEM] * 8,
        out_specs=[IN_VMEM] * 2,
        out_shape=[shaped(2, 2, CH, PIX)] * 2,
        compiler_params=PARAMS,
        cost_estimate=LONG,
        name="outputs",
    )(map_odd, map_even, gin_far, gin_near, mapped_own, gin_own, outputs_fwd, cotangent)
    got, rebuilt, grad_in = lax.optimization_barrier((got, rebuilt, grad_in))

    factor = 1.0 / math.sqrt(2 * ta * 2 * gz * PIX)
    grad_spatial, grad_bias, grad_temporal = pl.pallas_call(
        lambda *refs: grads_kernel(factor, *refs),
        in_specs=[IN_VMEM],
        out_specs=[IN_VMEM] * 3,
        out_shape=[shaped(3, HID, WIN, dtype=F32), shaped(1, HID, dtype=F32), shaped(3, CH, HID, dtype=F32)],
        compiler_params=PARAMS,
        name="grads",
    )(got.reshape(512, 128))
    return rebuilt, grad_in, grad_spatial, grad_bias.reshape(HID), grad_temporal


def solution(mesh):
    fine = jax.sharding.Mesh(mesh.devices.reshape(2, 8, 2, 2, 4), ("yl", "z", "c", "yh", "x"))
    placed = P(TA, GZ, None, None)
    return jax.shard_map(
        shards,
        mesh=fine,
        in_specs=(placed, placed, P(), P(), P()),
        out_specs=(placed, placed, P(), P(), P()),
        check_vma=False,
    )
```

time: 82.6 us -> 69.7 us (0.84)
  waiting for transfers between devices: 17.4 us -> 7.14 us
  starting transfers between devices: 46.4 us -> 39.4 us
  Pallas kernels: 11.7 us -> 15.2 us
    all_to_all x2 -> x3, waiting for transfers between devices: 13.5 us -> 5.98 us  [the longest x1 5.54 us: shards(): got = lax.all_to_all(total_of(parts, 32, 'all_sums'), FLAT, 0, 0)]
    unnamed x12 -> x22, local copies, waits for them, and re-layouts: 0.93 us -> 5.4 us
    slice x4 -> x0, local copies, waits for them, and re-layouts: 3.94 us -> none  [the longest x1 1.12 us: shards(): high = lax.ppermute(outputs_fwd[:, 0:1, :CH], 'gz', down)]
    ppermute x8, starting transfers between devices: 23.4 us -> 19.6 us  [the longest x1 6.03 us: shards(): g2_odd = lax.ppermute(g2_odd, TA, to_odd)]
    pallas_call x3 -> x7, Pallas kernels: 11.7 us -> 15.2 us  [the longest x1 6 us: shards(): pl.pallas_call(hidden_kernel, in_specs=[IN_VMEM] * 9, out_specs=[IN_VMEM]...]
    all_to_all x2 -> x3, starting transfers between devices: 23.1 us -> 19.8 us  [the longest x1 7.7 us: shards(): parts = lax.all_to_all(pay.reshape(32, 16, 128), FLAT, 0, 0)]
    ppermute x8, waiting for transfers between devices: 3.86 us -> 1.15 us  [the longest x1 1.14 us: shards(): y1_far = lax.ppermute(y1_far, GZ, to_far)]
    squeeze x0 -> x1, local copies, waits for them, and re-layouts: none -> 0.87 us  [shards(): spatial_weight[0]]
  transfers between devices with their start and end apart: 10 -> 11, of which waited for: 3 -> 3; matrix products, arithmetic and copies ran while one was open for 4% -> 2% of each run, Pallas kernels for 5% -> 9%
where the time goes in v2:
time: 69.7 us; the launch traced here: 69.1 us
  starting transfers between devices  39.4 us (57%)
  Pallas kernels  15.2 us (22%)
  waiting for transfers between devices  7.14 us (10%)
  local copies, waits for them, and re-layouts  6.36 us (9%)
  between operations  0.85 us (1%)
    all_to_all x1, starting transfers between devices, shards(): parts = lax.all_to_all(pay.reshape(32, 16, 128), FLAT, 0, 0)  7.7 us
    all_to_all x1, starting transfers between devices, shards(): got = lax.all_to_all(total_of(parts, 32, 'all_sums'), FLAT, 0, 0)  6.11 us
    ppermute x1, starting transfers between devices, shards(): g2_odd = lax.ppermute(g2_odd, TA, to_odd)  6.03 us
    pallas_call x1, Pallas kernels, shards(): pl.pallas_call(hidden_kernel, in_specs=[IN_VMEM] * 9, out_specs=[IN_VMEM]...  6 us
    all_to_all x1, starting transfers between devices, shards(): parts = lax.all_to_all(total_of(parts, 8, 'plane_sums'), 'z', 0, 0)  5.98 us
    all_to_all x1, waiting for transfers between devices, shards(): got = lax.all_to_all(total_of(parts, 32, 'all_sums'), FLAT, 0, 0)  5.54 us
    unnamed x22, local copies, waits for them, and re-layouts  5.4 us
    ppermute x1, starting transfers between devices, shards(): map_odd = lax.ppermute(map_odd, TA, to_odd)  4.65 us
  transfers between devices with their start and end apart: 11, of which 3 were waited for; matrix products, arithmetic and copies ran while one was open for 2% of the time, Pallas kernels for 9%

profile of v2, /device:TPU:1, one launch (start us, length us, event | category | flops | bytes accessed | tf_op | source)
XLA Modules:
  0.0 69.1 jit_solution(2105964460729748146)
XLA Ops:
  0.6 0.0 copy-start.1
  0.6 0.0 copy-start
  0.7 1.3 %edges.1 = (bf16[1,2,32,1280]{3,2,1,0:T(8,128)(2,1)S(1)}, bf16[1,2,32,1280]{3,2,1,0:T(8,128)(2,1)S(1)}, bf16[2,1,32,1280]{3,2,1,0:T(8,128)(2,1)S(1)}, bf16[2,1,32,1280]{3,2,1,0:T(8,128)(2,1)S(1)}) custom-call(bf16[2,2,64,1280]{3,2,1,0:T(8,128)(2,1)} %fwd_ref.5, bf16[2,2,64,1280]{3,2,1,0:T(8,128)(2,1)} %cot_ref.5), custom_call_target="tpu_custom_call" | custom-call | tf_op jit(solution)/shard_map/edges/pallas_call | solution.py:255
  2.0 6.0 %collective-permute-start = (bf16[1,2,32,1280]{3,2,1,0:T(8,128)(2,1)S(1)}, bf16[1,2,32,1280]{3,2,1,0:T(8,128)(2,1)S(1)}, u32[]{:S(2)}, u32[]{:S(2)}) collective-permute-start(bf16[1,2,32,1280]{3,2,1,0:T(8,128)(2,1)S(1)} %get-tuple-element.31), channel_id=1, source_target_pairs={{1,2},{3,4},{5,6},{7,0},{2,1},{4,3},{6,5},{0,7},{9,10},{11,12},{13... | collective-permute-start | bytes 491528 | tf_op jit(solution)/shard_map/ppermute | solution.py:264
  8.0 0.0 collective-permute-start.1
  8.0 4.4 %collective-permute-start.2 = (bf16[2,1,32,1280]{3,2,1,0:T(8,128)(2,1)S(1)}, bf16[2,1,32,1280]{3,2,1,0:T(8,128)(2,1)S(1)}, u32[]{:S(2)}, u32[]{:S(2)}) collective-permute-start(bf16[2,1,32,1280]{3,2,1,0:T(8,128)(2,1)S(1)} %get-tuple-element.33), channel_id=1, source_target_pairs={{8,16},{24,32},{40,48},{56,64},{72,80},{88,96},{104,112},{120,128}... | collective-permute-start | bytes 491528 | tf_op jit(solution)/shard_map/ppermute | solution.py:266
  12.4 0.1 collective-permute-start.3
  12.5 0.9 %slice_bitcast_fusion.2 = (bf16[64,288]{1,0:T(8,128)(2,1)S(1)}, bf16[64,288]{1,0:T(8,128)(2,1)S(1)}, bf16[64,288]{1,0:T(8,128)(2,1)S(1)}) fusion(bf16[3,64,288]{2,1,0:T(8,128)(2,1)} %sw_ref.1), kind=kLoop, calls=%fused_computation.3 | loop fusion | bytes 221184 | tf_op jit(solution)/shard_map/squeeze | solution.py:269
  13.3 0.0 copy-start.10
  13.3 0.6 copy-done.10
  14.0 0.1 copy.10.bias_ref
  14.1 0.0 copy-start.3
  14.1 0.1 pad_maximum_fusion.weight_ref
  14.2 0.0 collective-permute-done.odd_ref
  14.2 0.0 collective-permute-done.1.even_ref
  14.2 1.1 %collective-permute-done.2.far_ref = bf16[2,1,32,1280]{3,2,1,0:T(8,128)(2,1)S(1)} collective-permute-done((bf16[2,1,32,1280]{3,2,1,0:T(8,128)(2,1)S(1)}, bf16[2,1,32,1280]{3,2,1,0:T(8,128)(2,1)S(1)}, u32[]{:S(2)}, u32[]{:S(2)}) %collective-permute-start.2) | collective-permute-done | bytes 163872 | tf_op jit(solution)/shard_map/ppermute | solution.py:266
  15.4 0.0 collective-permute-done.3.near_ref
  15.4 0.0 copy-done.1
  15.4 0.0 copy-done
  15.4 0.0 copy-done.3
  15.4 6.0 %hidden.1 = (bf16[2,2,64,1280]{3,2,1,0:T(8,128)(2,1)S(1)}, bf16[2,2,64,1280]{3,2,1,0:T(8,128)(2,1)S(1)}, bf16[512,128]{1,0:T(8,128)(2,1)}) custom-call(bf16[1,2,32,1280]{3,2,1,0:T(8,128)(2,1)S(1)} %collective-permute-done.odd_ref, bf16[1,2,32,1280]{3,2,1,0:T(8,128)(2,1)S(1)} %collective-permute-done.1.even_ref, ...), custom_call_target="tpu_custom_call" | custom-call | flops 1000000000 | bytes 4000000 | tf_op jit(solution)/shard_map/hidden/pallas_call | solution.py:270
  21.4 0.0 copy-start.4
  21.4 0.8 %copy-done.4 = bf16[2,2,64,1280]{3,2,1,0:T(8,128)(2,1)} copy-done((bf16[2,2,64,1280]{3,2,1,0:T(8,128)(2,1)}, bf16[2,2,64,1280]{3,2,1,0:T(8,128)(2,1)S(1)}, u32[]{:S(2)}) %copy-start.4) | copy-done | bytes 655384
  22.2 0.0 copy-start.2
  22.2 7.7 %all-to-all-start = ((bf16[32,16,128]{2,1,0:T(8,128)(2,1)}), bf16[32,16,128]{2,1,0:T(8,128)(2,1)S(1)}, u32[]{:S(2)}, u32[]{:S(2)}) async-start(bf16[32,16,128]{2,1,0:T(8,128)(2,1)} %bitcast.4), calls=%async_computation | async-start | bytes 262144 | tf_op jit(solution)/shard_map/all_to_all | solution.py:281
  29.9 0.0 copy-done.2
  29.9 0.0 copy-start.5
  30.0 1.1 %copy-done.5 = bf16[2,2,64,1280]{3,2,1,0:T(8,128)(2,1)S(1)} copy-done((bf16[2,2,64,1280]{3,2,1,0:T(8,128)(2,1)S(1)}, bf16[2,2,64,1280]{3,2,1,0:T(8,128)(2,1)}, u32[]{:S(2)}) %copy-start.5) | copy-done | bytes 655384
  31.0 4.4 %own.1 = (f32[2,2,32,1280]{3,2,1,0:T(8,128)S(1)}, f32[2,2,32,1280]{3,2,1,0:T(8,128)S(1)}, bf16[1,2,32,1280]{3,2,1,0:T(8,128)(2,1)S(1)}, bf16[1,2,32,1280]{3,2,1,...) custom-call(bf16[2,2,64,1280]{3,2,1,0:T(8,128)(2,1)S(1)} %get-tuple-element.36.act_ref, ...), custom_call_target="tpu_custom_call" | custom-call | flops 2000000000 | bytes 4000000 | tf_op jit(solution)/shard_map/own/pallas_call | solution.py:282
  35.5 0.0 copy-start.6
  35.5 0.8 %copy-done.6 = f32[2,2,32,1280]{3,2,1,0:T(8,128)} copy-done((f32[2,2,32,1280]{3,2,1,0:T(8,128)}, f32[2,2,32,1280]{3,2,1,0:T(8,128)S(1)}, u32[]{:S(2)}) %copy-start.6) | copy-done | bytes 655384
  36.3 0.0 copy-start.8
  36.3 0.9 %copy-done.8 = f32[2,2,32,1280]{3,2,1,0:T(8,128)} copy-done((f32[2,2,32,1280]{3,2,1,0:T(8,128)}, f32[2,2,32,1280]{3,2,1,0:T(8,128)S(1)}, u32[]{:S(2)}) %copy-start.8) | copy-done | bytes 655384
  37.2 0.4 all-to-all-done.refs_0_
  37.6 0.8 %plane_sums.1 = bf16[8,16,128]{2,1,0:T(8,128)(2,1)} custom-call(bf16[32,16,128]{2,1,0:T(8,128)(2,1)S(1)} %all-to-all-done.refs_0_), custom_call_target="tpu_custom_call" | custom-call | flops 2000000000 | bytes 4000000 | tf_op jit(solution)/shard_map/plane_sums/pallas_call | solution.py:237
  38.4 6.0 %all-to-all-start.1 = ((bf16[8,16,128]{2,1,0:T(8,128)(2,1)}), bf16[8,16,128]{2,1,0:T(8,128)(2,1)S(1)}, u32[]{:S(2)}, u32[]{:S(2)}) async-start(bf16[8,16,128]{2,1,0:T(8,128)(2,1)} %plane_sums.1), calls=%async_computation.1 | async-start | bytes 65536 | tf_op jit(solution)/shard_map/all_to_all | solution.py:296
  44.4 0.0 copy-start.7
  44.4 4.6 %collective-permute-start.4 = (bf16[1,2,32,1280]{3,2,1,0:T(8,128)(2,1)S(1)}, bf16[1,2,32,1280]{3,2,1,0:T(8,128)(2,1)S(1)}, u32[]{:S(2)}, u32[]{:S(2)}) collective-permute-start(bf16[1,2,32,1280]{3,2,1,0:T(8,128)(2,1)S(1)} %get-tuple-element.43), channel_id=1, source_target_pairs={{1,2},{3,4},{5,6},{7,0},{2,1},{4,3},{6,5},{0,7},{9,10},{11,12},{13... | collective-permute-start | bytes 491528 | tf_op jit(solution)/shard_map/ppermute | solution.py:299
  49.1 0.0 collective-permute-start.5
  49.1 4.4 %collective-permute-start.6 = (bf16[2,1,32,1280]{3,2,1,0:T(8,128)(2,1)S(1)}, bf16[2,1,32,1280]{3,2,1,0:T(8,128)(2,1)S(1)}, u32[]{:S(2)}, u32[]{:S(2)}) collective-permute-start(bf16[2,1,32,1280]{3,2,1,0:T(8,128)(2,1)S(1)} %get-tuple-element.45), channel_id=1, source_target_pairs={{8,16},{24,32},{40,48},{56,64},{72,80},{88,96},{104,112},{120,128}... | collective-permute-start | bytes 491528 | tf_op jit(solution)/shard_map/ppermute | solution.py:301
  53.4 0.1 collective-permute-start.7
  53.5 0.0 all-to-all-done.1.refs_0_
  53.6 0.8 %all_sums.1 = bf16[32,16,128]{2,1,0:T(8,128)(2,1)} custom-call(bf16[8,16,128]{2,1,0:T(8,128)(2,1)S(1)} %all-to-all-done.1.refs_0_), custom_call_target="tpu_custom_call" | custom-call | flops 2000000000 | bytes 4000000 | tf_op jit(solution)/shard_map/all_sums/pallas_call | solution.py:237
  54.4 6.1 %all-to-all-start.2 = ((bf16[32,16,128]{2,1,0:T(8,128)(2,1)}), bf16[32,16,128]{2,1,0:T(8,128)(2,1)S(1)}, u32[]{:S(2)}, u32[]{:S(2)}) async-start(bf16[32,16,128]{2,1,0:T(8,128)(2,1)} %all_sums.1), calls=%async_computation.2 | async-start | bytes 262144 | tf_op jit(solution)/shard_map/all_to_all | solution.py:297
  60.5 0.0 collective-permute-done.4.odd_ref
  60.5 0.0 collective-permute-done.5.even_ref
  60.5 0.0 collective-permute-done.6.far_ref
  60.5 0.0 collective-permute-done.7.near_ref
  60.5 0.0 copy-done.7
  60.5 0.0 copy-start.9
  60.6 1.1 %copy-done.9 = f32[2,2,32,1280]{3,2,1,0:T(8,128)S(1)} copy-done((f32[2,2,32,1280]{3,2,1,0:T(8,128)S(1)}, f32[2,2,32,1280]{3,2,1,0:T(8,128)}, u32[]{:S(2)}) %copy-start.9) | copy-done | bytes 655384
  61.6 1.0 %outputs.1 = (bf16[2,2,32,1280]{3,2,1,0:T(8,128)(2,1)}, bf16[2,2,32,1280]{3,2,1,0:T(8,128)(2,1)}) custom-call(bf16[1,2,32,1280]{3,2,1,0:T(8,128)(2,1)S(1)} %collective-permute-done.4.odd_ref, bf16[1,2,32,1280]{3,2,1,0:T(8,128)(2,1)S(1)} %collective-permute-done.5.even_ref, bf16[2,1,32,1280]{3,2,1,0:T(8,128)(2,1)S(1)} %collective-permute-done.6.far_ref, ...), custom_call_target="tpu_custom_call" | custom-call | flops 2000000000 | bytes 4000000 | tf_op jit(solution)/shard_map/outputs/pallas_call | solution.py:304
  62.7 5.5 %all-to-all-done.2 = bf16[32,16,128]{2,1,0:T(8,128)(2,1)S(1)} async-done(((bf16[32,16,128]{2,1,0:T(8,128)(2,1)}), bf16[32,16,128]{2,1,0:T(8,128)(2,1)S(1)}, u32[]{:S(2)}, u32[]{:S(2)}) %all-to-all-start.2) | async-done | bytes 131104 | tf_op jit(solution)/shard_map/all_to_all | solution.py:297
  68.2 0.9 %grads.1 = (f32[3,64,288]{2,1,0:T(8,128)}, f32[1,64]{1,0:T(1,128)}, f32[3,32,64]{2,1,0:T(8,128)}) custom-call(bf16[512,128]{1,0:T(8,128)(2,1)S(1)} %bitcast.10), custom_call_target="tpu_custom_call" | custom-call | tf_op jit(solution)/shard_map/grads/pallas_call | solution.py:316
Async XLA Ops:
  0.6 14.7 %copy-start.1 = (bf16[2,2,64,1280]{3,2,1,0:T(8,128)(2,1)S(1)}, bf16[2,2,64,1280]{3,2,1,0:T(8,128)(2,1)}, u32[]{:S(2)}) copy-start(bf16[2,2,64,1280]{3,2,1,0:T(8,128)(2,1)} %cot_ref.5) | copy-start | bytes 1966084
  0.6 14.7 %copy-start = (bf16[2,2,64,1280]{3,2,1,0:T(8,128)(2,1)S(1)}, bf16[2,2,64,1280]{3,2,1,0:T(8,128)(2,1)}, u32[]{:S(2)}) copy-start(bf16[2,2,64,1280]{3,2,1,0:T(8,128)(2,1)} %fwd_ref.5) | copy-start | bytes 1966084
  2.0 12.2 %collective-permute-start = (bf16[1,2,32,1280]{3,2,1,0:T(8,128)(2,1)S(1)}, bf16[1,2,32,1280]{3,2,1,0:T(8,128)(2,1)S(1)}, u32[]{:S(2)}, u32[]{:S(2)}) collective-permute-start(bf16[1,2,32,1280]{3,2,1,0:T(8,128)(2,1)S(1)} %get-tuple-element.31), channel_id=1, source_target_pairs={{1,2},{3,4},{5,6},{7,0},{2,1},{4,3},{6,5},{0,7},{9,10},{11,12},{13... | collective-permute-start | bytes 491528 | tf_op jit(solution)/shard_map/ppermute | solution.py:264
  8.0 6.2 %collective-permute-start.1 = (bf16[1,2,32,1280]{3,2,1,0:T(8,128)(2,1)S(1)}, bf16[1,2,32,1280]{3,2,1,0:T(8,128)(2,1)S(1)}, u32[]{:S(2)}, u32[]{:S(2)}) collective-permute-start(bf16[1,2,32,1280]{3,2,1,0:T(8,128)(2,1)S(1)} %get-tuple-element.32), channel_id=1, source_target_pairs={{0,1},{2,3},{4,5},{6,7},{1,0},{3,2},{5,4},{7,6},{8,9},{10,11},{12,... | collective-permute-start | bytes 491528 | tf_op jit(solution)/shard_map/ppermute | solution.py:265
  8.0 7.4 %collective-permute-start.2 = (bf16[2,1,32,1280]{3,2,1,0:T(8,128)(2,1)S(1)}, bf16[2,1,32,1280]{3,2,1,0:T(8,128)(2,1)S(1)}, u32[]{:S(2)}, u32[]{:S(2)}) collective-permute-start(bf16[2,1,32,1280]{3,2,1,0:T(8,128)(2,1)S(1)} %get-tuple-element.33), channel_id=1, source_target_pairs={{8,16},{24,32},{40,48},{56,64},{72,80},{88,96},{104,112},{120,128}... | collective-permute-start | bytes 491528 | tf_op jit(solution)/shard_map/ppermute | solution.py:266
  12.4 3.0 %collective-permute-start.3 = (bf16[2,1,32,1280]{3,2,1,0:T(8,128)(2,1)S(1)}, bf16[2,1,32,1280]{3,2,1,0:T(8,128)(2,1)S(1)}, u32[]{:S(2)}, u32[]{:S(2)}) collective-permute-start(bf16[2,1,32,1280]{3,2,1,0:T(8,128)(2,1)S(1)} %get-tuple-element.34), channel_id=1, source_target_pairs={{0,8},{16,24},{32,40},{48,56},{64,72},{80,88},{96,104},{112,120},{... | collective-permute-start | bytes 491528 | tf_op jit(solution)/shard_map/ppermute | solution.py:267
  13.3 0.7 copy-start.10
  14.1 1.3 %copy-start.3 = (bf16[3,32,64]{2,1,0:T(8,128)(2,1)S(1)}, bf16[3,32,64]{2,1,0:T(8,128)(2,1)}, u32[]{:S(2)}) copy-start(bf16[3,32,64]{2,1,0:T(8,128)(2,1)} %tw_ref.3) | copy-start | bytes 36868
  21.4 0.8 %copy-start.4 = (bf16[2,2,64,1280]{3,2,1,0:T(8,128)(2,1)}, bf16[2,2,64,1280]{3,2,1,0:T(8,128)(2,1)S(1)}, u32[]{:S(2)}) copy-start(bf16[2,2,64,1280]{3,2,1,0:T(8,128)(2,1)S(1)} %get-tuple-element.37.hg_ref) | copy-start | bytes 1966084
  22.2 7.7 %copy-start.2 = (bf16[3,64,288]{2,1,0:T(8,128)(2,1)S(1)}, bf16[3,64,288]{2,1,0:T(8,128)(2,1)}, u32[]{:S(2)}) copy-start(bf16[3,64,288]{2,1,0:T(8,128)(2,1)} %sw_ref.1) | copy-start | bytes 331780
  22.2 15.4 %all-to-all-start = ((bf16[32,16,128]{2,1,0:T(8,128)(2,1)}), bf16[32,16,128]{2,1,0:T(8,128)(2,1)S(1)}, u32[]{:S(2)}, u32[]{:S(2)}) async-start(bf16[32,16,128]{2,1,0:T(8,128)(2,1)} %bitcast.4), calls=%async_computation | async-start | bytes 262144 | tf_op jit(solution)/shard_map/all_to_all | solution.py:281
  29.9 1.1 %copy-start.5 = (bf16[2,2,64,1280]{3,2,1,0:T(8,128)(2,1)S(1)}, bf16[2,2,64,1280]{3,2,1,0:T(8,128)(2,1)}, u32[]{:S(2)}) copy-start(bf16[2,2,64,1280]{3,2,1,0:T(8,128)(2,1)} %copy-done.4) | copy-start | bytes 1966084
  35.5 0.8 %copy-start.6 = (f32[2,2,32,1280]{3,2,1,0:T(8,128)}, f32[2,2,32,1280]{3,2,1,0:T(8,128)S(1)}, u32[]{:S(2)}) copy-start(f32[2,2,32,1280]{3,2,1,0:T(8,128)S(1)} %get-tuple-element.47.mapped_ref) | copy-start | bytes 1966084
  36.3 0.9 %copy-start.8 = (f32[2,2,32,1280]{3,2,1,0:T(8,128)}, f32[2,2,32,1280]{3,2,1,0:T(8,128)S(1)}, u32[]{:S(2)}) copy-start(f32[2,2,32,1280]{3,2,1,0:T(8,128)S(1)} %get-tuple-element.48.gpart_ref) | copy-start | bytes 1966084
  38.4 15.1 %all-to-all-start.1 = ((bf16[8,16,128]{2,1,0:T(8,128)(2,1)}), bf16[8,16,128]{2,1,0:T(8,128)(2,1)S(1)}, u32[]{:S(2)}, u32[]{:S(2)}) async-start(bf16[8,16,128]{2,1,0:T(8,128)(2,1)} %plane_sums.1), calls=%async_computation.1 | async-start | bytes 65536 | tf_op jit(solution)/shard_map/all_to_all | solution.py:296
  44.4 16.1 %copy-start.7 = (f32[2,2,32,1280]{3,2,1,0:T(8,128)S(1)}, f32[2,2,32,1280]{3,2,1,0:T(8,128)}, u32[]{:S(2)}) copy-start(f32[2,2,32,1280]{3,2,1,0:T(8,128)} %copy-done.6) | copy-start | bytes 1966084
  44.4 16.1 %collective-permute-start.4 = (bf16[1,2,32,1280]{3,2,1,0:T(8,128)(2,1)S(1)}, bf16[1,2,32,1280]{3,2,1,0:T(8,128)(2,1)S(1)}, u32[]{:S(2)}, u32[]{:S(2)}) collective-permute-start(bf16[1,2,32,1280]{3,2,1,0:T(8,128)(2,1)S(1)} %get-tuple-element.43), channel_id=1, source_target_pairs={{1,2},{3,4},{5,6},{7,0},{2,1},{4,3},{6,5},{0,7},{9,10},{11,12},{13... | collective-permute-start | bytes 491528 | tf_op jit(solution)/shard_map/ppermute | solution.py:299
  49.1 11.4 %collective-permute-start.5 = (bf16[1,2,32,1280]{3,2,1,0:T(8,128)(2,1)S(1)}, bf16[1,2,32,1280]{3,2,1,0:T(8,128)(2,1)S(1)}, u32[]{:S(2)}, u32[]{:S(2)}) collective-permute-start(bf16[1,2,32,1280]{3,2,1,0:T(8,128)(2,1)S(1)} %get-tuple-element.44), channel_id=1, source_target_pairs={{0,1},{2,3},{4,5},{6,7},{1,0},{3,2},{5,4},{7,6},{8,9},{10,11},{12,... | collective-permute-start | bytes 491528 | tf_op jit(solution)/shard_map/ppermute | solution.py:300
  49.1 11.4 %collective-permute-start.6 = (bf16[2,1,32,1280]{3,2,1,0:T(8,128)(2,1)S(1)}, bf16[2,1,32,1280]{3,2,1,0:T(8,128)(2,1)S(1)}, u32[]{:S(2)}, u32[]{:S(2)}) collective-permute-start(bf16[2,1,32,1280]{3,2,1,0:T(8,128)(2,1)S(1)} %get-tuple-element.45), channel_id=1, source_target_pairs={{8,16},{24,32},{40,48},{56,64},{72,80},{88,96},{104,112},{120,128}... | collective-permute-start | bytes 491528 | tf_op jit(solution)/shard_map/ppermute | solution.py:301
  53.4 7.1 %collective-permute-start.7 = (bf16[2,1,32,1280]{3,2,1,0:T(8,128)(2,1)S(1)}, bf16[2,1,32,1280]{3,2,1,0:T(8,128)(2,1)S(1)}, u32[]{:S(2)}, u32[]{:S(2)}) collective-permute-start(bf16[2,1,32,1280]{3,2,1,0:T(8,128)(2,1)S(1)} %get-tuple-element.46), channel_id=1, source_target_pairs={{0,8},{16,24},{32,40},{48,56},{64,72},{80,88},{96,104},{112,120},{... | collective-permute-start | bytes 491528 | tf_op jit(solution)/shard_map/ppermute | solution.py:302
  54.4 13.8 %all-to-all-start.2 = ((bf16[32,16,128]{2,1,0:T(8,128)(2,1)}), bf16[32,16,128]{2,1,0:T(8,128)(2,1)S(1)}, u32[]{:S(2)}, u32[]{:S(2)}) async-start(bf16[32,16,128]{2,1,0:T(8,128)(2,1)} %all_sums.1), calls=%async_computation.2 | async-start | bytes 262144 | tf_op jit(solution)/shard_map/all_to_all | solution.py:297
  60.5 1.1 %copy-start.9 = (f32[2,2,32,1280]{3,2,1,0:T(8,128)S(1)}, f32[2,2,32,1280]{3,2,1,0:T(8,128)}, u32[]{:S(2)}) copy-start(f32[2,2,32,1280]{3,2,1,0:T(8,128)} %copy-done.8) | copy-start | bytes 1966084

commit v3 on v2

--- a/solution.py
+++ b/solution.py
@@ -16,6 +16,10 @@
 F32 = jnp.float32
 BF16 = jnp.bfloat16
 VMEM_LIMIT = 24 * 1024 * 1024
+EDGES_KIB = 54200
+LATE_KIB = 54600
+LAST_KIB = 54000
+OWN_KIB = 24000
 GZ = ("yl", "z", "c")
 TA = ("yh", "x")
 FLAT = ("yl", "yh", "x", "c")
@@ -72,8 +76,15 @@
         copy.wait()
 
 
+def weights_kernel(sw_ref, bias_ref, tw_ref, weight_ref, bias_out_ref, tback_ref):
+    weight_ref[...] = jnp.concatenate([sw_ref[0], sw_ref[1], sw_ref[2]], axis=1)
+    bias_out_ref[...] = jnp.broadcast_to(bias_ref[...], (8, HID)).T[:, 0:1]
+    for k in range(3):
+        tback_ref[k * CH : (k + 1) * CH] = tw_ref[2 - k]
+
+
 def hidden_kernel(
-    odd_ref, even_ref, far_ref, near_ref, fwd_ref, cot_ref, weight_ref, bias_ref, tw_ref,
+    odd_ref, even_ref, far_ref, near_ref, fwd_ref, cot_ref, weight_ref, bias_ref, tback_ref,
     active_ref, hgrad_ref, pay_ref,
     columns, cots,
 ):
@@ -81,7 +92,7 @@
     col_of = lax.rem(lax.broadcasted_iota(jnp.int32, (CH, PIX), 1), COLS)
     weight = weight_ref[...]
     bias = bias_ref[...]
-    tback = jnp.concatenate([tw_ref[2], tw_ref[1], tw_ref[0]], axis=0)
+    tback = tback_ref[...]
     for z in range(2):
         cots[z, 0:32] = jnp.where(odd == 0, odd_ref[0, z], even_ref[0, z])
         cots[z, 32:64] = cot_ref[0, z, CH : 2 * CH]
@@ -90,16 +101,19 @@
     sgrad = [None, None, None]
     tgrad = None
     bgrad = None
+
+    def unfold(f, p, plane):
+        for c in (-1, 0, 1):
+            across = moved_cols(plane, c, col_of)
+            for r in (-1, 0, 1):
+                at = p * WIN + (3 * (r + 1) + c + 1) * CH
+                columns[f, at : at + CH, :] = moved_rows(across, r)
+
     for f in range(2):
-        low = jnp.where(core == 0, far_ref[f, 0], near_ref[f, 0])
-        high = jnp.where(core == 0, near_ref[f, 0], far_ref[f, 0])
-        for p in range(4):
-            plane = low if p == 0 else high if p == 3 else fwd_ref[f, p - 1, 0:CH]
-            for c in (-1, 0, 1):
-                across = moved_cols(plane, c, col_of)
-                for r in (-1, 0, 1):
-                    at = p * WIN + (3 * (r + 1) + c + 1) * CH
-                    columns[f, at : at + CH, :] = moved_rows(across, r)
+        unfold(f, 0, jnp.where(core == 0, far_ref[f, 0], near_ref[f, 0]))
+        unfold(f, 1, fwd_ref[f, 0, 0:CH])
+        unfold(f, 2, fwd_ref[f, 1, 0:CH])
+        unfold(f, 3, jnp.where(core == 0, near_ref[f, 0], far_ref[f, 0]))
         for z in range(2):
             pre = nn(weight, columns[f, z * WIN : (z + 3) * WIN, :]) + bias
             sigma = 1.0 / (1.0 + jnp.exp(-pre))
@@ -154,7 +168,6 @@
     mapped_ref, gin_ref, odd_ref, even_ref, far_ref, near_ref,
 ):
     core, odd = parities()
-    col_of = lax.rem(lax.broadcasted_iota(jnp.int32, (CH, PIX), 1), COLS)
     none = jnp.zeros((CH, HID), BF16)
     ahead = jnp.concatenate(
         [
@@ -173,41 +186,51 @@
         odd_ref[0, z] = jnp.where(odd == 0, sooner, later).astype(BF16)
         even_ref[0, z] = jnp.where(odd == 0, later, sooner).astype(BF16)
 
-    def gathered(spread):
-        total = None
-        for c in (-1, 0, 1):
-            lines = None
-            for r in (-1, 0, 1):
-                at = (3 * (r + 1) + c + 1) * CH
-                part = moved_rows(spread[at : at + CH], -r)
-                lines = part if lines is None else lines + part
-            lines = moved_cols(lines, -c, col_of)
-            total = lines if total is None else total + lines
-        return total
-
-    upper = jnp.concatenate([sw_ref[1], sw_ref[0]], axis=0)
-    lower = jnp.concatenate([sw_ref[2], sw_ref[1]], axis=0)
+    back = jnp.concatenate(
+        [
+            jnp.concatenate(
+                [sw_ref[dz, :, (3 * r + c) * CH : (3 * r + c + 1) * CH] for dz in range(3) for r in range(3)], axis=1
+            )
+            for c in range(3)
+        ],
+        axis=0,
+    )
+    col_of = lax.rem(lax.broadcasted_iota(jnp.int32, (HID, PIX), 1), COLS)
+
+    def rows_joined(lines):
+        return lines[CH : 2 * CH] + moved_rows(lines[0:CH], 1) + moved_rows(lines[2 * CH : 3 * CH], -1)
+
     for f in range(2):
-        both = jnp.concatenate([hg_ref[f, 0], hg_ref[f, 1]], axis=0)
-        below = gathered(tn(sw_ref[0], hg_ref[f, 0]))
-        above = gathered(tn(sw_ref[2], hg_ref[f, 1]))
+        spread = []
+        for z in range(2):
+            field = hg_ref[f, z]
+            spread.append(tn(back, jnp.concatenate([moved_cols(field, -c, col_of) for c in (-1, 0, 1)], axis=0)))
+        below = rows_joined(spread[0][0:96])
+        above = rows_joined(spread[1][192:288])
+        gin_ref[f, 0] = rows_joined(spread[0][96:192] + spread[1][0:96])
+        gin_ref[f, 1] = rows_joined(spread[0][192:288] + spread[1][96:192])
         far_ref[f, 0] = jnp.where(core == 0, below, above).astype(BF16)
         near_ref[f, 0] = jnp.where(core == 0, above, below).astype(BF16)
-        gin_ref[f, 0] = gathered(tn(upper, both))
-        gin_ref[f, 1] = gathered(tn(lower, both))
-
-
-def outputs_kernel(
-    odd_ref, even_ref, far_ref, near_ref, mapped_ref, gpart_ref, fwd_ref, cot_ref, rebuilt_ref, gin_ref
-):
-    core, odd = parities()
+
+
+def rebuilt_kernel(seam_ref, inner_ref, even_ref, mapped_ref, fwd_ref, rebuilt_ref):
+    odd = parities()[1]
+    place = lax.axis_index("x")
+    seam = jnp.logical_or(place == 0, place == lax.axis_size("x") - 1)
+    for z in range(2):
+        from_odd = jnp.where(seam, seam_ref[0, z], inner_ref[0, z])
+        for f in range(2):
+            beside = jnp.where(odd == f, from_odd, even_ref[0, z])
+            mapped = mapped_ref[f, z] + beside.astype(F32)
+            rebuilt_ref[f, z] = (fwd_ref[f, z, CH : 2 * CH].astype(F32) - mapped).astype(BF16)
+
+
+def gin_kernel(far_ref, near_ref, own_ref, cot_ref, gin_ref):
+    core = parities()[0]
     for f in range(2):
         for z in range(2):
-            beside = jnp.where(odd == f, odd_ref[0, z], even_ref[0, z])
-            mapped = mapped_ref[f, z] + beside.astype(F32)
-            rebuilt_ref[f, z] = (fwd_ref[f, z, CH : 2 * CH].astype(F32) - mapped).astype(BF16)
             beside = jnp.where(core == z, far_ref[f, 0], near_ref[f, 0])
-            back = gpart_ref[f, z] + beside.astype(F32)
+            back = own_ref[f, z] + beside.astype(F32)
             gin_ref[f, z] = (cot_ref[f, z, 0:CH].astype(F32) + back).astype(BF16)
 
 
@@ -245,12 +268,27 @@
     )(parts)
 
 
+def finished(kernel, name, operands, kib, cost):
+    return pl.pallas_call(
+        kernel,
+        in_specs=[IN_VMEM] * len(operands),
+        out_specs=IN_VMEM,
+        out_shape=shaped(2, 2, CH, PIX),
+        compiler_params=pltpu.CompilerParams(vmem_limit_bytes=kib * 1024),
+        cost_estimate=cost,
+        name=name,
+    )(*operands)
+
+
 def shards(outputs_fwd, cotangent, spatial_weight, hidden_bias, temporal_weight):
     gz, ta = lax.axis_size(GZ), lax.axis_size(TA)
     to_far = swaps([(i, i + 1) for i in range(1, gz - 1, 2)])
     to_near = swaps([(i, i + 1) for i in range(0, gz, 2)])
     to_even = swaps([(i, i + 1) for i in range(0, ta, 2)])
     to_odd = swaps([(i, (i + 1) % ta) for i in range(1, ta, 2)])
+    row = lax.axis_size("x")
+    to_inner = swaps([(i, i + 1) for i in range(1, ta, 2) if (i + 1) % row])
+    to_seam = swaps([(i, (i + 1) % ta) for i in range(1, ta, 2) if (i + 1) % row == 0])
 
     g2_odd, g2_even, y1_far, y1_near = pl.pallas_call(
         edges_kernel,
@@ -258,25 +296,36 @@
         out_specs=[ANYWHERE] * 4,
         out_shape=[shaped(1, 2, CH, PIX)] * 2 + [shaped(2, 1, CH, PIX)] * 2,
         scratch_shapes=[pltpu.SemaphoreType.DMA((4,))],
-        compiler_params=pltpu.CompilerParams(vmem_limit_bytes=54200 * 1024),
+        compiler_params=pltpu.CompilerParams(vmem_limit_bytes=EDGES_KIB * 1024),
+        cost_estimate=pl.CostEstimate(flops=4 * 10**9, bytes_accessed=10**6, transcendentals=0),
         name="edges",
     )(outputs_fwd, cotangent)
+    weight, bias, tback = pl.pallas_call(
+        weights_kernel,
+        in_specs=[IN_VMEM] * 3,
+        out_specs=[IN_VMEM] * 3,
+        out_shape=[shaped(HID, 3 * WIN), shaped(HID, 1, dtype=F32), shaped(3 * CH, HID)],
+        compiler_params=PARAMS,
+        name="weights",
+    )(spatial_weight, hidden_bias.reshape(1, HID), temporal_weight)
     g2_odd = lax.ppermute(g2_odd, TA, to_odd)
     g2_even = lax.ppermute(g2_even, TA, to_even)
     y1_far = lax.ppermute(y1_far, GZ, to_far)
     y1_near = lax.ppermute(y1_near, GZ, to_near)
 
-    weight = jnp.concatenate([spatial_weight[0], spatial_weight[1], spatial_weight[2]], axis=1)
     active, hgrad, pay = pl.pallas_call(
         hidden_kernel,
         in_specs=[IN_VMEM] * 9,
         out_specs=[IN_VMEM] * 3,
         out_shape=[shaped(2, 2, HID, PIX)] * 2 + [shaped(512, 128)],
-        scratch_shapes=[pltpu.VMEM((2, 4 * WIN, PIX), BF16), pltpu.VMEM((2, 4 * CH, PIX), BF16)],
+        scratch_shapes=[
+            pltpu.VMEM((2, 4 * WIN, PIX), BF16),
+            pltpu.VMEM((2, 4 * CH, PIX), BF16),
+        ],
         compiler_params=PARAMS,
         cost_estimate=pl.CostEstimate(flops=10**9, bytes_accessed=4 * 10**6, transcendentals=0),
         name="hidden",
-    )(g2_odd, g2_even, y1_far, y1_near, outputs_fwd, cotangent, weight, hidden_bias.reshape(HID, 1), temporal_weight)
+    )(g2_odd, g2_even, y1_far, y1_near, outputs_fwd, cotangent, weight, bias, tback)
 
     parts = lax.all_to_all(pay.reshape(32, 16, 128), FLAT, 0, 0)
     mapped_own, gin_own, map_odd, map_even, gin_far, gin_near = pl.pallas_call(
@@ -286,31 +335,24 @@
         out_shape=[shaped(2, 2, CH, PIX, dtype=F32)] * 2
         + [shaped(1, 2, CH, PIX)] * 2
         + [shaped(2, 1, CH, PIX)] * 2,
-        compiler_params=PARAMS,
+        compiler_params=pltpu.CompilerParams(vmem_limit_bytes=OWN_KIB * 1024),
         cost_estimate=LONG,
         name="own",
     )(active, hgrad, spatial_weight, temporal_weight)
-    parts, map_odd, map_even, gin_far, gin_near = lax.optimization_barrier(
-        (parts, map_odd, map_even, gin_far, gin_near)
-    )
+    map_even = lax.ppermute(map_even, TA, to_even)
+    map_inner = lax.ppermute(map_odd, TA, to_inner)
+    parts, map_odd = lax.optimization_barrier((parts, map_odd))
     parts = lax.all_to_all(total_of(parts, 8, "plane_sums"), "z", 0, 0)
+    map_seam = lax.ppermute(map_odd, TA, to_seam)
+    parts, gin_far, gin_near = lax.optimization_barrier((parts, gin_far, gin_near))
     got = lax.all_to_all(total_of(parts, 32, "all_sums"), FLAT, 0, 0)
-
-    map_odd = lax.ppermute(map_odd, TA, to_odd)
-    map_even = lax.ppermute(map_even, TA, to_even)
+    rebuilt = finished(
+        rebuilt_kernel, "rebuilt", (map_seam, map_inner, map_even, mapped_own, outputs_fwd), LATE_KIB, LONG
+    )
     gin_far = lax.ppermute(gin_far, GZ, to_far)
     gin_near = lax.ppermute(gin_near, GZ, to_near)
 
-    rebuilt, grad_in = pl.pallas_call(
-        outputs_kernel,
-        in_specs=[IN_VMEM] * 8,
-        out_specs=[IN_VMEM] * 2,
-        out_shape=[shaped(2, 2, CH, PIX)] * 2,
-        compiler_params=PARAMS,
-        cost_estimate=LONG,
-        name="outputs",
-    )(map_odd, map_even, gin_far, gin_near, mapped_own, gin_own, outputs_fwd, cotangent)
-    got, rebuilt, grad_in = lax.optimization_barrier((got, rebuilt, grad_in))
+    got, rebuilt = lax.optimization_barrier((got, rebuilt))
 
     factor = 1.0 / math.sqrt(2 * ta * 2 * gz * PIX)
     grad_spatial, grad_bias, grad_temporal = pl.pallas_call(
@@ -319,8 +361,11 @@
         out_specs=[IN_VMEM] * 3,
         out_shape=[shaped(3, HID, WIN, dtype=F32), shaped(1, HID, dtype=F32), shaped(3, CH, HID, dtype=F32)],
         compiler_params=PARAMS,
+        cost_estimate=LONG,
         name="grads",
     )(got.reshape(512, 128))
+    gin_own, grad_spatial = lax.optimization_barrier((gin_own, grad_spatial))
+    grad_in = finished(gin_kernel, "grad_in", (gin_far, gin_near, gin_own, cotangent), LAST_KIB, LONG)
     return rebuilt, grad_in, grad_spatial, grad_bias.reshape(HID), grad_temporal
 
 

time: 69.7 us -> 68.3 us (0.980)
  local copies, waits for them, and re-layouts: 6.36 us -> 1.64 us
  waiting for transfers between devices: 7.14 us -> 9.35 us
  starting transfers between devices: 39.4 us -> 40.5 us
    all_to_all x1, waiting for transfers between devices: 0.45 us -> 5.48 us  [shards(): parts = lax.all_to_all(pay.reshape(32, 16, 128), FLAT, 0, 0)]
    all_to_all x1, waiting for transfers between devices: 5.54 us -> 1.65 us  [shards(): got = lax.all_to_all(total_of(parts, 32, 'all_sums'), FLAT, 0, 0)]
    unnamed x22 -> x16, local copies, waits for them, and re-layouts: 5.4 us -> 1.64 us
    pallas_call x1 -> x3, Pallas kernels: 1.02 us -> 4.18 us  [the longest x2 4.07 us: finished(): pl.pallas_call(kernel, in_specs=[IN_VMEM] * len(operands), out_specs=IN_V...]
    pallas_call x1, Pallas kernels: 4.42 us -> 1.37 us  [shards(): pl.pallas_call(own_kernel, in_specs=[IN_VMEM] * 4, out_specs=[IN_VMEM] *...]
    ppermute x1, starting transfers between devices: 0.01 us -> 1.76 us  [shards(): map_even = lax.ppermute(map_even, TA, to_even)]
    ppermute x1, waiting for transfers between devices: 1.14 us -> 2.2 us  [shards(): y1_far = lax.ppermute(y1_far, GZ, to_far)]
    squeeze x1 -> x0, local copies, waits for them, and re-layouts: 0.87 us -> none  [shards(): spatial_weight[0]]
  transfers between devices with their start and end apart: 11 -> 12, of which waited for: 3 -> 3; matrix products, arithmetic and copies ran while one was open for 2% -> 0% of each run, Pallas kernels for 9% -> 8%
where the time goes in v3:
time: 68.3 us; the launch traced here: 67.8 us
  starting transfers between devices  40.5 us (59%)
  Pallas kernels  15.4 us (23%)
  waiting for transfers between devices  9.35 us (14%)
  local copies, waits for them, and re-layouts  1.64 us (2%)
  between operations  0.83 us (1%)
    all_to_all x1, starting transfers between devices, shards(): parts = lax.all_to_all(pay.reshape(32, 16, 128), FLAT, 0, 0)  7.57 us
    pallas_call x1, Pallas kernels, shards(): pl.pallas_call(hidden_kernel, in_specs=[IN_VMEM] * 9, out_specs=[IN_VMEM]...  6.07 us
    ppermute x1, starting transfers between devices, shards(): g2_odd = lax.ppermute(g2_odd, TA, to_odd)  6.03 us
    all_to_all x1, starting transfers between devices, shards(): parts = lax.all_to_all(total_of(parts, 8, 'plane_sums'), 'z', 0, 0)  5.98 us
    all_to_all x1, starting transfers between devices, shards(): got = lax.all_to_all(total_of(parts, 32, 'all_sums'), FLAT, 0, 0)  5.69 us
    all_to_all x1, waiting for transfers between devices, shards(): parts = lax.all_to_all(pay.reshape(32, 16, 128), FLAT, 0, 0)  5.48 us
    ppermute x1, starting transfers between devices, shards(): map_seam = lax.ppermute(map_odd, TA, to_seam)  4.5 us
    ppermute x1, starting transfers between devices, shards(): y1_far = lax.ppermute(y1_far, GZ, to_far)  4.37 us
  transfers between devices with their start and end apart: 12, of which 3 were waited for; matrix products, arithmetic and copies ran while one was open for 0% of the time, Pallas kernels for 8%

profile of v3, /device:TPU:1, one launch (start us, length us, event | category | flops | bytes accessed | tf_op | source)
XLA Modules:
  0.0 67.8 jit_solution(9269737611075307038)
XLA Ops:
  0.6 0.0 copy-start.4
  0.6 0.0 copy-start.3
  0.7 0.0 copy-start
  0.7 0.0 copy-start.1
  0.7 1.3 %edges.1 = (bf16[1,2,32,1280]{3,2,1,0:T(8,128)(2,1)S(1)}, bf16[1,2,32,1280]{3,2,1,0:T(8,128)(2,1)S(1)}, bf16[2,1,32,1280]{3,2,1,0:T(8,128)(2,1)S(1)}, bf16[2,1,32,1280]{3,2,1,0:T(8,128)(2,1)S(1)}) custom-call(bf16[2,2,64,1280]{3,2,1,0:T(8,128)(2,1)} %fwd_ref.5, bf16[2,2,64,1280]{3,2,1,0:T(8,128)(2,1)} %cot_ref.5), custom_call_target="tpu_custom_call" | custom-call | flops 4000000000 | bytes 1000000 | tf_op jit(solution)/shard_map/edges/pallas_call | solution.py:293
  2.0 6.0 %collective-permute-start = (bf16[1,2,32,1280]{3,2,1,0:T(8,128)(2,1)S(1)}, bf16[1,2,32,1280]{3,2,1,0:T(8,128)(2,1)S(1)}, u32[]{:S(2)}, u32[]{:S(2)}) collective-permute-start(bf16[1,2,32,1280]{3,2,1,0:T(8,128)(2,1)S(1)} %get-tuple-element.33), channel_id=1, source_target_pairs={{1,2},{3,4},{5,6},{7,0},{2,1},{4,3},{6,5},{0,7},{9,10},{11,12},{13... | collective-permute-start | bytes 491528 | tf_op jit(solution)/shard_map/ppermute | solution.py:311
  8.0 0.0 collective-permute-start.1
  8.0 4.4 %collective-permute-start.2 = (bf16[2,1,32,1280]{3,2,1,0:T(8,128)(2,1)S(1)}, bf16[2,1,32,1280]{3,2,1,0:T(8,128)(2,1)S(1)}, u32[]{:S(2)}, u32[]{:S(2)}) collective-permute-start(bf16[2,1,32,1280]{3,2,1,0:T(8,128)(2,1)S(1)} %get-tuple-element.35), channel_id=1, source_target_pairs={{8,16},{24,32},{40,48},{56,64},{72,80},{88,96},{104,112},{120,128}... | collective-permute-start | bytes 491528 | tf_op jit(solution)/shard_map/ppermute | solution.py:313
  12.4 0.0 copy-start.2
  12.4 0.1 collective-permute-start.3
  12.5 0.0 copy-done
  12.5 0.0 copy-done.1
  12.5 0.5 copy-done.2
  13.1 0.1 weights.1
  13.2 0.0 collective-permute-done.odd_ref
  13.2 0.0 collective-permute-done.1.even_ref
  13.2 2.2 %collective-permute-done.2.far_ref = bf16[2,1,32,1280]{3,2,1,0:T(8,128)(2,1)S(1)} collective-permute-done((bf16[2,1,32,1280]{3,2,1,0:T(8,128)(2,1)S(1)}, bf16[2,1,32,1280]{3,2,1,0:T(8,128)(2,1)S(1)}, u32[]{:S(2)}, u32[]{:S(2)}) %collective-permute-start.2) | collective-permute-done | bytes 163872 | tf_op jit(solution)/shard_map/ppermute | solution.py:313
  15.4 0.0 collective-permute-done.3.near_ref
  15.4 0.0 copy-done.4
  15.4 0.0 copy-done.3
  15.4 6.1 %hidden.1 = (bf16[2,2,64,1280]{3,2,1,0:T(8,128)(2,1)S(1)}, bf16[2,2,64,1280]{3,2,1,0:T(8,128)(2,1)S(1)}, bf16[512,128]{1,0:T(8,128)(2,1)}) custom-call(bf16[1,2,32,1280]{3,2,1,0:T(8,128)(2,1)S(1)} %collective-permute-done.odd_ref, bf16[1,2,32,1280]{3,2,1,0:T(8,128)(2,1)S(1)} %collective-permute-done.1.even_ref, ...), custom_call_target="tpu_custom_call" | custom-call | flops 1000000000 | bytes 4000000 | tf_op jit(solution)/shard_map/hidden/pallas_call | solution.py:316
  21.5 7.6 %all-to-all-start = ((bf16[32,16,128]{2,1,0:T(8,128)(2,1)}), bf16[32,16,128]{2,1,0:T(8,128)(2,1)S(1)}, u32[]{:S(2)}, u32[]{:S(2)}) async-start(bf16[32,16,128]{2,1,0:T(8,128)(2,1)} %bitcast.1), calls=%async_computation | async-start | bytes 262144 | tf_op jit(solution)/shard_map/all_to_all | solution.py:330
  29.0 1.4 %own.1 = (f32[2,2,32,1280]{3,2,1,0:T(8,128)S(1)}, f32[2,2,32,1280]{3,2,1,0:T(8,128)S(1)}, bf16[1,2,32,1280]{3,2,1,0:T(8,128)(2,1)S(1)}, bf16[1,2,32,1280]{3,2,1,...) custom-call(bf16[2,2,64,1280]{3,2,1,0:T(8,128)(2,1)S(1)} %get-tuple-element.41.act_ref, ...), custom_call_target="tpu_custom_call" | custom-call | flops 2000000000 | bytes 4000000 | tf_op jit(solution)/shard_map/own/pallas_call | solution.py:331
  30.4 0.0 copy-start.6
  30.4 0.8 %copy-done.6 = f32[2,2,32,1280]{3,2,1,0:T(8,128)} copy-done((f32[2,2,32,1280]{3,2,1,0:T(8,128)}, f32[2,2,32,1280]{3,2,1,0:T(8,128)S(1)}, u32[]{:S(2)}) %copy-start.6) | copy-done | bytes 655384
  31.3 0.0 copy-start.5
  31.3 5.5 %all-to-all-done.refs_0_ = bf16[32,16,128]{2,1,0:T(8,128)(2,1)S(1)} async-done(((bf16[32,16,128]{2,1,0:T(8,128)(2,1)}), bf16[32,16,128]{2,1,0:T(8,128)(2,1)S(1)}, u32[]{:S(2)}, u32[]{:S(2)}) %all-to-all-start) | async-done | bytes 131104 | tf_op jit(solution)/shard_map/all_to_all | solution.py:330
  36.7 0.8 %plane_sums.1 = bf16[8,16,128]{2,1,0:T(8,128)(2,1)} custom-call(bf16[32,16,128]{2,1,0:T(8,128)(2,1)S(1)} %all-to-all-done.refs_0_), custom_call_target="tpu_custom_call" | custom-call | flops 2000000000 | bytes 4000000 | tf_op jit(solution)/shard_map/plane_sums/pallas_call | solution.py:260
  37.5 0.0 copy-done.5
  37.5 6.0 %all-to-all-start.1 = ((bf16[8,16,128]{2,1,0:T(8,128)(2,1)}), bf16[8,16,128]{2,1,0:T(8,128)(2,1)S(1)}, u32[]{:S(2)}, u32[]{:S(2)}) async-start(bf16[8,16,128]{2,1,0:T(8,128)(2,1)} %plane_sums.1), calls=%async_computation.1 | async-start | bytes 65536 | tf_op jit(solution)/shard_map/all_to_all | solution.py:345
  43.5 0.7 collective-permute-start.5
  44.2 1.8 %collective-permute-start.6 = (bf16[1,2,32,1280]{3,2,1,0:T(8,128)(2,1)S(1)}, bf16[1,2,32,1280]{3,2,1,0:T(8,128)(2,1)S(1)}, u32[]{:S(2)}, u32[]{:S(2)}) collective-permute-start(bf16[1,2,32,1280]{3,2,1,0:T(8,128)(2,1)S(1)} %get-tuple-element.49), channel_id=1, source_target_pairs={{0,1},{2,3},{4,5},{6,7},{1,0},{3,2},{5,4},{7,6},{8,9},{10,11},{12,... | collective-permute-start | bytes 491528 | tf_op jit(solution)/shard_map/ppermute | solution.py:342
  46.0 4.5 %collective-permute-start.4 = (bf16[1,2,32,1280]{3,2,1,0:T(8,128)(2,1)S(1)}, bf16[1,2,32,1280]{3,2,1,0:T(8,128)(2,1)S(1)}, u32[]{:S(2)}, u32[]{:S(2)}) collective-permute-start(bf16[1,2,32,1280]{3,2,1,0:T(8,128)(2,1)S(1)} %get-tuple-element.48), channel_id=1, source_target_pairs={{3,4},{7,0},{4,3},{0,7},{11,12},{15,8},{12,11},{8,15},{19,20},{23,... | collective-permute-start | bytes 491528 | tf_op jit(solution)/shard_map/ppermute | solution.py:346
  50.5 0.0 all-to-all-done.1.refs_0_
  50.5 0.8 %all_sums.1 = bf16[32,16,128]{2,1,0:T(8,128)(2,1)} custom-call(bf16[8,16,128]{2,1,0:T(8,128)(2,1)S(1)} %all-to-all-done.1.refs_0_), custom_call_target="tpu_custom_call" | custom-call | flops 2000000000 | bytes 4000000 | tf_op jit(solution)/shard_map/all_sums/pallas_call | solution.py:260
  51.3 5.7 %all-to-all-start.2 = ((bf16[32,16,128]{2,1,0:T(8,128)(2,1)}), bf16[32,16,128]{2,1,0:T(8,128)(2,1)S(1)}, u32[]{:S(2)}, u32[]{:S(2)}) async-start(bf16[32,16,128]{2,1,0:T(8,128)(2,1)} %all_sums.1), calls=%async_computation.2 | async-start | bytes 262144 | tf_op jit(solution)/shard_map/all_to_all | solution.py:348
  57.0 3.8 %collective-permute-start.7 = (bf16[2,1,32,1280]{3,2,1,0:T(8,128)(2,1)S(1)}, bf16[2,1,32,1280]{3,2,1,0:T(8,128)(2,1)S(1)}, u32[]{:S(2)}, u32[]{:S(2)}) collective-permute-start(bf16[2,1,32,1280]{3,2,1,0:T(8,128)(2,1)S(1)} %get-tuple-element.52), channel_id=1, source_target_pairs={{8,16},{24,32},{40,48},{56,64},{72,80},{88,96},{104,112},{120,128}... | collective-permute-start | bytes 491528 | tf_op jit(solution)/shard_map/ppermute | solution.py:352
  60.8 0.1 collective-permute-start.8
  60.9 0.0 collective-permute-done.6.even_ref
  60.9 0.0 collective-permute-done.5.inner_ref
  60.9 0.0 collective-permute-done.4.seam_ref
  60.9 2.1 %rebuilt.1 = bf16[2,2,32,1280]{3,2,1,0:T(8,128)(2,1)} custom-call(bf16[1,2,32,1280]{3,2,1,0:T(8,128)(2,1)S(1)} %collective-permute-done.4.seam_ref, bf16[1,2,32,1280]{3,2,1,0:T(8,128)(2,1)S(1)} %collective-permute-done.5.inner_ref, bf16[1,2,32,1280]{3,2,1,0:T(8,128)(2,1)S(1)} %collective-permute-done.6.even_ref, f32[2,2,32,1280]{3,2,1,0:T(8,128)} %copy-done.5, ...), custom_call_target="tpu_custom_call" | custom-call | flops 2000000000 | bytes 4000000 | tf_op jit(solution)/shard_map/rebuilt/pallas_call | solution.py:272
  63.1 1.7 %all-to-all-done.2 = bf16[32,16,128]{2,1,0:T(8,128)(2,1)S(1)} async-done(((bf16[32,16,128]{2,1,0:T(8,128)(2,1)}), bf16[32,16,128]{2,1,0:T(8,128)(2,1)S(1)}, u32[]{:S(2)}, u32[]{:S(2)}) %all-to-all-start.2) | async-done | bytes 131104 | tf_op jit(solution)/shard_map/all_to_all | solution.py:348
  64.7 0.0 copy-start.7
  64.7 0.9 %grads.1 = (f32[3,64,288]{2,1,0:T(8,128)}, f32[1,64]{1,0:T(1,128)}, f32[3,32,64]{2,1,0:T(8,128)}) custom-call(bf16[512,128]{1,0:T(8,128)(2,1)S(1)} %bitcast.4), custom_call_target="tpu_custom_call" | custom-call | flops 2000000000 | bytes 4000000 | tf_op jit(solution)/shard_map/grads/pallas_call | solution.py:358
  65.6 0.0 collective-permute-done.7.far_ref
  65.6 0.0 collective-permute-done.8.near_ref
  65.6 0.2 copy-done.7
  65.8 1.9 %grad_in.1 = bf16[2,2,32,1280]{3,2,1,0:T(8,128)(2,1)} custom-call(bf16[2,1,32,1280]{3,2,1,0:T(8,128)(2,1)S(1)} %collective-permute-done.7.far_ref, bf16[2,1,32,1280]{3,2,1,0:T(8,128)(2,1)S(1)} %collective-permute-done.8.near_ref, f32[2,2,32,1280]{3,2,1,0:T(8,128)S(1)} %copy-done.7, bf16[2,2,64,1280]{3,2,1,0:T(8,128)(2,1)} %cot_ref.5), custom_call_target="tpu_custom_call" | custom-call | flops 2000000000 | bytes 4000000 | tf_op jit(solution)/shard_map/grad_in/pallas_call | solution.py:272
Async XLA Ops:
  0.6 14.8 %copy-start.4 = (bf16[2,2,64,1280]{3,2,1,0:T(8,128)(2,1)S(1)}, bf16[2,2,64,1280]{3,2,1,0:T(8,128)(2,1)}, u32[]{:S(2)}) copy-start(bf16[2,2,64,1280]{3,2,1,0:T(8,128)(2,1)} %cot_ref.5) | copy-start | bytes 1966084
  0.6 14.7 %copy-start.3 = (bf16[2,2,64,1280]{3,2,1,0:T(8,128)(2,1)S(1)}, bf16[2,2,64,1280]{3,2,1,0:T(8,128)(2,1)}, u32[]{:S(2)}) copy-start(bf16[2,2,64,1280]{3,2,1,0:T(8,128)(2,1)} %fwd_ref.5) | copy-start | bytes 1966084
  0.7 11.9 %copy-start = (bf16[3,64,288]{2,1,0:T(8,128)(2,1)S(1)}, bf16[3,64,288]{2,1,0:T(8,128)(2,1)}, u32[]{:S(2)}) copy-start(bf16[3,64,288]{2,1,0:T(8,128)(2,1)} %sw_ref.3) | copy-start | bytes 331780
  0.7 11.9 %copy-start.1 = (bf16[3,32,64]{2,1,0:T(8,128)(2,1)S(1)}, bf16[3,32,64]{2,1,0:T(8,128)(2,1)}, u32[]{:S(2)}) copy-start(bf16[3,32,64]{2,1,0:T(8,128)(2,1)} %tw_ref.3) | copy-start | bytes 36868
  2.0 11.2 %collective-permute-start = (bf16[1,2,32,1280]{3,2,1,0:T(8,128)(2,1)S(1)}, bf16[1,2,32,1280]{3,2,1,0:T(8,128)(2,1)S(1)}, u32[]{:S(2)}, u32[]{:S(2)}) collective-permute-start(bf16[1,2,32,1280]{3,2,1,0:T(8,128)(2,1)S(1)} %get-tuple-element.33), channel_id=1, source_target_pairs={{1,2},{3,4},{5,6},{7,0},{2,1},{4,3},{6,5},{0,7},{9,10},{11,12},{13... | collective-permute-start | bytes 491528 | tf_op jit(solution)/shard_map/ppermute | solution.py:311
  8.0 5.2 %collective-permute-start.1 = (bf16[1,2,32,1280]{3,2,1,0:T(8,128)(2,1)S(1)}, bf16[1,2,32,1280]{3,2,1,0:T(8,128)(2,1)S(1)}, u32[]{:S(2)}, u32[]{:S(2)}) collective-permute-start(bf16[1,2,32,1280]{3,2,1,0:T(8,128)(2,1)S(1)} %get-tuple-element.34), channel_id=1, source_target_pairs={{0,1},{2,3},{4,5},{6,7},{1,0},{3,2},{5,4},{7,6},{8,9},{10,11},{12,... | collective-permute-start | bytes 491528 | tf_op jit(solution)/shard_map/ppermute | solution.py:312
  8.0 7.4 %collective-permute-start.2 = (bf16[2,1,32,1280]{3,2,1,0:T(8,128)(2,1)S(1)}, bf16[2,1,32,1280]{3,2,1,0:T(8,128)(2,1)S(1)}, u32[]{:S(2)}, u32[]{:S(2)}) collective-permute-start(bf16[2,1,32,1280]{3,2,1,0:T(8,128)(2,1)S(1)} %get-tuple-element.35), channel_id=1, source_target_pairs={{8,16},{24,32},{40,48},{56,64},{72,80},{88,96},{104,112},{120,128}... | collective-permute-start | bytes 491528 | tf_op jit(solution)/shard_map/ppermute | solution.py:313
  12.4 0.7 copy-start.2
  12.4 3.0 %collective-permute-start.3 = (bf16[2,1,32,1280]{3,2,1,0:T(8,128)(2,1)S(1)}, bf16[2,1,32,1280]{3,2,1,0:T(8,128)(2,1)S(1)}, u32[]{:S(2)}, u32[]{:S(2)}) collective-permute-start(bf16[2,1,32,1280]{3,2,1,0:T(8,128)(2,1)S(1)} %get-tuple-element.36), channel_id=1, source_target_pairs={{0,8},{16,24},{32,40},{48,56},{64,72},{80,88},{96,104},{112,120},{... | collective-permute-start | bytes 491528 | tf_op jit(solution)/shard_map/ppermute | solution.py:314
  21.5 15.3 %all-to-all-start = ((bf16[32,16,128]{2,1,0:T(8,128)(2,1)}), bf16[32,16,128]{2,1,0:T(8,128)(2,1)S(1)}, u32[]{:S(2)}, u32[]{:S(2)}) async-start(bf16[32,16,128]{2,1,0:T(8,128)(2,1)} %bitcast.1), calls=%async_computation | async-start | bytes 262144 | tf_op jit(solution)/shard_map/all_to_all | solution.py:330
  30.4 0.8 %copy-start.6 = (f32[2,2,32,1280]{3,2,1,0:T(8,128)}, f32[2,2,32,1280]{3,2,1,0:T(8,128)S(1)}, u32[]{:S(2)}) copy-start(f32[2,2,32,1280]{3,2,1,0:T(8,128)S(1)} %get-tuple-element.57.own_ref) | copy-start | bytes 1966084
  31.3 6.3 %copy-start.5 = (f32[2,2,32,1280]{3,2,1,0:T(8,128)}, f32[2,2,32,1280]{3,2,1,0:T(8,128)S(1)}, u32[]{:S(2)}) copy-start(f32[2,2,32,1280]{3,2,1,0:T(8,128)S(1)} %get-tuple-element.50.mapped_ref) | copy-start | bytes 1966084
  37.5 12.9 %all-to-all-start.1 = ((bf16[8,16,128]{2,1,0:T(8,128)(2,1)}), bf16[8,16,128]{2,1,0:T(8,128)(2,1)S(1)}, u32[]{:S(2)}, u32[]{:S(2)}) async-start(bf16[8,16,128]{2,1,0:T(8,128)(2,1)} %plane_sums.1), calls=%async_computation.1 | async-start | bytes 65536 | tf_op jit(solution)/shard_map/all_to_all | solution.py:345
  43.5 17.4 %collective-permute-start.5 = (bf16[1,2,32,1280]{3,2,1,0:T(8,128)(2,1)S(1)}, bf16[1,2,32,1280]{3,2,1,0:T(8,128)(2,1)S(1)}, u32[]{:S(2)}, u32[]{:S(2)}) collective-permute-start(bf16[1,2,32,1280]{3,2,1,0:T(8,128)(2,1)S(1)} %get-tuple-element.48), channel_id=1, source_target_pairs={{1,2},{5,6},{2,1},{6,5},{9,10},{13,14},{10,9},{14,13},{17,18},{21,... | collective-permute-start | bytes 491528 | tf_op jit(solution)/shard_map/ppermute | solution.py:343
  44.2 16.7 %collective-permute-start.6 = (bf16[1,2,32,1280]{3,2,1,0:T(8,128)(2,1)S(1)}, bf16[1,2,32,1280]{3,2,1,0:T(8,128)(2,1)S(1)}, u32[]{:S(2)}, u32[]{:S(2)}) collective-permute-start(bf16[1,2,32,1280]{3,2,1,0:T(8,128)(2,1)S(1)} %get-tuple-element.49), channel_id=1, source_target_pairs={{0,1},{2,3},{4,5},{6,7},{1,0},{3,2},{5,4},{7,6},{8,9},{10,11},{12,... | collective-permute-start | bytes 491528 | tf_op jit(solution)/shard_map/ppermute | solution.py:342
  46.0 14.9 %collective-permute-start.4 = (bf16[1,2,32,1280]{3,2,1,0:T(8,128)(2,1)S(1)}, bf16[1,2,32,1280]{3,2,1,0:T(8,128)(2,1)S(1)}, u32[]{:S(2)}, u32[]{:S(2)}) collective-permute-start(bf16[1,2,32,1280]{3,2,1,0:T(8,128)(2,1)S(1)} %get-tuple-element.48), channel_id=1, source_target_pairs={{3,4},{7,0},{4,3},{0,7},{11,12},{15,8},{12,11},{8,15},{19,20},{23,... | collective-permute-start | bytes 491528 | tf_op jit(solution)/shard_map/ppermute | solution.py:346
  51.3 13.4 %all-to-all-start.2 = ((bf16[32,16,128]{2,1,0:T(8,128)(2,1)}), bf16[32,16,128]{2,1,0:T(8,128)(2,1)S(1)}, u32[]{:S(2)}, u32[]{:S(2)}) async-start(bf16[32,16,128]{2,1,0:T(8,128)(2,1)} %all_sums.1), calls=%async_computation.2 | async-start | bytes 262144 | tf_op jit(solution)/shard_map/all_to_all | solution.py:348
  57.0 8.6 %collective-permute-start.7 = (bf16[2,1,32,1280]{3,2,1,0:T(8,128)(2,1)S(1)}, bf16[2,1,32,1280]{3,2,1,0:T(8,128)(2,1)S(1)}, u32[]{:S(2)}, u32[]{:S(2)}) collective-permute-start(bf16[2,1,32,1280]{3,2,1,0:T(8,128)(2,1)S(1)} %get-tuple-element.52), channel_id=1, source_target_pairs={{8,16},{24,32},{40,48},{56,64},{72,80},{88,96},{104,112},{120,128}... | collective-permute-start | bytes 491528 | tf_op jit(solution)/shard_map/ppermute | solution.py:352
  60.8 4.8 %collective-permute-start.8 = (bf16[2,1,32,1280]{3,2,1,0:T(8,128)(2,1)S(1)}, bf16[2,1,32,1280]{3,2,1,0:T(8,128)(2,1)S(1)}, u32[]{:S(2)}, u32[]{:S(2)}) collective-permute-start(bf16[2,1,32,1280]{3,2,1,0:T(8,128)(2,1)S(1)} %get-tuple-element.53), channel_id=1, source_target_pairs={{0,8},{16,24},{32,40},{48,56},{64,72},{80,88},{96,104},{112,120},{... | collective-permute-start | bytes 491528 | tf_op jit(solution)/shard_map/ppermute | solution.py:353
  64.7 1.1 %copy-start.7 = (f32[2,2,32,1280]{3,2,1,0:T(8,128)S(1)}, f32[2,2,32,1280]{3,2,1,0:T(8,128)}, u32[]{:S(2)}) copy-start(f32[2,2,32,1280]{3,2,1,0:T(8,128)} %copy-done.6) | copy-start | bytes 1966084

commit v4 on v3

--- a/solution.py
+++ b/solution.py
@@ -18,7 +18,7 @@
 VMEM_LIMIT = 24 * 1024 * 1024
 EDGES_KIB = 54200
 LATE_KIB = 54600
-LAST_KIB = 54000
+LAST_KIB = 24000
 OWN_KIB = 24000
 GZ = ("yl", "z", "c")
 TA = ("yh", "x")
@@ -127,9 +127,14 @@
             tgrad = tpart if tgrad is None else tgrad + tpart
             bpart = jnp.sum(hgrad.astype(F32), axis=1, keepdims=True)
             bgrad = bpart if bgrad is None else bgrad + bpart
-            for dz in range(3):
-                part = nt(hgrad, columns[f, (z + dz) * WIN : (z + dz + 1) * WIN, :])
-                sgrad[dz] = part if sgrad[dz] is None else sgrad[dz] + part
+        both = hgrad_ref[f].reshape(2 * HID, PIX)
+        for p in range(4):
+            part = nt(both if 0 < p < 3 else hgrad_ref[f, p // 3], columns[f, p * WIN : (p + 1) * WIN, :])
+            for z in range(2):
+                dz = p - z
+                if 0 <= dz < 3:
+                    term = part[z * HID : (z + 1) * HID] if 0 < p < 3 else part
+                    sgrad[dz] = term if sgrad[dz] is None else sgrad[dz] + term
     for dz in range(3):
         for side in range(2):
             at = (2 * dz + side) * HID

time: 68.3 us -> 66.7 us (0.977)
  Pallas kernels: 15.4 us -> 13.8 us
  local copies, waits for them, and re-layouts: 1.64 us -> 2.5 us
  waiting for transfers between devices: 9.35 us -> 8.49 us
    pallas_call x2, Pallas kernels: 4.07 us -> 2.99 us  [finished(): pl.pallas_call(kernel, in_specs=[IN_VMEM] * len(operands), out_specs=IN_V...]
    unnamed x16, local copies, waits for them, and re-layouts: 1.64 us -> 2.5 us
    all_to_all x1, waiting for transfers between devices: 5.48 us -> 4.62 us  [shards(): parts = lax.all_to_all(pay.reshape(32, 16, 128), FLAT, 0, 0)]
where the time goes in v4:
time: 66.7 us; the launch traced here: 66.2 us
  starting transfers between devices  40.5 us (61%)
  Pallas kernels  13.8 us (21%)
  waiting for transfers between devices  8.49 us (13%)
  local copies, waits for them, and re-layouts  2.5 us (4%)
  between operations  0.83 us (1%)
    all_to_all x1, starting transfers between devices, shards(): parts = lax.all_to_all(pay.reshape(32, 16, 128), FLAT, 0, 0)  7.56 us
    ppermute x1, starting transfers between devices, shards(): g2_odd = lax.ppermute(g2_odd, TA, to_odd)  6.03 us
    all_to_all x1, starting transfers between devices, shards(): parts = lax.all_to_all(total_of(parts, 8, 'plane_sums'), 'z', 0, 0)  5.99 us
    all_to_all x1, starting transfers between devices, shards(): got = lax.all_to_all(total_of(parts, 32, 'all_sums'), FLAT, 0, 0)  5.69 us
    pallas_call x1, Pallas kernels, shards(): pl.pallas_call(hidden_kernel, in_specs=[IN_VMEM] * 9, out_specs=[IN_VMEM]...  5.58 us
    all_to_all x1, waiting for transfers between devices, shards(): parts = lax.all_to_all(pay.reshape(32, 16, 128), FLAT, 0, 0)  4.62 us
    ppermute x1, starting transfers between devices, shards(): map_seam = lax.ppermute(map_odd, TA, to_seam)  4.5 us
    ppermute x1, starting transfers between devices, shards(): y1_far = lax.ppermute(y1_far, GZ, to_far)  4.37 us
  transfers between devices with their start and end apart: 12, of which 3 were waited for; matrix products, arithmetic and copies ran while one was open for 0% of the time, Pallas kernels for 8%

profile of v4, /device:TPU:1, one launch (start us, length us, event | category | flops | bytes accessed | tf_op | source)
XLA Modules:
  0.0 66.2 jit_solution(1809686038672256734)
XLA Ops:
  0.6 0.0 copy-start.4
  0.6 0.0 copy-start.3
  0.7 0.0 copy-start
  0.7 0.0 copy-start.1
  0.7 1.3 %edges.1 = (bf16[1,2,32,1280]{3,2,1,0:T(8,128)(2,1)S(1)}, bf16[1,2,32,1280]{3,2,1,0:T(8,128)(2,1)S(1)}, bf16[2,1,32,1280]{3,2,1,0:T(8,128)(2,1)S(1)}, bf16[2,1,32,1280]{3,2,1,0:T(8,128)(2,1)S(1)}) custom-call(bf16[2,2,64,1280]{3,2,1,0:T(8,128)(2,1)} %fwd_ref.5, bf16[2,2,64,1280]{3,2,1,0:T(8,128)(2,1)} %cot_ref.5), custom_call_target="tpu_custom_call" | custom-call | flops 4000000000 | bytes 1000000 | tf_op jit(solution)/shard_map/edges/pallas_call | solution.py:298
  2.0 6.0 %collective-permute-start = (bf16[1,2,32,1280]{3,2,1,0:T(8,128)(2,1)S(1)}, bf16[1,2,32,1280]{3,2,1,0:T(8,128)(2,1)S(1)}, u32[]{:S(2)}, u32[]{:S(2)}) collective-permute-start(bf16[1,2,32,1280]{3,2,1,0:T(8,128)(2,1)S(1)} %get-tuple-element.33), channel_id=1, source_target_pairs={{1,2},{3,4},{5,6},{7,0},{2,1},{4,3},{6,5},{0,7},{9,10},{11,12},{13... | collective-permute-start | bytes 491528 | tf_op jit(solution)/shard_map/ppermute | solution.py:316
  8.0 0.0 collective-permute-start.1
  8.0 4.4 %collective-permute-start.2 = (bf16[2,1,32,1280]{3,2,1,0:T(8,128)(2,1)S(1)}, bf16[2,1,32,1280]{3,2,1,0:T(8,128)(2,1)S(1)}, u32[]{:S(2)}, u32[]{:S(2)}) collective-permute-start(bf16[2,1,32,1280]{3,2,1,0:T(8,128)(2,1)S(1)} %get-tuple-element.35), channel_id=1, source_target_pairs={{8,16},{24,32},{40,48},{56,64},{72,80},{88,96},{104,112},{120,128}... | collective-permute-start | bytes 491528 | tf_op jit(solution)/shard_map/ppermute | solution.py:318
  12.4 0.0 copy-start.2
  12.4 0.1 collective-permute-start.3
  12.5 0.0 copy-done
  12.5 0.0 copy-done.1
  12.5 0.5 copy-done.2
  13.1 0.1 weights.1
  13.2 0.0 collective-permute-done.odd_ref
  13.2 0.0 collective-permute-done.1.even_ref
  13.2 2.2 %collective-permute-done.2.far_ref = bf16[2,1,32,1280]{3,2,1,0:T(8,128)(2,1)S(1)} collective-permute-done((bf16[2,1,32,1280]{3,2,1,0:T(8,128)(2,1)S(1)}, bf16[2,1,32,1280]{3,2,1,0:T(8,128)(2,1)S(1)}, u32[]{:S(2)}, u32[]{:S(2)}) %collective-permute-start.2) | collective-permute-done | bytes 163872 | tf_op jit(solution)/shard_map/ppermute | solution.py:318
  15.4 0.0 collective-permute-done.3.near_ref
  15.4 0.0 copy-done.4
  15.4 0.0 copy-done.3
  15.4 5.6 %hidden.1 = (bf16[2,2,64,1280]{3,2,1,0:T(8,128)(2,1)S(1)}, bf16[2,2,64,1280]{3,2,1,0:T(8,128)(2,1)S(1)}, bf16[512,128]{1,0:T(8,128)(2,1)}) custom-call(bf16[1,2,32,1280]{3,2,1,0:T(8,128)(2,1)S(1)} %collective-permute-done.odd_ref, bf16[1,2,32,1280]{3,2,1,0:T(8,128)(2,1)S(1)} %collective-permute-done.1.even_ref, ...), custom_call_target="tpu_custom_call" | custom-call | flops 1000000000 | bytes 4000000 | tf_op jit(solution)/shard_map/hidden/pallas_call | solution.py:321
  21.0 7.6 %all-to-all-start = ((bf16[32,16,128]{2,1,0:T(8,128)(2,1)}), bf16[32,16,128]{2,1,0:T(8,128)(2,1)S(1)}, u32[]{:S(2)}, u32[]{:S(2)}) async-start(bf16[32,16,128]{2,1,0:T(8,128)(2,1)} %bitcast.1), calls=%async_computation | async-start | bytes 262144 | tf_op jit(solution)/shard_map/all_to_all | solution.py:335
  28.5 1.4 %own.1 = (f32[2,2,32,1280]{3,2,1,0:T(8,128)S(1)}, f32[2,2,32,1280]{3,2,1,0:T(8,128)S(1)}, bf16[1,2,32,1280]{3,2,1,0:T(8,128)(2,1)S(1)}, bf16[1,2,32,1280]{3,2,1,...) custom-call(bf16[2,2,64,1280]{3,2,1,0:T(8,128)(2,1)S(1)} %get-tuple-element.41.act_ref, ...), custom_call_target="tpu_custom_call" | custom-call | flops 2000000000 | bytes 4000000 | tf_op jit(solution)/shard_map/own/pallas_call | solution.py:336
  29.9 0.0 copy-start.5
  29.9 0.8 %copy-done.5 = f32[2,2,32,1280]{3,2,1,0:T(8,128)} copy-done((f32[2,2,32,1280]{3,2,1,0:T(8,128)}, f32[2,2,32,1280]{3,2,1,0:T(8,128)S(1)}, u32[]{:S(2)}) %copy-start.5) | copy-done | bytes 655384
  30.8 0.0 copy-start.6
  30.8 0.9 %copy-done.6 = f32[2,2,32,1280]{3,2,1,0:T(8,128)} copy-done((f32[2,2,32,1280]{3,2,1,0:T(8,128)}, f32[2,2,32,1280]{3,2,1,0:T(8,128)S(1)}, u32[]{:S(2)}) %copy-start.6) | copy-done | bytes 655384
  31.6 4.6 %all-to-all-done.refs_0_ = bf16[32,16,128]{2,1,0:T(8,128)(2,1)S(1)} async-done(((bf16[32,16,128]{2,1,0:T(8,128)(2,1)}), bf16[32,16,128]{2,1,0:T(8,128)(2,1)S(1)}, u32[]{:S(2)}, u32[]{:S(2)}) %all-to-all-start) | async-done | bytes 131104 | tf_op jit(solution)/shard_map/all_to_all | solution.py:335
  36.2 0.8 %plane_sums.1 = bf16[8,16,128]{2,1,0:T(8,128)(2,1)} custom-call(bf16[32,16,128]{2,1,0:T(8,128)(2,1)S(1)} %all-to-all-done.refs_0_), custom_call_target="tpu_custom_call" | custom-call | flops 2000000000 | bytes 4000000 | tf_op jit(solution)/shard_map/plane_sums/pallas_call | solution.py:265
  37.0 6.0 %all-to-all-start.1 = ((bf16[8,16,128]{2,1,0:T(8,128)(2,1)}), bf16[8,16,128]{2,1,0:T(8,128)(2,1)S(1)}, u32[]{:S(2)}, u32[]{:S(2)}) async-start(bf16[8,16,128]{2,1,0:T(8,128)(2,1)} %plane_sums.1), calls=%async_computation.1 | async-start | bytes 65536 | tf_op jit(solution)/shard_map/all_to_all | solution.py:350
  43.0 0.7 collective-permute-start.5
  43.7 1.8 %collective-permute-start.6 = (bf16[1,2,32,1280]{3,2,1,0:T(8,128)(2,1)S(1)}, bf16[1,2,32,1280]{3,2,1,0:T(8,128)(2,1)S(1)}, u32[]{:S(2)}, u32[]{:S(2)}) collective-permute-start(bf16[1,2,32,1280]{3,2,1,0:T(8,128)(2,1)S(1)} %get-tuple-element.49), channel_id=1, source_target_pairs={{0,1},{2,3},{4,5},{6,7},{1,0},{3,2},{5,4},{7,6},{8,9},{10,11},{12,... | collective-permute-start | bytes 491528 | tf_op jit(solution)/shard_map/ppermute | solution.py:347
  45.5 4.5 %collective-permute-start.4 = (bf16[1,2,32,1280]{3,2,1,0:T(8,128)(2,1)S(1)}, bf16[1,2,32,1280]{3,2,1,0:T(8,128)(2,1)S(1)}, u32[]{:S(2)}, u32[]{:S(2)}) collective-permute-start(bf16[1,2,32,1280]{3,2,1,0:T(8,128)(2,1)S(1)} %get-tuple-element.48), channel_id=1, source_target_pairs={{3,4},{7,0},{4,3},{0,7},{11,12},{15,8},{12,11},{8,15},{19,20},{23,... | collective-permute-start | bytes 491528 | tf_op jit(solution)/shard_map/ppermute | solution.py:351
  50.0 0.0 all-to-all-done.1.refs_0_
  50.0 0.8 %all_sums.1 = bf16[32,16,128]{2,1,0:T(8,128)(2,1)} custom-call(bf16[8,16,128]{2,1,0:T(8,128)(2,1)S(1)} %all-to-all-done.1.refs_0_), custom_call_target="tpu_custom_call" | custom-call | flops 2000000000 | bytes 4000000 | tf_op jit(solution)/shard_map/all_sums/pallas_call | solution.py:265
  50.8 5.7 %all-to-all-start.2 = ((bf16[32,16,128]{2,1,0:T(8,128)(2,1)}), bf16[32,16,128]{2,1,0:T(8,128)(2,1)S(1)}, u32[]{:S(2)}, u32[]{:S(2)}) async-start(bf16[32,16,128]{2,1,0:T(8,128)(2,1)} %all_sums.1), calls=%async_computation.2 | async-start | bytes 262144 | tf_op jit(solution)/shard_map/all_to_all | solution.py:353
  56.5 3.8 %collective-permute-start.7 = (bf16[2,1,32,1280]{3,2,1,0:T(8,128)(2,1)S(1)}, bf16[2,1,32,1280]{3,2,1,0:T(8,128)(2,1)S(1)}, u32[]{:S(2)}, u32[]{:S(2)}) collective-permute-start(bf16[2,1,32,1280]{3,2,1,0:T(8,128)(2,1)S(1)} %get-tuple-element.52), channel_id=1, source_target_pairs={{8,16},{24,32},{40,48},{56,64},{72,80},{88,96},{104,112},{120,128}... | collective-permute-start | bytes 491528 | tf_op jit(solution)/shard_map/ppermute | solution.py:357
  60.3 0.1 collective-permute-start.8
  60.4 0.0 collective-permute-done.6.even_ref
  60.4 0.0 collective-permute-done.5.inner_ref
  60.4 0.0 collective-permute-done.4.seam_ref
  60.4 2.1 %rebuilt.1 = bf16[2,2,32,1280]{3,2,1,0:T(8,128)(2,1)} custom-call(bf16[1,2,32,1280]{3,2,1,0:T(8,128)(2,1)S(1)} %collective-permute-done.4.seam_ref, bf16[1,2,32,1280]{3,2,1,0:T(8,128)(2,1)S(1)} %collective-permute-done.5.inner_ref, bf16[1,2,32,1280]{3,2,1,0:T(8,128)(2,1)S(1)} %collective-permute-done.6.even_ref, f32[2,2,32,1280]{3,2,1,0:T(8,128)} %copy-done.5, ...), custom_call_target="tpu_custom_call" | custom-call | flops 2000000000 | bytes 4000000 | tf_op jit(solution)/shard_map/rebuilt/pallas_call | solution.py:277
  62.6 1.7 %all-to-all-done.2 = bf16[32,16,128]{2,1,0:T(8,128)(2,1)S(1)} async-done(((bf16[32,16,128]{2,1,0:T(8,128)(2,1)}), bf16[32,16,128]{2,1,0:T(8,128)(2,1)S(1)}, u32[]{:S(2)}, u32[]{:S(2)}) %all-to-all-start.2) | async-done | bytes 131104 | tf_op jit(solution)/shard_map/all_to_all | solution.py:353
  64.2 0.0 copy-start.7
  64.2 0.9 %grads.1 = (f32[3,64,288]{2,1,0:T(8,128)}, f32[1,64]{1,0:T(1,128)}, f32[3,32,64]{2,1,0:T(8,128)}) custom-call(bf16[512,128]{1,0:T(8,128)(2,1)S(1)} %bitcast.4), custom_call_target="tpu_custom_call" | custom-call | flops 2000000000 | bytes 4000000 | tf_op jit(solution)/shard_map/grads/pallas_call | solution.py:363
  65.1 0.0 collective-permute-done.7.far_ref
  65.1 0.0 collective-permute-done.8.near_ref
  65.1 0.2 copy-done.7
  65.3 0.9 %grad_in.1 = bf16[2,2,32,1280]{3,2,1,0:T(8,128)(2,1)} custom-call(bf16[2,1,32,1280]{3,2,1,0:T(8,128)(2,1)S(1)} %collective-permute-done.7.far_ref, bf16[2,1,32,1280]{3,2,1,0:T(8,128)(2,1)S(1)} %collective-permute-done.8.near_ref, f32[2,2,32,1280]{3,2,1,0:T(8,128)S(1)} %copy-done.7, bf16[2,2,64,1280]{3,2,1,0:T(8,128)(2,1)S(1)} %copy-done.4), custom_call_target="tpu_custom_call" | custom-call | flops 2000000000 | bytes 4000000 | tf_op jit(solution)/shard_map/grad_in/pallas_call | solution.py:277
Async XLA Ops:
  0.6 14.8 %copy-start.4 = (bf16[2,2,64,1280]{3,2,1,0:T(8,128)(2,1)S(1)}, bf16[2,2,64,1280]{3,2,1,0:T(8,128)(2,1)}, u32[]{:S(2)}) copy-start(bf16[2,2,64,1280]{3,2,1,0:T(8,128)(2,1)} %cot_ref.5) | copy-start | bytes 1966084
  0.6 14.7 %copy-start.3 = (bf16[2,2,64,1280]{3,2,1,0:T(8,128)(2,1)S(1)}, bf16[2,2,64,1280]{3,2,1,0:T(8,128)(2,1)}, u32[]{:S(2)}) copy-start(bf16[2,2,64,1280]{3,2,1,0:T(8,128)(2,1)} %fwd_ref.5) | copy-start | bytes 1966084
  0.7 11.9 %copy-start = (bf16[3,64,288]{2,1,0:T(8,128)(2,1)S(1)}, bf16[3,64,288]{2,1,0:T(8,128)(2,1)}, u32[]{:S(2)}) copy-start(bf16[3,64,288]{2,1,0:T(8,128)(2,1)} %sw_ref.3) | copy-start | bytes 331780
  0.7 11.9 %copy-start.1 = (bf16[3,32,64]{2,1,0:T(8,128)(2,1)S(1)}, bf16[3,32,64]{2,1,0:T(8,128)(2,1)}, u32[]{:S(2)}) copy-start(bf16[3,32,64]{2,1,0:T(8,128)(2,1)} %tw_ref.3) | copy-start | bytes 36868
  2.0 11.2 %collective-permute-start = (bf16[1,2,32,1280]{3,2,1,0:T(8,128)(2,1)S(1)}, bf16[1,2,32,1280]{3,2,1,0:T(8,128)(2,1)S(1)}, u32[]{:S(2)}, u32[]{:S(2)}) collective-permute-start(bf16[1,2,32,1280]{3,2,1,0:T(8,128)(2,1)S(1)} %get-tuple-element.33), channel_id=1, source_target_pairs={{1,2},{3,4},{5,6},{7,0},{2,1},{4,3},{6,5},{0,7},{9,10},{11,12},{13... | collective-permute-start | bytes 491528 | tf_op jit(solution)/shard_map/ppermute | solution.py:316
  8.0 5.2 %collective-permute-start.1 = (bf16[1,2,32,1280]{3,2,1,0:T(8,128)(2,1)S(1)}, bf16[1,2,32,1280]{3,2,1,0:T(8,128)(2,1)S(1)}, u32[]{:S(2)}, u32[]{:S(2)}) collective-permute-start(bf16[1,2,32,1280]{3,2,1,0:T(8,128)(2,1)S(1)} %get-tuple-element.34), channel_id=1, source_target_pairs={{0,1},{2,3},{4,5},{6,7},{1,0},{3,2},{5,4},{7,6},{8,9},{10,11},{12,... | collective-permute-start | bytes 491528 | tf_op jit(solution)/shard_map/ppermute | solution.py:317
  8.0 7.4 %collective-permute-start.2 = (bf16[2,1,32,1280]{3,2,1,0:T(8,128)(2,1)S(1)}, bf16[2,1,32,1280]{3,2,1,0:T(8,128)(2,1)S(1)}, u32[]{:S(2)}, u32[]{:S(2)}) collective-permute-start(bf16[2,1,32,1280]{3,2,1,0:T(8,128)(2,1)S(1)} %get-tuple-element.35), channel_id=1, source_target_pairs={{8,16},{24,32},{40,48},{56,64},{72,80},{88,96},{104,112},{120,128}... | collective-permute-start | bytes 491528 | tf_op jit(solution)/shard_map/ppermute | solution.py:318
  12.4 0.7 copy-start.2
  12.4 3.0 %collective-permute-start.3 = (bf16[2,1,32,1280]{3,2,1,0:T(8,128)(2,1)S(1)}, bf16[2,1,32,1280]{3,2,1,0:T(8,128)(2,1)S(1)}, u32[]{:S(2)}, u32[]{:S(2)}) collective-permute-start(bf16[2,1,32,1280]{3,2,1,0:T(8,128)(2,1)S(1)} %get-tuple-element.36), channel_id=1, source_target_pairs={{0,8},{16,24},{32,40},{48,56},{64,72},{80,88},{96,104},{112,120},{... | collective-permute-start | bytes 491528 | tf_op jit(solution)/shard_map/ppermute | solution.py:319
  21.0 15.3 %all-to-all-start = ((bf16[32,16,128]{2,1,0:T(8,128)(2,1)}), bf16[32,16,128]{2,1,0:T(8,128)(2,1)S(1)}, u32[]{:S(2)}, u32[]{:S(2)}) async-start(bf16[32,16,128]{2,1,0:T(8,128)(2,1)} %bitcast.1), calls=%async_computation | async-start | bytes 262144 | tf_op jit(solution)/shard_map/all_to_all | solution.py:335
  29.9 0.8 %copy-start.5 = (f32[2,2,32,1280]{3,2,1,0:T(8,128)}, f32[2,2,32,1280]{3,2,1,0:T(8,128)S(1)}, u32[]{:S(2)}) copy-start(f32[2,2,32,1280]{3,2,1,0:T(8,128)S(1)} %get-tuple-element.50.mapped_ref) | copy-start | bytes 1966084
  30.8 0.9 %copy-start.6 = (f32[2,2,32,1280]{3,2,1,0:T(8,128)}, f32[2,2,32,1280]{3,2,1,0:T(8,128)S(1)}, u32[]{:S(2)}) copy-start(f32[2,2,32,1280]{3,2,1,0:T(8,128)S(1)} %get-tuple-element.57.own_ref) | copy-start | bytes 1966084
  37.0 12.9 %all-to-all-start.1 = ((bf16[8,16,128]{2,1,0:T(8,128)(2,1)}), bf16[8,16,128]{2,1,0:T(8,128)(2,1)S(1)}, u32[]{:S(2)}, u32[]{:S(2)}) async-start(bf16[8,16,128]{2,1,0:T(8,128)(2,1)} %plane_sums.1), calls=%async_computation.1 | async-start | bytes 65536 | tf_op jit(solution)/shard_map/all_to_all | solution.py:350
  43.0 17.4 %collective-permute-start.5 = (bf16[1,2,32,1280]{3,2,1,0:T(8,128)(2,1)S(1)}, bf16[1,2,32,1280]{3,2,1,0:T(8,128)(2,1)S(1)}, u32[]{:S(2)}, u32[]{:S(2)}) collective-permute-start(bf16[1,2,32,1280]{3,2,1,0:T(8,128)(2,1)S(1)} %get-tuple-element.48), channel_id=1, source_target_pairs={{1,2},{5,6},{2,1},{6,5},{9,10},{13,14},{10,9},{14,13},{17,18},{21,... | collective-permute-start | bytes 491528 | tf_op jit(solution)/shard_map/ppermute | solution.py:348
  43.7 16.7 %collective-permute-start.6 = (bf16[1,2,32,1280]{3,2,1,0:T(8,128)(2,1)S(1)}, bf16[1,2,32,1280]{3,2,1,0:T(8,128)(2,1)S(1)}, u32[]{:S(2)}, u32[]{:S(2)}) collective-permute-start(bf16[1,2,32,1280]{3,2,1,0:T(8,128)(2,1)S(1)} %get-tuple-element.49), channel_id=1, source_target_pairs={{0,1},{2,3},{4,5},{6,7},{1,0},{3,2},{5,4},{7,6},{8,9},{10,11},{12,... | collective-permute-start | bytes 491528 | tf_op jit(solution)/shard_map/ppermute | solution.py:347
  45.5 14.9 %collective-permute-start.4 = (bf16[1,2,32,1280]{3,2,1,0:T(8,128)(2,1)S(1)}, bf16[1,2,32,1280]{3,2,1,0:T(8,128)(2,1)S(1)}, u32[]{:S(2)}, u32[]{:S(2)}) collective-permute-start(bf16[1,2,32,1280]{3,2,1,0:T(8,128)(2,1)S(1)} %get-tuple-element.48), channel_id=1, source_target_pairs={{3,4},{7,0},{4,3},{0,7},{11,12},{15,8},{12,11},{8,15},{19,20},{23,... | collective-permute-start | bytes 491528 | tf_op jit(solution)/shard_map/ppermute | solution.py:351
  50.8 13.4 %all-to-all-start.2 = ((bf16[32,16,128]{2,1,0:T(8,128)(2,1)}), bf16[32,16,128]{2,1,0:T(8,128)(2,1)S(1)}, u32[]{:S(2)}, u32[]{:S(2)}) async-start(bf16[32,16,128]{2,1,0:T(8,128)(2,1)} %all_sums.1), calls=%async_computation.2 | async-start | bytes 262144 | tf_op jit(solution)/shard_map/all_to_all | solution.py:353
  56.5 8.6 %collective-permute-start.7 = (bf16[2,1,32,1280]{3,2,1,0:T(8,128)(2,1)S(1)}, bf16[2,1,32,1280]{3,2,1,0:T(8,128)(2,1)S(1)}, u32[]{:S(2)}, u32[]{:S(2)}) collective-permute-start(bf16[2,1,32,1280]{3,2,1,0:T(8,128)(2,1)S(1)} %get-tuple-element.52), channel_id=1, source_target_pairs={{8,16},{24,32},{40,48},{56,64},{72,80},{88,96},{104,112},{120,128}... | collective-permute-start | bytes 491528 | tf_op jit(solution)/shard_map/ppermute | solution.py:357
  60.3 4.8 %collective-permute-start.8 = (bf16[2,1,32,1280]{3,2,1,0:T(8,128)(2,1)S(1)}, bf16[2,1,32,1280]{3,2,1,0:T(8,128)(2,1)S(1)}, u32[]{:S(2)}, u32[]{:S(2)}) collective-permute-start(bf16[2,1,32,1280]{3,2,1,0:T(8,128)(2,1)S(1)} %get-tuple-element.53), channel_id=1, source_target_pairs={{0,8},{16,24},{32,40},{48,56},{64,72},{80,88},{96,104},{112,120},{... | collective-permute-start | bytes 491528 | tf_op jit(solution)/shard_map/ppermute | solution.py:358
  64.2 1.1 %copy-start.7 = (f32[2,2,32,1280]{3,2,1,0:T(8,128)S(1)}, f32[2,2,32,1280]{3,2,1,0:T(8,128)}, u32[]{:S(2)}) copy-start(f32[2,2,32,1280]{3,2,1,0:T(8,128)} %copy-done.6) | copy-start | bytes 1966084

commit v5 on v4

--- a/solution.py
+++ b/solution.py
@@ -18,12 +18,13 @@
 VMEM_LIMIT = 24 * 1024 * 1024
 EDGES_KIB = 54200
 LATE_KIB = 54600
-LAST_KIB = 24000
+LAST_KIB = 54600
 OWN_KIB = 24000
 GZ = ("yl", "z", "c")
 TA = ("yh", "x")
 FLAT = ("yl", "yh", "x", "c")
 LONG = pl.CostEstimate(flops=2 * 10**9, bytes_accessed=4 * 10**6, transcendentals=0)
+SHORT = pl.CostEstimate(flops=10**6, bytes_accessed=10**5, transcendentals=0)
 PARAMS = pltpu.CompilerParams(vmem_limit_bytes=VMEM_LIMIT)
 IN_VMEM = pl.BlockSpec(memory_space=pltpu.VMEM)
 ANYWHERE = pl.BlockSpec(memory_space=pl.ANY)
@@ -344,20 +345,20 @@
         cost_estimate=LONG,
         name="own",
     )(active, hgrad, spatial_weight, temporal_weight)
+    gin_far = lax.ppermute(gin_far, GZ, to_far)
+    gin_near = lax.ppermute(gin_near, GZ, to_near)
+    parts, map_odd, map_even = lax.optimization_barrier((parts, map_odd, map_even))
+    parts = lax.all_to_all(total_of(parts, 8, "plane_sums"), "z", 0, 0)
     map_even = lax.ppermute(map_even, TA, to_even)
     map_inner = lax.ppermute(map_odd, TA, to_inner)
-    parts, map_odd = lax.optimization_barrier((parts, map_odd))
-    parts = lax.all_to_all(total_of(parts, 8, "plane_sums"), "z", 0, 0)
     map_seam = lax.ppermute(map_odd, TA, to_seam)
     parts, gin_far, gin_near = lax.optimization_barrier((parts, gin_far, gin_near))
     got = lax.all_to_all(total_of(parts, 32, "all_sums"), FLAT, 0, 0)
     rebuilt = finished(
         rebuilt_kernel, "rebuilt", (map_seam, map_inner, map_even, mapped_own, outputs_fwd), LATE_KIB, LONG
     )
-    gin_far = lax.ppermute(gin_far, GZ, to_far)
-    gin_near = lax.ppermute(gin_near, GZ, to_near)
-
-    got, rebuilt = lax.optimization_barrier((got, rebuilt))
+    grad_in = finished(gin_kernel, "grad_in", (gin_far, gin_near, gin_own, cotangent), LAST_KIB, SHORT)
+    got, rebuilt, grad_in = lax.optimization_barrier((got, rebuilt, grad_in))
 
     factor = 1.0 / math.sqrt(2 * ta * 2 * gz * PIX)
     grad_spatial, grad_bias, grad_temporal = pl.pallas_call(
@@ -369,8 +370,6 @@
         cost_estimate=LONG,
         name="grads",
     )(got.reshape(512, 128))
-    gin_own, grad_spatial = lax.optimization_barrier((gin_own, grad_spatial))
-    grad_in = finished(gin_kernel, "grad_in", (gin_far, gin_near, gin_own, cotangent), LAST_KIB, LONG)
     return rebuilt, grad_in, grad_spatial, grad_bias.reshape(HID), grad_temporal
 
 

time: 66.7 us -> 66.6 us (level)
  starting transfers between devices: 40.5 us -> 38.6 us
  Pallas kernels: 13.8 us -> 15.1 us
  waiting for transfers between devices: 8.49 us -> 9.34 us
    all_to_all x1, waiting for transfers between devices: 4.62 us -> 2.58 us  [shards(): parts = lax.all_to_all(pay.reshape(32, 16, 128), FLAT, 0, 0)]
    ppermute x1, starting transfers between devices: 3.77 us -> 1.91 us  [shards(): gin_far = lax.ppermute(gin_far, GZ, to_far)]
    all_to_all x1, waiting for transfers between devices: 1.65 us -> 3.43 us  [shards(): got = lax.all_to_all(total_of(parts, 32, 'all_sums'), FLAT, 0, 0)]
    ppermute x1, starting transfers between devices: 1.76 us -> 0.09 us  [shards(): map_even = lax.ppermute(map_even, TA, to_even)]
    pallas_call x2, Pallas kernels: 2.99 us -> 4.26 us  [finished(): pl.pallas_call(kernel, in_specs=[IN_VMEM] * len(operands), out_specs=IN_V...]
    all_to_all x1, starting transfers between devices: 5.69 us -> 6.86 us  [shards(): got = lax.all_to_all(total_of(parts, 32, 'all_sums'), FLAT, 0, 0)]
    all_to_all x1, waiting for transfers between devices: 0.01 us -> 1.11 us  [shards(): parts = lax.all_to_all(total_of(parts, 8, 'plane_sums'), 'z', 0, 0)]
    unnamed x16 -> x14, local copies, waits for them, and re-layouts: 2.5 us -> 2.27 us
  transfers between devices with their start and end apart: 12 -> 12, of which waited for: 3 -> 4; matrix products, arithmetic and copies ran while one was open for 0% -> 0% of each run, Pallas kernels for 8% -> 11%
where the time goes in v5:
time: 66.6 us; the launch traced here: 66.2 us
  starting transfers between devices  38.6 us (58%)
  Pallas kernels  15.1 us (23%)
  waiting for transfers between devices  9.34 us (14%)
  local copies, waits for them, and re-layouts  2.27 us (3%)
  between operations  0.83 us (1%)
    all_to_all x1, starting transfers between devices, shards(): parts = lax.all_to_all(pay.reshape(32, 16, 128), FLAT, 0, 0)  7.56 us
    all_to_all x1, starting transfers between devices, shards(): got = lax.all_to_all(total_of(parts, 32, 'all_sums'), FLAT, 0, 0)  6.86 us
    ppermute x1, starting transfers between devices, shards(): g2_odd = lax.ppermute(g2_odd, TA, to_odd)  6.03 us
    all_to_all x1, starting transfers between devices, shards(): parts = lax.all_to_all(total_of(parts, 8, 'plane_sums'), 'z', 0, 0)  5.99 us
    pallas_call x1, Pallas kernels, shards(): pl.pallas_call(hidden_kernel, in_specs=[IN_VMEM] * 9, out_specs=[IN_VMEM]...  5.56 us
    ppermute x1, starting transfers between devices, shards(): map_seam = lax.ppermute(map_odd, TA, to_seam)  4.97 us
    ppermute x1, starting transfers between devices, shards(): y1_far = lax.ppermute(y1_far, GZ, to_far)  4.37 us
    pallas_call x2, Pallas kernels, finished(): pl.pallas_call(kernel, in_specs=[IN_VMEM] * len(operands), out_specs=IN_V...  4.26 us
  transfers between devices with their start and end apart: 12, of which 4 were waited for; matrix products, arithmetic and copies ran while one was open for 0% of the time, Pallas kernels for 11%

profile of v5, /device:TPU:1, one launch (start us, length us, event | category | flops | bytes accessed | tf_op | source)
XLA Modules:
  0.0 66.2 jit_solution(7722679413807639887)
XLA Ops:
  0.6 0.0 copy-start
  0.6 0.0 copy-start.5
  0.7 0.0 copy-start.2
  0.7 0.0 copy-start.3
  0.7 1.3 %edges.1 = (bf16[1,2,32,1280]{3,2,1,0:T(8,128)(2,1)S(1)}, bf16[1,2,32,1280]{3,2,1,0:T(8,128)(2,1)S(1)}, bf16[2,1,32,1280]{3,2,1,0:T(8,128)(2,1)S(1)}, bf16[2,1,32,1280]{3,2,1,0:T(8,128)(2,1)S(1)}) custom-call(bf16[2,2,64,1280]{3,2,1,0:T(8,128)(2,1)} %fwd_ref.5, bf16[2,2,64,1280]{3,2,1,0:T(8,128)(2,1)} %cot_ref.5), custom_call_target="tpu_custom_call" | custom-call | flops 4000000000 | bytes 1000000 | tf_op jit(solution)/shard_map/edges/pallas_call | solution.py:299
  2.0 6.0 %collective-permute-start = (bf16[1,2,32,1280]{3,2,1,0:T(8,128)(2,1)S(1)}, bf16[1,2,32,1280]{3,2,1,0:T(8,128)(2,1)S(1)}, u32[]{:S(2)}, u32[]{:S(2)}) collective-permute-start(bf16[1,2,32,1280]{3,2,1,0:T(8,128)(2,1)S(1)} %get-tuple-element.33), channel_id=1, source_target_pairs={{1,2},{3,4},{5,6},{7,0},{2,1},{4,3},{6,5},{0,7},{9,10},{11,12},{13... | collective-permute-start | bytes 491528 | tf_op jit(solution)/shard_map/ppermute | solution.py:317
  8.0 0.0 collective-permute-start.1
  8.0 4.4 %collective-permute-start.2 = (bf16[2,1,32,1280]{3,2,1,0:T(8,128)(2,1)S(1)}, bf16[2,1,32,1280]{3,2,1,0:T(8,128)(2,1)S(1)}, u32[]{:S(2)}, u32[]{:S(2)}) collective-permute-start(bf16[2,1,32,1280]{3,2,1,0:T(8,128)(2,1)S(1)} %get-tuple-element.35), channel_id=1, source_target_pairs={{8,16},{24,32},{40,48},{56,64},{72,80},{88,96},{104,112},{120,128}... | collective-permute-start | bytes 491528 | tf_op jit(solution)/shard_map/ppermute | solution.py:319
  12.4 0.0 copy-start.4
  12.4 0.1 collective-permute-start.3
  12.5 0.0 copy-done.2
  12.5 0.0 copy-done.3
  12.5 0.5 copy-done.4
  13.1 0.1 weights.1
  13.2 0.0 collective-permute-done.odd_ref
  13.2 0.0 collective-permute-done.1.even_ref
  13.2 2.2 %collective-permute-done.2.far_ref = bf16[2,1,32,1280]{3,2,1,0:T(8,128)(2,1)S(1)} collective-permute-done((bf16[2,1,32,1280]{3,2,1,0:T(8,128)(2,1)S(1)}, bf16[2,1,32,1280]{3,2,1,0:T(8,128)(2,1)S(1)}, u32[]{:S(2)}, u32[]{:S(2)}) %collective-permute-start.2) | collective-permute-done | bytes 163872 | tf_op jit(solution)/shard_map/ppermute | solution.py:319
  15.4 0.0 collective-permute-done.3.near_ref
  15.4 0.0 copy-done
  15.4 0.0 copy-done.5
  15.4 5.6 %hidden.1 = (bf16[2,2,64,1280]{3,2,1,0:T(8,128)(2,1)S(1)}, bf16[2,2,64,1280]{3,2,1,0:T(8,128)(2,1)S(1)}, bf16[512,128]{1,0:T(8,128)(2,1)}) custom-call(bf16[1,2,32,1280]{3,2,1,0:T(8,128)(2,1)S(1)} %collective-permute-done.odd_ref, bf16[1,2,32,1280]{3,2,1,0:T(8,128)(2,1)S(1)} %collective-permute-done.1.even_ref, ...), custom_call_target="tpu_custom_call" | custom-call | flops 1000000000 | bytes 4000000 | tf_op jit(solution)/shard_map/hidden/pallas_call | solution.py:322
  21.0 7.6 %all-to-all-start = ((bf16[32,16,128]{2,1,0:T(8,128)(2,1)}), bf16[32,16,128]{2,1,0:T(8,128)(2,1)S(1)}, u32[]{:S(2)}, u32[]{:S(2)}) async-start(bf16[32,16,128]{2,1,0:T(8,128)(2,1)} %bitcast.1), calls=%async_computation | async-start | bytes 262144 | tf_op jit(solution)/shard_map/all_to_all | solution.py:336
  28.5 1.4 %own.1 = (f32[2,2,32,1280]{3,2,1,0:T(8,128)S(1)}, f32[2,2,32,1280]{3,2,1,0:T(8,128)S(1)}, bf16[1,2,32,1280]{3,2,1,0:T(8,128)(2,1)S(1)}, bf16[1,2,32,1280]{3,2,1,...) custom-call(bf16[2,2,64,1280]{3,2,1,0:T(8,128)(2,1)S(1)} %get-tuple-element.41.act_ref, ...), custom_call_target="tpu_custom_call" | custom-call | flops 2000000000 | bytes 4000000 | tf_op jit(solution)/shard_map/own/pallas_call | solution.py:337
  29.9 0.0 copy-start.1
  29.9 0.9 %copy-done.1 = f32[2,2,32,1280]{3,2,1,0:T(8,128)} copy-done((f32[2,2,32,1280]{3,2,1,0:T(8,128)}, f32[2,2,32,1280]{3,2,1,0:T(8,128)S(1)}, u32[]{:S(2)}) %copy-start.1) | copy-done | bytes 655384
  30.8 0.0 copy-start.6
  30.8 0.9 %copy-done.6 = f32[2,2,32,1280]{3,2,1,0:T(8,128)} copy-done((f32[2,2,32,1280]{3,2,1,0:T(8,128)}, f32[2,2,32,1280]{3,2,1,0:T(8,128)S(1)}, u32[]{:S(2)}) %copy-start.6) | copy-done | bytes 655384
  31.6 1.9 %collective-permute-start.4 = (bf16[2,1,32,1280]{3,2,1,0:T(8,128)(2,1)S(1)}, bf16[2,1,32,1280]{3,2,1,0:T(8,128)(2,1)S(1)}, u32[]{:S(2)}, u32[]{:S(2)}) collective-permute-start(bf16[2,1,32,1280]{3,2,1,0:T(8,128)(2,1)S(1)} %get-tuple-element.46), channel_id=1, source_target_pairs={{8,16},{24,32},{40,48},{56,64},{72,80},{88,96},{104,112},{120,128}... | collective-permute-start | bytes 491528 | tf_op jit(solution)/shard_map/ppermute | solution.py:348
  33.5 0.1 collective-permute-start.5
  33.6 2.6 %all-to-all-done.refs_0_ = bf16[32,16,128]{2,1,0:T(8,128)(2,1)S(1)} async-done(((bf16[32,16,128]{2,1,0:T(8,128)(2,1)}), bf16[32,16,128]{2,1,0:T(8,128)(2,1)S(1)}, u32[]{:S(2)}, u32[]{:S(2)}) %all-to-all-start) | async-done | bytes 131104 | tf_op jit(solution)/shard_map/all_to_all | solution.py:336
  36.2 0.8 %plane_sums.1 = bf16[8,16,128]{2,1,0:T(8,128)(2,1)} custom-call(bf16[32,16,128]{2,1,0:T(8,128)(2,1)S(1)} %all-to-all-done.refs_0_), custom_call_target="tpu_custom_call" | custom-call | flops 2000000000 | bytes 4000000 | tf_op jit(solution)/shard_map/plane_sums/pallas_call | solution.py:266
  37.0 6.0 %all-to-all-start.1 = ((bf16[8,16,128]{2,1,0:T(8,128)(2,1)}), bf16[8,16,128]{2,1,0:T(8,128)(2,1)S(1)}, u32[]{:S(2)}, u32[]{:S(2)}) async-start(bf16[8,16,128]{2,1,0:T(8,128)(2,1)} %plane_sums.1), calls=%async_computation.1 | async-start | bytes 65536 | tf_op jit(solution)/shard_map/all_to_all | solution.py:351
  43.0 0.7 collective-permute-start.7
  43.7 5.0 %collective-permute-start.6 = (bf16[1,2,32,1280]{3,2,1,0:T(8,128)(2,1)S(1)}, bf16[1,2,32,1280]{3,2,1,0:T(8,128)(2,1)S(1)}, u32[]{:S(2)}, u32[]{:S(2)}) collective-permute-start(bf16[1,2,32,1280]{3,2,1,0:T(8,128)(2,1)S(1)} %get-tuple-element.49), channel_id=1, source_target_pairs={{3,4},{7,0},{4,3},{0,7},{11,12},{15,8},{12,11},{8,15},{19,20},{23,... | collective-permute-start | bytes 491528 | tf_op jit(solution)/shard_map/ppermute | solution.py:354
  48.7 0.1 collective-permute-start.8
  48.8 0.0 collective-permute-done.4.far_ref
  48.8 0.0 collective-permute-done.5.near_ref
  48.8 1.1 %all-to-all-done.1.refs_0_ = bf16[8,16,128]{2,1,0:T(8,128)(2,1)S(1)} async-done(((bf16[8,16,128]{2,1,0:T(8,128)(2,1)}), bf16[8,16,128]{2,1,0:T(8,128)(2,1)S(1)}, u32[]{:S(2)}, u32[]{:S(2)}) %all-to-all-start.1) | async-done | bytes 32800 | tf_op jit(solution)/shard_map/all_to_all | solution.py:351
  49.9 0.8 %all_sums.1 = bf16[32,16,128]{2,1,0:T(8,128)(2,1)} custom-call(bf16[8,16,128]{2,1,0:T(8,128)(2,1)S(1)} %all-to-all-done.1.refs_0_), custom_call_target="tpu_custom_call" | custom-call | flops 2000000000 | bytes 4000000 | tf_op jit(solution)/shard_map/all_sums/pallas_call | solution.py:266
  50.7 6.9 %all-to-all-start.2 = ((bf16[32,16,128]{2,1,0:T(8,128)(2,1)}), bf16[32,16,128]{2,1,0:T(8,128)(2,1)S(1)}, u32[]{:S(2)}, u32[]{:S(2)}) async-start(bf16[32,16,128]{2,1,0:T(8,128)(2,1)} %all_sums.1), calls=%async_computation.2 | async-start | bytes 262144 | tf_op jit(solution)/shard_map/all_to_all | solution.py:356
  57.6 2.1 %grad_in.1 = bf16[2,2,32,1280]{3,2,1,0:T(8,128)(2,1)} custom-call(bf16[2,1,32,1280]{3,2,1,0:T(8,128)(2,1)S(1)} %collective-permute-done.4.far_ref, bf16[2,1,32,1280]{3,2,1,0:T(8,128)(2,1)S(1)} %collective-permute-done.5.near_ref, f32[2,2,32,1280]{3,2,1,0:T(8,128)} %copy-done.1, bf16[2,2,64,1280]{3,2,1,0:T(8,128)(2,1)} %cot_ref.5), custom_call_target="tpu_custom_call" | custom-call | flops 1000000 | bytes 100000 | tf_op jit(solution)/shard_map/grad_in/pallas_call | solution.py:278
  59.7 0.0 collective-permute-done.8.even_ref
  59.7 0.0 collective-permute-done.7.inner_ref
  59.7 0.0 collective-permute-done.6.seam_ref
  59.7 2.1 %rebuilt.1 = bf16[2,2,32,1280]{3,2,1,0:T(8,128)(2,1)} custom-call(bf16[1,2,32,1280]{3,2,1,0:T(8,128)(2,1)S(1)} %collective-permute-done.6.seam_ref, bf16[1,2,32,1280]{3,2,1,0:T(8,128)(2,1)S(1)} %collective-permute-done.7.inner_ref, bf16[1,2,32,1280]{3,2,1,0:T(8,128)(2,1)S(1)} %collective-permute-done.8.even_ref, f32[2,2,32,1280]{3,2,1,0:T(8,128)} %copy-done.6, ...), custom_call_target="tpu_custom_call" | custom-call | flops 2000000000 | bytes 4000000 | tf_op jit(solution)/shard_map/rebuilt/pallas_call | solution.py:278
  61.9 3.4 %all-to-all-done.2 = bf16[32,16,128]{2,1,0:T(8,128)(2,1)S(1)} async-done(((bf16[32,16,128]{2,1,0:T(8,128)(2,1)}), bf16[32,16,128]{2,1,0:T(8,128)(2,1)S(1)}, u32[]{:S(2)}, u32[]{:S(2)}) %all-to-all-start.2) | async-done | bytes 131104 | tf_op jit(solution)/shard_map/all_to_all | solution.py:356
  65.3 0.9 %grads.1 = (f32[3,64,288]{2,1,0:T(8,128)}, f32[1,64]{1,0:T(1,128)}, f32[3,32,64]{2,1,0:T(8,128)}) custom-call(bf16[512,128]{1,0:T(8,128)(2,1)S(1)} %bitcast.4), custom_call_target="tpu_custom_call" | custom-call | flops 2000000000 | bytes 4000000 | tf_op jit(solution)/shard_map/grads/pallas_call | solution.py:364
Async XLA Ops:
  0.6 14.8 %copy-start = (bf16[2,2,64,1280]{3,2,1,0:T(8,128)(2,1)S(1)}, bf16[2,2,64,1280]{3,2,1,0:T(8,128)(2,1)}, u32[]{:S(2)}) copy-start(bf16[2,2,64,1280]{3,2,1,0:T(8,128)(2,1)} %cot_ref.5) | copy-start | bytes 1966084
  0.6 14.7 %copy-start.5 = (bf16[2,2,64,1280]{3,2,1,0:T(8,128)(2,1)S(1)}, bf16[2,2,64,1280]{3,2,1,0:T(8,128)(2,1)}, u32[]{:S(2)}) copy-start(bf16[2,2,64,1280]{3,2,1,0:T(8,128)(2,1)} %fwd_ref.5) | copy-start | bytes 1966084
  0.7 11.9 %copy-start.2 = (bf16[3,64,288]{2,1,0:T(8,128)(2,1)S(1)}, bf16[3,64,288]{2,1,0:T(8,128)(2,1)}, u32[]{:S(2)}) copy-start(bf16[3,64,288]{2,1,0:T(8,128)(2,1)} %sw_ref.3) | copy-start | bytes 331780
  0.7 11.9 %copy-start.3 = (bf16[3,32,64]{2,1,0:T(8,128)(2,1)S(1)}, bf16[3,32,64]{2,1,0:T(8,128)(2,1)}, u32[]{:S(2)}) copy-start(bf16[3,32,64]{2,1,0:T(8,128)(2,1)} %tw_ref.3) | copy-start | bytes 36868
  2.0 11.2 %collective-permute-start = (bf16[1,2,32,1280]{3,2,1,0:T(8,128)(2,1)S(1)}, bf16[1,2,32,1280]{3,2,1,0:T(8,128)(2,1)S(1)}, u32[]{:S(2)}, u32[]{:S(2)}) collective-permute-start(bf16[1,2,32,1280]{3,2,1,0:T(8,128)(2,1)S(1)} %get-tuple-element.33), channel_id=1, source_target_pairs={{1,2},{3,4},{5,6},{7,0},{2,1},{4,3},{6,5},{0,7},{9,10},{11,12},{13... | collective-permute-start | bytes 491528 | tf_op jit(solution)/shard_map/ppermute | solution.py:317
  8.0 5.2 %collective-permute-start.1 = (bf16[1,2,32,1280]{3,2,1,0:T(8,128)(2,1)S(1)}, bf16[1,2,32,1280]{3,2,1,0:T(8,128)(2,1)S(1)}, u32[]{:S(2)}, u32[]{:S(2)}) collective-permute-start(bf16[1,2,32,1280]{3,2,1,0:T(8,128)(2,1)S(1)} %get-tuple-element.34), channel_id=1, source_target_pairs={{0,1},{2,3},{4,5},{6,7},{1,0},{3,2},{5,4},{7,6},{8,9},{10,11},{12,... | collective-permute-start | bytes 491528 | tf_op jit(solution)/shard_map/ppermute | solution.py:318
  8.0 7.4 %collective-permute-start.2 = (bf16[2,1,32,1280]{3,2,1,0:T(8,128)(2,1)S(1)}, bf16[2,1,32,1280]{3,2,1,0:T(8,128)(2,1)S(1)}, u32[]{:S(2)}, u32[]{:S(2)}) collective-permute-start(bf16[2,1,32,1280]{3,2,1,0:T(8,128)(2,1)S(1)} %get-tuple-element.35), channel_id=1, source_target_pairs={{8,16},{24,32},{40,48},{56,64},{72,80},{88,96},{104,112},{120,128}... | collective-permute-start | bytes 491528 | tf_op jit(solution)/shard_map/ppermute | solution.py:319
  12.4 0.7 copy-start.4
  12.4 3.0 %collective-permute-start.3 = (bf16[2,1,32,1280]{3,2,1,0:T(8,128)(2,1)S(1)}, bf16[2,1,32,1280]{3,2,1,0:T(8,128)(2,1)S(1)}, u32[]{:S(2)}, u32[]{:S(2)}) collective-permute-start(bf16[2,1,32,1280]{3,2,1,0:T(8,128)(2,1)S(1)} %get-tuple-element.36), channel_id=1, source_target_pairs={{0,8},{16,24},{32,40},{48,56},{64,72},{80,88},{96,104},{112,120},{... | collective-permute-start | bytes 491528 | tf_op jit(solution)/shard_map/ppermute | solution.py:320
  21.0 15.3 %all-to-all-start = ((bf16[32,16,128]{2,1,0:T(8,128)(2,1)}), bf16[32,16,128]{2,1,0:T(8,128)(2,1)S(1)}, u32[]{:S(2)}, u32[]{:S(2)}) async-start(bf16[32,16,128]{2,1,0:T(8,128)(2,1)} %bitcast.1), calls=%async_computation | async-start | bytes 262144 | tf_op jit(solution)/shard_map/all_to_all | solution.py:336
  29.9 0.9 %copy-start.1 = (f32[2,2,32,1280]{3,2,1,0:T(8,128)}, f32[2,2,32,1280]{3,2,1,0:T(8,128)S(1)}, u32[]{:S(2)}) copy-start(f32[2,2,32,1280]{3,2,1,0:T(8,128)S(1)} %get-tuple-element.54.own_ref) | copy-start | bytes 1966084
  30.8 0.9 %copy-start.6 = (f32[2,2,32,1280]{3,2,1,0:T(8,128)}, f32[2,2,32,1280]{3,2,1,0:T(8,128)S(1)}, u32[]{:S(2)}) copy-start(f32[2,2,32,1280]{3,2,1,0:T(8,128)S(1)} %get-tuple-element.51.mapped_ref) | copy-start | bytes 1966084
  31.6 17.1 %collective-permute-start.4 = (bf16[2,1,32,1280]{3,2,1,0:T(8,128)(2,1)S(1)}, bf16[2,1,32,1280]{3,2,1,0:T(8,128)(2,1)S(1)}, u32[]{:S(2)}, u32[]{:S(2)}) collective-permute-start(bf16[2,1,32,1280]{3,2,1,0:T(8,128)(2,1)S(1)} %get-tuple-element.46), channel_id=1, source_target_pairs={{8,16},{24,32},{40,48},{56,64},{72,80},{88,96},{104,112},{120,128}... | collective-permute-start | bytes 491528 | tf_op jit(solution)/shard_map/ppermute | solution.py:348
  33.5 15.2 %collective-permute-start.5 = (bf16[2,1,32,1280]{3,2,1,0:T(8,128)(2,1)S(1)}, bf16[2,1,32,1280]{3,2,1,0:T(8,128)(2,1)S(1)}, u32[]{:S(2)}, u32[]{:S(2)}) collective-permute-start(bf16[2,1,32,1280]{3,2,1,0:T(8,128)(2,1)S(1)} %get-tuple-element.47), channel_id=1, source_target_pairs={{0,8},{16,24},{32,40},{48,56},{64,72},{80,88},{96,104},{112,120},{... | collective-permute-start | bytes 491528 | tf_op jit(solution)/shard_map/ppermute | solution.py:349
  37.0 12.9 %all-to-all-start.1 = ((bf16[8,16,128]{2,1,0:T(8,128)(2,1)}), bf16[8,16,128]{2,1,0:T(8,128)(2,1)S(1)}, u32[]{:S(2)}, u32[]{:S(2)}) async-start(bf16[8,16,128]{2,1,0:T(8,128)(2,1)} %plane_sums.1), calls=%async_computation.1 | async-start | bytes 65536 | tf_op jit(solution)/shard_map/all_to_all | solution.py:351
  43.0 16.7 %collective-permute-start.7 = (bf16[1,2,32,1280]{3,2,1,0:T(8,128)(2,1)S(1)}, bf16[1,2,32,1280]{3,2,1,0:T(8,128)(2,1)S(1)}, u32[]{:S(2)}, u32[]{:S(2)}) collective-permute-start(bf16[1,2,32,1280]{3,2,1,0:T(8,128)(2,1)S(1)} %get-tuple-element.49), channel_id=1, source_target_pairs={{1,2},{5,6},{2,1},{6,5},{9,10},{13,14},{10,9},{14,13},{17,18},{21,... | collective-permute-start | bytes 491528 | tf_op jit(solution)/shard_map/ppermute | solution.py:353
  43.7 16.0 %collective-permute-start.6 = (bf16[1,2,32,1280]{3,2,1,0:T(8,128)(2,1)S(1)}, bf16[1,2,32,1280]{3,2,1,0:T(8,128)(2,1)S(1)}, u32[]{:S(2)}, u32[]{:S(2)}) collective-permute-start(bf16[1,2,32,1280]{3,2,1,0:T(8,128)(2,1)S(1)} %get-tuple-element.49), channel_id=1, source_target_pairs={{3,4},{7,0},{4,3},{0,7},{11,12},{15,8},{12,11},{8,15},{19,20},{23,... | collective-permute-start | bytes 491528 | tf_op jit(solution)/shard_map/ppermute | solution.py:354
  48.7 11.1 %collective-permute-start.8 = (bf16[1,2,32,1280]{3,2,1,0:T(8,128)(2,1)S(1)}, bf16[1,2,32,1280]{3,2,1,0:T(8,128)(2,1)S(1)}, u32[]{:S(2)}, u32[]{:S(2)}) collective-permute-start(bf16[1,2,32,1280]{3,2,1,0:T(8,128)(2,1)S(1)} %get-tuple-element.50), channel_id=1, source_target_pairs={{0,1},{2,3},{4,5},{6,7},{1,0},{3,2},{5,4},{7,6},{8,9},{10,11},{12,... | collective-permute-start | bytes 491528 | tf_op jit(solution)/shard_map/ppermute | solution.py:352
  50.7 14.6 %all-to-all-start.2 = ((bf16[32,16,128]{2,1,0:T(8,128)(2,1)}), bf16[32,16,128]{2,1,0:T(8,128)(2,1)S(1)}, u32[]{:S(2)}, u32[]{:S(2)}) async-start(bf16[32,16,128]{2,1,0:T(8,128)(2,1)} %all_sums.1), calls=%async_computation.2 | async-start | bytes 262144 | tf_op jit(solution)/shard_map/all_to_all | solution.py:356

commit v6 on v5

--- a/solution.py
+++ b/solution.py
@@ -219,14 +219,11 @@
         near_ref[f, 0] = jnp.where(core == 0, above, below).astype(BF16)
 
 
-def rebuilt_kernel(seam_ref, inner_ref, even_ref, mapped_ref, fwd_ref, rebuilt_ref):
+def rebuilt_kernel(odd_ref, even_ref, mapped_ref, fwd_ref, rebuilt_ref):
     odd = parities()[1]
-    place = lax.axis_index("x")
-    seam = jnp.logical_or(place == 0, place == lax.axis_size("x") - 1)
     for z in range(2):
-        from_odd = jnp.where(seam, seam_ref[0, z], inner_ref[0, z])
         for f in range(2):
-            beside = jnp.where(odd == f, from_odd, even_ref[0, z])
+            beside = jnp.where(odd == f, odd_ref[0, z], even_ref[0, z])
             mapped = mapped_ref[f, z] + beside.astype(F32)
             rebuilt_ref[f, z] = (fwd_ref[f, z, CH : 2 * CH].astype(F32) - mapped).astype(BF16)
 
@@ -292,9 +289,6 @@
     to_near = swaps([(i, i + 1) for i in range(0, gz, 2)])
     to_even = swaps([(i, i + 1) for i in range(0, ta, 2)])
     to_odd = swaps([(i, (i + 1) % ta) for i in range(1, ta, 2)])
-    row = lax.axis_size("x")
-    to_inner = swaps([(i, i + 1) for i in range(1, ta, 2) if (i + 1) % row])
-    to_seam = swaps([(i, (i + 1) % ta) for i in range(1, ta, 2) if (i + 1) % row == 0])
 
     g2_odd, g2_even, y1_far, y1_near = pl.pallas_call(
         edges_kernel,
@@ -349,13 +343,12 @@
     gin_near = lax.ppermute(gin_near, GZ, to_near)
     parts, map_odd, map_even = lax.optimization_barrier((parts, map_odd, map_even))
     parts = lax.all_to_all(total_of(parts, 8, "plane_sums"), "z", 0, 0)
+    map_odd = lax.ppermute(map_odd, TA, to_odd)
     map_even = lax.ppermute(map_even, TA, to_even)
-    map_inner = lax.ppermute(map_odd, TA, to_inner)
-    map_seam = lax.ppermute(map_odd, TA, to_seam)
     parts, gin_far, gin_near = lax.optimization_barrier((parts, gin_far, gin_near))
     got = lax.all_to_all(total_of(parts, 32, "all_sums"), FLAT, 0, 0)
     rebuilt = finished(
-        rebuilt_kernel, "rebuilt", (map_seam, map_inner, map_even, mapped_own, outputs_fwd), LATE_KIB, LONG
+        rebuilt_kernel, "rebuilt", (map_odd, map_even, mapped_own, outputs_fwd), LATE_KIB, LONG
     )
     grad_in = finished(gin_kernel, "grad_in", (gin_far, gin_near, gin_own, cotangent), LAST_KIB, SHORT)
     got, rebuilt, grad_in = lax.optimization_barrier((got, rebuilt, grad_in))

time: 66.6 us -> 66.6 us (level)
  waiting for transfers between devices: 9.34 us -> 12.1 us
  starting transfers between devices: 38.6 us -> 36 us
    all_to_all x1, waiting for transfers between devices: 1.11 us -> 3.81 us  [shards(): parts = lax.all_to_all(total_of(parts, 8, 'plane_sums'), 'z', 0, 0)]
    ppermute x2 -> x1, starting transfers between devices: 5.63 us -> 3.06 us  [shards(): map_odd = lax.ppermute(map_odd, TA, to_odd)]
  transfers between devices with their start and end apart: 12 -> 11, of which waited for: 4 -> 4; matrix products, arithmetic and copies ran while one was open for 0% -> 0% of each run, Pallas kernels for 11% -> 11%
where the time goes in v6:
time: 66.6 us; the launch traced here: 66.2 us
  starting transfers between devices  36 us (54%)
  Pallas kernels  15.1 us (23%)
  waiting for transfers between devices  12.1 us (18%)
  local copies, waits for them, and re-layouts  2.26 us (3%)
  between operations  0.79 us (1%)
    all_to_all x1, starting transfers between devices, shards(): parts = lax.all_to_all(pay.reshape(32, 16, 128), FLAT, 0, 0)  7.57 us
    all_to_all x1, starting transfers between devices, shards(): got = lax.all_to_all(total_of(parts, 32, 'all_sums'), FLAT, 0, 0)  6.86 us
    ppermute x1, starting transfers between devices, shards(): g2_odd = lax.ppermute(g2_odd, TA, to_odd)  6.03 us
    all_to_all x1, starting transfers between devices, shards(): parts = lax.all_to_all(total_of(parts, 8, 'plane_sums'), 'z', 0, 0)  5.98 us
    pallas_call x1, Pallas kernels, shards(): pl.pallas_call(hidden_kernel, in_specs=[IN_VMEM] * 9, out_specs=[IN_VMEM]...  5.56 us
    ppermute x1, starting transfers between devices, shards(): y1_far = lax.ppermute(y1_far, GZ, to_far)  4.37 us
    pallas_call x2, Pallas kernels, finished(): pl.pallas_call(kernel, in_specs=[IN_VMEM] * len(operands), out_specs=IN_V...  4.25 us
    all_to_all x1, waiting for transfers between devices, shards(): parts = lax.all_to_all(total_of(parts, 8, 'plane_sums'), 'z', 0, 0)  3.81 us
  transfers between devices with their start and end apart: 11, of which 4 were waited for; matrix products, arithmetic and copies ran while one was open for 0% of the time, Pallas kernels for 11%

profile of v6, /device:TPU:1, one launch (start us, length us, event | category | flops | bytes accessed | tf_op | source)
XLA Modules:
  0.0 66.2 jit_solution(571327316205071312)
XLA Ops:
  0.6 0.0 copy-start
  0.6 0.0 copy-start.5
  0.7 0.0 copy-start.2
  0.7 0.0 copy-start.3
  0.7 1.3 %edges.1 = (bf16[1,2,32,1280]{3,2,1,0:T(8,128)(2,1)S(1)}, bf16[1,2,32,1280]{3,2,1,0:T(8,128)(2,1)S(1)}, bf16[2,1,32,1280]{3,2,1,0:T(8,128)(2,1)S(1)}, bf16[2,1,32,1280]{3,2,1,0:T(8,128)(2,1)S(1)}) custom-call(bf16[2,2,64,1280]{3,2,1,0:T(8,128)(2,1)} %fwd_ref.5, bf16[2,2,64,1280]{3,2,1,0:T(8,128)(2,1)} %cot_ref.5), custom_call_target="tpu_custom_call" | custom-call | flops 4000000000 | bytes 1000000 | tf_op jit(solution)/shard_map/edges/pallas_call | solution.py:293
  2.0 6.0 %collective-permute-start = (bf16[1,2,32,1280]{3,2,1,0:T(8,128)(2,1)S(1)}, bf16[1,2,32,1280]{3,2,1,0:T(8,128)(2,1)S(1)}, u32[]{:S(2)}, u32[]{:S(2)}) collective-permute-start(bf16[1,2,32,1280]{3,2,1,0:T(8,128)(2,1)S(1)} %get-tuple-element.33), channel_id=1, source_target_pairs={{1,2},{3,4},{5,6},{7,0},{2,1},{4,3},{6,5},{0,7},{9,10},{11,12},{13... | collective-permute-start | bytes 491528 | tf_op jit(solution)/shard_map/ppermute | solution.py:311
  8.0 0.0 collective-permute-start.1
  8.0 4.4 %collective-permute-start.2 = (bf16[2,1,32,1280]{3,2,1,0:T(8,128)(2,1)S(1)}, bf16[2,1,32,1280]{3,2,1,0:T(8,128)(2,1)S(1)}, u32[]{:S(2)}, u32[]{:S(2)}) collective-permute-start(bf16[2,1,32,1280]{3,2,1,0:T(8,128)(2,1)S(1)} %get-tuple-element.35), channel_id=1, source_target_pairs={{8,16},{24,32},{40,48},{56,64},{72,80},{88,96},{104,112},{120,128}... | collective-permute-start | bytes 491528 | tf_op jit(solution)/shard_map/ppermute | solution.py:313
  12.4 0.0 copy-start.4
  12.4 0.1 collective-permute-start.3
  12.5 0.0 copy-done.2
  12.5 0.0 copy-done.3
  12.5 0.5 copy-done.4
  13.1 0.1 weights.1
  13.2 0.0 collective-permute-done.odd_ref
  13.2 0.0 collective-permute-done.1.even_ref
  13.2 2.2 %collective-permute-done.2.far_ref = bf16[2,1,32,1280]{3,2,1,0:T(8,128)(2,1)S(1)} collective-permute-done((bf16[2,1,32,1280]{3,2,1,0:T(8,128)(2,1)S(1)}, bf16[2,1,32,1280]{3,2,1,0:T(8,128)(2,1)S(1)}, u32[]{:S(2)}, u32[]{:S(2)}) %collective-permute-start.2) | collective-permute-done | bytes 163872 | tf_op jit(solution)/shard_map/ppermute | solution.py:313
  15.4 0.0 collective-permute-done.3.near_ref
  15.4 0.0 copy-done
  15.4 0.0 copy-done.5
  15.4 5.6 %hidden.1 = (bf16[2,2,64,1280]{3,2,1,0:T(8,128)(2,1)S(1)}, bf16[2,2,64,1280]{3,2,1,0:T(8,128)(2,1)S(1)}, bf16[512,128]{1,0:T(8,128)(2,1)}) custom-call(bf16[1,2,32,1280]{3,2,1,0:T(8,128)(2,1)S(1)} %collective-permute-done.odd_ref, bf16[1,2,32,1280]{3,2,1,0:T(8,128)(2,1)S(1)} %collective-permute-done.1.even_ref, ...), custom_call_target="tpu_custom_call" | custom-call | flops 1000000000 | bytes 4000000 | tf_op jit(solution)/shard_map/hidden/pallas_call | solution.py:316
  21.0 7.6 %all-to-all-start = ((bf16[32,16,128]{2,1,0:T(8,128)(2,1)}), bf16[32,16,128]{2,1,0:T(8,128)(2,1)S(1)}, u32[]{:S(2)}, u32[]{:S(2)}) async-start(bf16[32,16,128]{2,1,0:T(8,128)(2,1)} %bitcast.1), calls=%async_computation | async-start | bytes 262144 | tf_op jit(solution)/shard_map/all_to_all | solution.py:330
  28.5 1.4 %own.1 = (f32[2,2,32,1280]{3,2,1,0:T(8,128)S(1)}, f32[2,2,32,1280]{3,2,1,0:T(8,128)S(1)}, bf16[1,2,32,1280]{3,2,1,0:T(8,128)(2,1)S(1)}, bf16[1,2,32,1280]{3,2,1,...) custom-call(bf16[2,2,64,1280]{3,2,1,0:T(8,128)(2,1)S(1)} %get-tuple-element.41.act_ref, ...), custom_call_target="tpu_custom_call" | custom-call | flops 2000000000 | bytes 4000000 | tf_op jit(solution)/shard_map/own/pallas_call | solution.py:331
  29.9 0.0 copy-start.1
  29.9 0.9 %copy-done.1 = f32[2,2,32,1280]{3,2,1,0:T(8,128)} copy-done((f32[2,2,32,1280]{3,2,1,0:T(8,128)}, f32[2,2,32,1280]{3,2,1,0:T(8,128)S(1)}, u32[]{:S(2)}) %copy-start.1) | copy-done | bytes 655384
  30.8 0.0 copy-start.6
  30.8 0.9 %copy-done.6 = f32[2,2,32,1280]{3,2,1,0:T(8,128)} copy-done((f32[2,2,32,1280]{3,2,1,0:T(8,128)}, f32[2,2,32,1280]{3,2,1,0:T(8,128)S(1)}, u32[]{:S(2)}) %copy-start.6) | copy-done | bytes 655384
  31.6 1.9 %collective-permute-start.4 = (bf16[2,1,32,1280]{3,2,1,0:T(8,128)(2,1)S(1)}, bf16[2,1,32,1280]{3,2,1,0:T(8,128)(2,1)S(1)}, u32[]{:S(2)}, u32[]{:S(2)}) collective-permute-start(bf16[2,1,32,1280]{3,2,1,0:T(8,128)(2,1)S(1)} %get-tuple-element.46), channel_id=1, source_target_pairs={{8,16},{24,32},{40,48},{56,64},{72,80},{88,96},{104,112},{120,128}... | collective-permute-start | bytes 491528 | tf_op jit(solution)/shard_map/ppermute | solution.py:342
  33.5 0.1 collective-permute-start.5
  33.6 2.6 %all-to-all-done.refs_0_ = bf16[32,16,128]{2,1,0:T(8,128)(2,1)S(1)} async-done(((bf16[32,16,128]{2,1,0:T(8,128)(2,1)}), bf16[32,16,128]{2,1,0:T(8,128)(2,1)S(1)}, u32[]{:S(2)}, u32[]{:S(2)}) %all-to-all-start) | async-done | bytes 131104 | tf_op jit(solution)/shard_map/all_to_all | solution.py:330
  36.2 0.8 %plane_sums.1 = bf16[8,16,128]{2,1,0:T(8,128)(2,1)} custom-call(bf16[32,16,128]{2,1,0:T(8,128)(2,1)S(1)} %all-to-all-done.refs_0_), custom_call_target="tpu_custom_call" | custom-call | flops 2000000000 | bytes 4000000 | tf_op jit(solution)/shard_map/plane_sums/pallas_call | solution.py:263
  37.0 6.0 %all-to-all-start.1 = ((bf16[8,16,128]{2,1,0:T(8,128)(2,1)}), bf16[8,16,128]{2,1,0:T(8,128)(2,1)S(1)}, u32[]{:S(2)}, u32[]{:S(2)}) async-start(bf16[8,16,128]{2,1,0:T(8,128)(2,1)} %plane_sums.1), calls=%async_computation.1 | async-start | bytes 65536 | tf_op jit(solution)/shard_map/all_to_all | solution.py:345
  43.0 3.1 %collective-permute-start.6 = (bf16[1,2,32,1280]{3,2,1,0:T(8,128)(2,1)S(1)}, bf16[1,2,32,1280]{3,2,1,0:T(8,128)(2,1)S(1)}, u32[]{:S(2)}, u32[]{:S(2)}) collective-permute-start(bf16[1,2,32,1280]{3,2,1,0:T(8,128)(2,1)S(1)} %get-tuple-element.49), channel_id=1, source_target_pairs={{1,2},{3,4},{5,6},{7,0},{2,1},{4,3},{6,5},{0,7},{9,10},{11,12},{13... | collective-permute-start | bytes 491528 | tf_op jit(solution)/shard_map/ppermute | solution.py:346
  46.1 0.0 collective-permute-start.7
  46.1 0.0 collective-permute-done.4.far_ref
  46.1 0.0 collective-permute-done.5.near_ref
  46.1 3.8 %all-to-all-done.1.refs_0_ = bf16[8,16,128]{2,1,0:T(8,128)(2,1)S(1)} async-done(((bf16[8,16,128]{2,1,0:T(8,128)(2,1)}), bf16[8,16,128]{2,1,0:T(8,128)(2,1)S(1)}, u32[]{:S(2)}, u32[]{:S(2)}) %all-to-all-start.1) | async-done | bytes 32800 | tf_op jit(solution)/shard_map/all_to_all | solution.py:345
  49.9 0.8 %all_sums.1 = bf16[32,16,128]{2,1,0:T(8,128)(2,1)} custom-call(bf16[8,16,128]{2,1,0:T(8,128)(2,1)S(1)} %all-to-all-done.1.refs_0_), custom_call_target="tpu_custom_call" | custom-call | flops 2000000000 | bytes 4000000 | tf_op jit(solution)/shard_map/all_sums/pallas_call | solution.py:263
  50.7 6.9 %all-to-all-start.2 = ((bf16[32,16,128]{2,1,0:T(8,128)(2,1)}), bf16[32,16,128]{2,1,0:T(8,128)(2,1)S(1)}, u32[]{:S(2)}, u32[]{:S(2)}) async-start(bf16[32,16,128]{2,1,0:T(8,128)(2,1)} %all_sums.1), calls=%async_computation.2 | async-start | bytes 262144 | tf_op jit(solution)/shard_map/all_to_all | solution.py:349
  57.6 2.1 %grad_in.1 = bf16[2,2,32,1280]{3,2,1,0:T(8,128)(2,1)} custom-call(bf16[2,1,32,1280]{3,2,1,0:T(8,128)(2,1)S(1)} %collective-permute-done.4.far_ref, bf16[2,1,32,1280]{3,2,1,0:T(8,128)(2,1)S(1)} %collective-permute-done.5.near_ref, f32[2,2,32,1280]{3,2,1,0:T(8,128)} %copy-done.1, bf16[2,2,64,1280]{3,2,1,0:T(8,128)(2,1)} %cot_ref.5), custom_call_target="tpu_custom_call" | custom-call | flops 1000000 | bytes 100000 | tf_op jit(solution)/shard_map/grad_in/pallas_call | solution.py:275
  59.7 0.0 collective-permute-done.6.odd_ref
  59.7 0.0 collective-permute-done.7.even_ref
  59.7 2.1 %rebuilt.1 = bf16[2,2,32,1280]{3,2,1,0:T(8,128)(2,1)} custom-call(bf16[1,2,32,1280]{3,2,1,0:T(8,128)(2,1)S(1)} %collective-permute-done.6.odd_ref, bf16[1,2,32,1280]{3,2,1,0:T(8,128)(2,1)S(1)} %collective-permute-done.7.even_ref, f32[2,2,32,1280]{3,2,1,0:T(8,128)} %copy-done.6, bf16[2,2,64,1280]{3,2,1,0:T(8,128)(2,1)} %fwd_ref.5), custom_call_target="tpu_custom_call" | custom-call | flops 2000000000 | bytes 4000000 | tf_op jit(solution)/shard_map/rebuilt/pallas_call | solution.py:275
  61.9 3.4 %all-to-all-done.2 = bf16[32,16,128]{2,1,0:T(8,128)(2,1)S(1)} async-done(((bf16[32,16,128]{2,1,0:T(8,128)(2,1)}), bf16[32,16,128]{2,1,0:T(8,128)(2,1)S(1)}, u32[]{:S(2)}, u32[]{:S(2)}) %all-to-all-start.2) | async-done | bytes 131104 | tf_op jit(solution)/shard_map/all_to_all | solution.py:349
  65.3 0.9 %grads.1 = (f32[3,64,288]{2,1,0:T(8,128)}, f32[1,64]{1,0:T(1,128)}, f32[3,32,64]{2,1,0:T(8,128)}) custom-call(bf16[512,128]{1,0:T(8,128)(2,1)S(1)} %bitcast.4), custom_call_target="tpu_custom_call" | custom-call | flops 2000000000 | bytes 4000000 | tf_op jit(solution)/shard_map/grads/pallas_call | solution.py:357
Async XLA Ops:
  0.6 14.8 %copy-start = (bf16[2,2,64,1280]{3,2,1,0:T(8,128)(2,1)S(1)}, bf16[2,2,64,1280]{3,2,1,0:T(8,128)(2,1)}, u32[]{:S(2)}) copy-start(bf16[2,2,64,1280]{3,2,1,0:T(8,128)(2,1)} %cot_ref.5) | copy-start | bytes 1966084
  0.6 14.7 %copy-start.5 = (bf16[2,2,64,1280]{3,2,1,0:T(8,128)(2,1)S(1)}, bf16[2,2,64,1280]{3,2,1,0:T(8,128)(2,1)}, u32[]{:S(2)}) copy-start(bf16[2,2,64,1280]{3,2,1,0:T(8,128)(2,1)} %fwd_ref.5) | copy-start | bytes 1966084
  0.7 11.9 %copy-start.2 = (bf16[3,64,288]{2,1,0:T(8,128)(2,1)S(1)}, bf16[3,64,288]{2,1,0:T(8,128)(2,1)}, u32[]{:S(2)}) copy-start(bf16[3,64,288]{2,1,0:T(8,128)(2,1)} %sw_ref.3) | copy-start | bytes 331780
  0.7 11.9 %copy-start.3 = (bf16[3,32,64]{2,1,0:T(8,128)(2,1)S(1)}, bf16[3,32,64]{2,1,0:T(8,128)(2,1)}, u32[]{:S(2)}) copy-start(bf16[3,32,64]{2,1,0:T(8,128)(2,1)} %tw_ref.3) | copy-start | bytes 36868
  2.0 11.2 %collective-permute-start = (bf16[1,2,32,1280]{3,2,1,0:T(8,128)(2,1)S(1)}, bf16[1,2,32,1280]{3,2,1,0:T(8,128)(2,1)S(1)}, u32[]{:S(2)}, u32[]{:S(2)}) collective-permute-start(bf16[1,2,32,1280]{3,2,1,0:T(8,128)(2,1)S(1)} %get-tuple-element.33), channel_id=1, source_target_pairs={{1,2},{3,4},{5,6},{7,0},{2,1},{4,3},{6,5},{0,7},{9,10},{11,12},{13... | collective-permute-start | bytes 491528 | tf_op jit(solution)/shard_map/ppermute | solution.py:311
  8.0 5.2 %collective-permute-start.1 = (bf16[1,2,32,1280]{3,2,1,0:T(8,128)(2,1)S(1)}, bf16[1,2,32,1280]{3,2,1,0:T(8,128)(2,1)S(1)}, u32[]{:S(2)}, u32[]{:S(2)}) collective-permute-start(bf16[1,2,32,1280]{3,2,1,0:T(8,128)(2,1)S(1)} %get-tuple-element.34), channel_id=1, source_target_pairs={{0,1},{2,3},{4,5},{6,7},{1,0},{3,2},{5,4},{7,6},{8,9},{10,11},{12,... | collective-permute-start | bytes 491528 | tf_op jit(solution)/shard_map/ppermute | solution.py:312
  8.0 7.4 %collective-permute-start.2 = (bf16[2,1,32,1280]{3,2,1,0:T(8,128)(2,1)S(1)}, bf16[2,1,32,1280]{3,2,1,0:T(8,128)(2,1)S(1)}, u32[]{:S(2)}, u32[]{:S(2)}) collective-permute-start(bf16[2,1,32,1280]{3,2,1,0:T(8,128)(2,1)S(1)} %get-tuple-element.35), channel_id=1, source_target_pairs={{8,16},{24,32},{40,48},{56,64},{72,80},{88,96},{104,112},{120,128}... | collective-permute-start | bytes 491528 | tf_op jit(solution)/shard_map/ppermute | solution.py:313
  12.4 0.7 copy-start.4
  12.4 3.0 %collective-permute-start.3 = (bf16[2,1,32,1280]{3,2,1,0:T(8,128)(2,1)S(1)}, bf16[2,1,32,1280]{3,2,1,0:T(8,128)(2,1)S(1)}, u32[]{:S(2)}, u32[]{:S(2)}) collective-permute-start(bf16[2,1,32,1280]{3,2,1,0:T(8,128)(2,1)S(1)} %get-tuple-element.36), channel_id=1, source_target_pairs={{0,8},{16,24},{32,40},{48,56},{64,72},{80,88},{96,104},{112,120},{... | collective-permute-start | bytes 491528 | tf_op jit(solution)/shard_map/ppermute | solution.py:314
  21.0 15.3 %all-to-all-start = ((bf16[32,16,128]{2,1,0:T(8,128)(2,1)}), bf16[32,16,128]{2,1,0:T(8,128)(2,1)S(1)}, u32[]{:S(2)}, u32[]{:S(2)}) async-start(bf16[32,16,128]{2,1,0:T(8,128)(2,1)} %bitcast.1), calls=%async_computation | async-start | bytes 262144 | tf_op jit(solution)/shard_map/all_to_all | solution.py:330
  29.9 0.9 %copy-start.1 = (f32[2,2,32,1280]{3,2,1,0:T(8,128)}, f32[2,2,32,1280]{3,2,1,0:T(8,128)S(1)}, u32[]{:S(2)}) copy-start(f32[2,2,32,1280]{3,2,1,0:T(8,128)S(1)} %get-tuple-element.54.own_ref) | copy-start | bytes 1966084
  30.8 0.9 %copy-start.6 = (f32[2,2,32,1280]{3,2,1,0:T(8,128)}, f32[2,2,32,1280]{3,2,1,0:T(8,128)S(1)}, u32[]{:S(2)}) copy-start(f32[2,2,32,1280]{3,2,1,0:T(8,128)S(1)} %get-tuple-element.51.mapped_ref) | copy-start | bytes 1966084
  31.6 14.5 %collective-permute-start.4 = (bf16[2,1,32,1280]{3,2,1,0:T(8,128)(2,1)S(1)}, bf16[2,1,32,1280]{3,2,1,0:T(8,128)(2,1)S(1)}, u32[]{:S(2)}, u32[]{:S(2)}) collective-permute-start(bf16[2,1,32,1280]{3,2,1,0:T(8,128)(2,1)S(1)} %get-tuple-element.46), channel_id=1, source_target_pairs={{8,16},{24,32},{40,48},{56,64},{72,80},{88,96},{104,112},{120,128}... | collective-permute-start | bytes 491528 | tf_op jit(solution)/shard_map/ppermute | solution.py:342
  33.5 12.5 %collective-permute-start.5 = (bf16[2,1,32,1280]{3,2,1,0:T(8,128)(2,1)S(1)}, bf16[2,1,32,1280]{3,2,1,0:T(8,128)(2,1)S(1)}, u32[]{:S(2)}, u32[]{:S(2)}) collective-permute-start(bf16[2,1,32,1280]{3,2,1,0:T(8,128)(2,1)S(1)} %get-tuple-element.47), channel_id=1, source_target_pairs={{0,8},{16,24},{32,40},{48,56},{64,72},{80,88},{96,104},{112,120},{... | collective-permute-start | bytes 491528 | tf_op jit(solution)/shard_map/ppermute | solution.py:343
  37.0 12.9 %all-to-all-start.1 = ((bf16[8,16,128]{2,1,0:T(8,128)(2,1)}), bf16[8,16,128]{2,1,0:T(8,128)(2,1)S(1)}, u32[]{:S(2)}, u32[]{:S(2)}) async-start(bf16[8,16,128]{2,1,0:T(8,128)(2,1)} %plane_sums.1), calls=%async_computation.1 | async-start | bytes 65536 | tf_op jit(solution)/shard_map/all_to_all | solution.py:345
  43.0 16.7 %collective-permute-start.6 = (bf16[1,2,32,1280]{3,2,1,0:T(8,128)(2,1)S(1)}, bf16[1,2,32,1280]{3,2,1,0:T(8,128)(2,1)S(1)}, u32[]{:S(2)}, u32[]{:S(2)}) collective-permute-start(bf16[1,2,32,1280]{3,2,1,0:T(8,128)(2,1)S(1)} %get-tuple-element.49), channel_id=1, source_target_pairs={{1,2},{3,4},{5,6},{7,0},{2,1},{4,3},{6,5},{0,7},{9,10},{11,12},{13... | collective-permute-start | bytes 491528 | tf_op jit(solution)/shard_map/ppermute | solution.py:346
  46.1 13.6 %collective-permute-start.7 = (bf16[1,2,32,1280]{3,2,1,0:T(8,128)(2,1)S(1)}, bf16[1,2,32,1280]{3,2,1,0:T(8,128)(2,1)S(1)}, u32[]{:S(2)}, u32[]{:S(2)}) collective-permute-start(bf16[1,2,32,1280]{3,2,1,0:T(8,128)(2,1)S(1)} %get-tuple-element.50), channel_id=1, source_target_pairs={{0,1},{2,3},{4,5},{6,7},{1,0},{3,2},{5,4},{7,6},{8,9},{10,11},{12,... | collective-permute-start | bytes 491528 | tf_op jit(solution)/shard_map/ppermute | solution.py:347
  50.7 14.6 %all-to-all-start.2 = ((bf16[32,16,128]{2,1,0:T(8,128)(2,1)}), bf16[32,16,128]{2,1,0:T(8,128)(2,1)S(1)}, u32[]{:S(2)}, u32[]{:S(2)}) async-start(bf16[32,16,128]{2,1,0:T(8,128)(2,1)} %all_sums.1), calls=%async_computation.2 | async-start | bytes 262144 | tf_op jit(solution)/shard_map/all_to_all | solution.py:349
